TPU v7x, 256 devices: a whole 4x4x8 slice. The times are simulated.
256 devices in a mesh: row: 8 (over x, core), col: 32 (over y, z).
Axes of the slice: x: 4, y: 4, z: 8, core: 2. Of those that a mesh axis runs over, the one named last changes fastest.
Arguments:
- activations: bfloat16 [32768, 8192], P(('row', 'col')), may hold values from -24 to 24
- key_grads: bfloat16 [32768, 1024], P(('row', 'col')), may hold values from -24 to 24
- value_grads: bfloat16 [32768, 1024], P(('row', 'col')), may hold values from -24 to 24
- block_lengths: int32 [64], replicated, may hold values from 64 to 512, as said below
Outputs:
- key_clipped: bfloat16 [8192, 1024], P(('col', 'row'))
- value_clipped: bfloat16 [8192, 1024], P(('col', 'row'))
Inputs may be any that keep to these rules, and one draw needn't show every extreme that they name: `block_lengths`: some block is full and some block holds 64 real tokens.
All inputs are finite; a program needn't handle non-finite values.
Results may differ from a plain program's by a relative error of at most 0.001.
Values may be sent and summed in bfloat16 or wider, within the bound.
No kernel may reach another device: no remote copies, remote signals or barrier semaphores. Data moves between devices by JAX's collectives and lax.ppermute only.
A program may use at most 64 MiB of HBM per device.

v0:
```python
import math

import jax
import jax.numpy as jnp
from jax import lax
from jax.sharding import PartitionSpec as P

CH = 512


def body(activations, key_grads, value_grads, block_lengths):
    col_count = lax.axis_size("col")
    tok_count = activations.shape[0]
    model_width = activations.shape[1]
    head_width = key_grads.shape[1]
    shard_index = lax.axis_index("row") * col_count + lax.axis_index("col")
    position = shard_index * tok_count + jnp.arange(tok_count, dtype=jnp.int32)
    block_ids = jnp.arange(block_lengths.shape[0], dtype=jnp.int32)
    inside = (position // CH)[:, None] == block_ids[None, :]
    limit_len = jnp.sum(jnp.where(inside, block_lengths[None, :], 0), axis=1)
    is_real = position % CH < limit_len
    keys_kept = jnp.where(is_real[:, None], key_grads, jnp.zeros_like(key_grads))
    values_kept = jnp.where(is_real[:, None], value_grads, jnp.zeros_like(value_grads))
    clip_norm = math.sqrt(2.0 * model_width * head_width)
    contract = (((0,), (0,)), ((), ()))
    local_acts = lax.all_to_all(activations, "col", split_axis=1, concat_axis=0, tiled=True)
    local_keys, local_values = (
        lax.all_gather(keys_kept, "col", axis=0, tiled=True),
        lax.all_gather(values_kept, "col", axis=0, tiled=True),
    )
    grads_both = jnp.concatenate((local_keys, local_values), axis=1)
    owned_rows = lax.psum_scatter(
        lax.dot_general(local_acts, grads_both, contract, preferred_element_type=jnp.float32),
        "row",
        scatter_dimension=0,
        tiled=True,
    )
    squares = lax.psum(jnp.sum(owned_rows * owned_rows), ("row", "col"))
    factor = jnp.minimum(1.0, clip_norm / jnp.sqrt(squares))
    key_clipped = (owned_rows[:, :head_width] * factor).astype(jnp.bfloat16)
    value_clipped = (owned_rows[:, head_width:] * factor).astype(jnp.bfloat16)
    return (key_clipped, value_clipped)


def solution(mesh):
    in_specs = (P(("row", "col"), None), P(("row", "col"), None), P(("row", "col"), None), P())
    out_specs = (P(("col", "row"), None), P(("col", "row"), None))
    return jax.shard_map(body, mesh=mesh, in_specs=in_specs, out_specs=out_specs, check_vma=False)
```

profile of v0, /device:TPU:1, one launch (start us, length us, event | category | flops | bytes accessed | tf_op | source)
XLA Modules:
  0.0 361.6 jit_solution(4711121262898197171)
XLA Ops:
  7.2 0.0 all-gather.5.cloned.1.call-start
  7.2 0.7 select_reduce_fusion
  8.0 1.9 broadcast_select_fusion.1
  9.9 0.0 all-gather.5.cloned.1.call-update
  9.9 0.0 all-gather.3.cloned.1.call-start
  10.0 0.7 all-gather.3.cloned.1.call-update
  10.7 0.0 reduce-scatter.4.cloned.1.call-start
  10.7 4.1 %copy.18 = bf16[128,8192]{0,1:T(8,128)(2,1)} copy(bf16[128,8192]{1,0:T(8,128)(2,1)} %param.4) | data formatting | bytes 4194304 | tf_op args[0]
  14.9 69.5 %all_to_all.19 = bf16[128,32,256]{0,2,1:T(8,128)(2,1)S(1)} all-to-all(bf16[128,32,256]{0,2,1:T(8,128)(2,1)} %bitcast.8), channel_id=1, replica_groups=mesh['row'=8,'col'=32] {'col'}, dimensions={1} | all-to-all | bytes 4194304 | tf_op jit(solution)/shard_map/all_to_all | solution.py:26
  84.4 2.9 copy.19
  87.3 42.2 %all-gather.5.cloned.1.call-done = bf16[4096,1024]{1,0:T(8,128)(2,1)} async-done(((bf16[128,1024]{1,0:T(8,128)(2,1)}), bf16[4096,1024]{1,0:T(8,128)(2,1)}) %all-gather.5.cloned.1.call-update) | async-done | bytes 8388624 | tf_op jit(solution)/shard_map/all_gather | solution.py:29
  129.5 98.1 %all-gather.3.cloned.1.call-done = bf16[4096,1024]{1,0:T(8,128)(2,1)} async-done(((bf16[128,1024]{1,0:T(8,128)(2,1)}), bf16[4096,1024]{1,0:T(8,128)(2,1)}) %all-gather.3.cloned.1.call-update) | async-done | bytes 8388624 | tf_op jit(solution)/shard_map/all_gather | solution.py:28
  227.6 11.3 %fusion.4 = f32[256,2048]{0,1:T(8,128)S(1)} fusion(bf16[4096,256]{1,0:T(8,128)(2,1)} %bitcast.9, bf16[4096,1024]{1,0:T(8,128)(2,1)} %all-gather.5.cloned.1.call-done, bf16[4096,1024]{1,0:T(8,128)(2,1)} %all-gather.3.cloned.1.call-done), kind=kOutput, calls=%fused_computation.4 | convolution fusion | flops 4328521728 | bytes 20971520 | tf_op jit(solution)/shard_map/dot_general | solution.py:33
  238.9 1.9 copy.22
  240.8 0.0 reduce-scatter.4.cloned.1.call-update
  240.8 31.2 %reduce-scatter.4.cloned.1.call-done = f32[32,2048]{1,0:T(8,128)} async-done(((f32[256,2048]{1,0:T(8,128)}), f32[32,2048]{1,0:T(8,128)}) %reduce-scatter.4.cloned.1.call-update) | async-done | bytes 262160
  272.0 1.3 copy.23
  273.3 0.9 multiply_reduce_fusion
  274.1 78.6 %psum.7 = f32[]{:T(128)} all-reduce(f32[]{:T(128)} %multiply_reduce_fusion), channel_id=1, replica_groups=mesh['row'=8,'col'=32] {'row','col'}, use_global_device_ids=true, to_apply=%region_3.4 | all-reduce | flops 1 | bytes 8 | tf_op jit(solution)/shard_map/psum | solution.py:38
  353.5 0.1 fusion.7
  353.6 0.8 copy.20
  354.3 0.8 copy.21
  (2 shorter events, 0.0 us)
Async XLA Ops:
  7.2 122.3 %all-gather.5.cloned.1.call-start = ((), (), s32[]{:S(2)}) async-start(), calls=%async_computation.3 | async-start | bytes 8650752 | tf_op jit(solution)/shard_map/all_gather | solution.py:29
  9.9 217.7 %all-gather.3.cloned.1.call-start = ((), (), s32[]{:S(2)}) async-start(), calls=%async_computation.2 | async-start | bytes 8650752 | tf_op jit(solution)/shard_map/all_gather | solution.py:28
  10.7 261.3 %reduce-scatter.4.cloned.1.call-start = ((), (), s32[]{:S(2)}) async-start(), calls=%async_computation.4 | async-start | bytes 2359296
Sparse Core Ops, SparseCore 0:
  10.6 118.8 all-gather.4
  132.1 95.4 all-gather.2
  240.9 31.0 reduce-scatter.3
where the time goes:
time: 362 us
  waiting for transfers between devices  172 us (48%)
  blocking collectives  148 us (41%)
  between operations  14.5 us (4%)
  local copies, waits for them, and re-layouts  11.7 us (3%)
  matrix products  11.3 us (3%)
  other arithmetic  3.66 us (1%)
    all_gather x1, waiting for transfers between devices, body(): lax.all_gather(keys_kept, 'col', axis=0, tiled=True)  98.1 us
    psum x1, blocking collectives, body(): squares = lax.psum(jnp.sum(owned_rows * owned_rows), ('row', 'col'))  78.6 us
    all_to_all x1, blocking collectives, body(): lax.all_to_all(activations, 'col', split_axis=1, concat_axis=0, tiled=True)  69.5 us
    all_gather x1, waiting for transfers between devices, body(): lax.all_gather(values_kept, 'col', axis=0, tiled=True)  42.2 us
    unnamed x4, waiting for transfers between devices  31.9 us
    dot_general x1, matrix products, body(): lax.dot_general(local_acts, grads_both, contract, preferred_element_type=...  11.3 us
    unnamed x5, local copies, waits for them, and re-layouts  8.77 us
  transfers between devices with their start and end apart: 3, of which 3 were waited for; matrix products, arithmetic and copies ran while one was open for 2% of the time, Pallas kernels for 0%

commit v1 on v0

v1 whole, which is shorter than its diff:
```python
import itertools
import math

import jax
import jax.numpy as jnp
from jax import lax
from jax.sharding import Mesh, PartitionSpec as P

CH = 512
AXES = ("x", "c", "y", "z")
NX, NC, NY, NZ = 4, 2, 4, 8
CONTRACT = (((0,), (0,)), ((), ()))


def pairs(move):
    out = []
    for x, c, y, z in itertools.product(range(NX), range(NC), range(NY), range(NZ)):
        tx, tc, ty, tz = move(x, c, y, z)
        source = ((x * NC + c) * NY + y) * NZ + z
        target = (((tx % NX) * NC + tc % NC) * NY + ty % NY) * NZ + tz % NZ
        out.append((source, target))
    return out


def send(value, move):
    return lax.ppermute(value, AXES, pairs(move))


def swap_cores(value):
    return send(value, lambda x, c, y, z: (x, 1 - c, y, z))


def first_ring(value, step):
    return send(value, lambda x, c, y, z: (x + step, c, y, z) if c == 0 else (x, c, y + step, z))


def second_ring(value, step):
    return send(value, lambda x, c, y, z: (x, c, y + step, z) if c == 0 else (x + step, c, y, z))


def z_ring(value, step):
    return send(value, lambda x, c, y, z: (x, c, y, z + step))


def gather_ring(value, ring):
    half = value.shape[0] // 2
    before = ring(value, 1)
    after = ring(value, -1)
    opposite = jnp.concatenate((ring(before[:half], 1), ring(after[half:], -1)), axis=0)
    return value, before, after, opposite


OFFSETS = (0, -1, 1, 2)


def reduce_z(partial, z):
    rows = partial.shape[0] // NZ
    half = rows // 2

    def block(offset):
        return lax.dynamic_slice_in_dim(partial, lax.rem(z + offset + NZ, NZ) * rows, rows, axis=0)

    far = block(4)
    up = z_ring(far[:half], 1)
    down = z_ring(far[half:], -1)
    near_up, near_down = block(3), block(-3)
    up = z_ring(jnp.concatenate((near_up[:half] + up, near_up[half:]), axis=0), 1)
    down = z_ring(jnp.concatenate((near_down[:half], near_down[half:] + down), axis=0), -1)
    for offset in (2, 1):
        up = z_ring(block(offset) + up, 1)
        down = z_ring(block(-offset) + down, -1)
    return block(0) + up + down


def sum_all(value):
    value = value + swap_cores(value)
    for bit in (1, 2):
        value = value + send(value, lambda x, c, y, z: (x ^ bit, c, y, z))
    for bit in (1, 2):
        value = value + send(value, lambda x, c, y, z: (x, c, y ^ bit, z))
    for bit in (1, 2, 4):
        value = value + send(value, lambda x, c, y, z: (x, c, y, z ^ bit))
    return value


def body(activations, key_grads, value_grads, block_lengths):
    tok_count, model_width = activations.shape
    head_width = key_grads.shape[1]
    x, c, y, z = (lax.axis_index(axis) for axis in AXES)
    is_keys = c == 0
    position = (((x * NC + c) * NY + y) * NZ + z) * tok_count
    limit_len = lax.dynamic_index_in_dim(block_lengths, position // CH, keepdims=False)
    rows = lax.broadcasted_iota(jnp.int32, (tok_count, 1), 0)
    is_real = rows + lax.rem(position, CH) < limit_len
    clip_norm = math.sqrt(2.0 * model_width * head_width)

    zero = jnp.zeros((), key_grads.dtype)
    mine = jnp.where(is_real, jnp.where(is_keys, key_grads, value_grads), zero)
    theirs = jnp.where(is_real, jnp.where(is_keys, value_grads, key_grads), zero)
    grads = jnp.concatenate((mine, swap_cores(theirs)), axis=0)

    lump = jnp.concatenate(gather_ring(grads, first_ring), axis=0)

    acts = lax.all_to_all(activations, ("y", "x"), split_axis=1, concat_axis=0, tiled=True)
    acts_other = swap_cores(acts)
    acts = acts.reshape(NX * NY, tok_count, -1)
    acts_other = acts_other.reshape(NX * NY, tok_count, -1)

    first, second = jnp.where(is_keys, x, y), jnp.where(is_keys, y, x)
    weight = None
    for offset2, part in zip(OFFSETS, gather_ring(lump, second_ring)):
        blocks = []
        for offset1 in OFFSETS:
            at1, at2 = lax.rem(first + offset1 + 4, 4), lax.rem(second + offset2 + 4, 4)
            index = jnp.where(is_keys, at2 * NX + at1, at1 * NX + at2)
            blocks.append(lax.dynamic_index_in_dim(acts, index, keepdims=False))
            blocks.append(lax.dynamic_index_in_dim(acts_other, index, keepdims=False))
        product = lax.dot_general(
            jnp.concatenate(blocks, axis=0), part, CONTRACT, preferred_element_type=jnp.float32
        )
        weight = product if weight is None else weight + product

    owned = reduce_z(weight, z)
    squares = jnp.broadcast_to(jnp.sum(owned * owned), (8, 128))
    total = sum_all(squares)[0, 0]

    half = owned.shape[0] // 2
    low, high = owned[:half], owned[half:]
    same = send(
        jnp.where(is_keys, low, high), lambda x, c, y, z: (z % NX, c, y, 2 * x + z // NX)
    )
    cross = send(
        jnp.where(is_keys, high, low), lambda x, c, y, z: (z % NX, 1 - c, y, 2 * x + z // NX)
    )
    factor = jnp.minimum(1.0, clip_norm / jnp.sqrt(total))
    key_clipped = (jnp.where(is_keys, same, cross) * factor).astype(jnp.bfloat16)
    value_clipped = (jnp.where(is_keys, cross, same) * factor).astype(jnp.bfloat16)
    return key_clipped, value_clipped


def solution(mesh):
    fine = Mesh(mesh.devices.reshape(NX, NC, NY, NZ), AXES)
    tokens = P(AXES, None)
    owners = P(("y", "z", "x", "c"), None)
    return jax.shard_map(
        body,
        mesh=fine,
        in_specs=(tokens, tokens, tokens, P()),
        out_specs=(owners, owners),
        check_vma=False,
    )
```

time: 362 us -> 193 us (0.53)
  the two profiles are of different devices: /device:TPU:1 before, /device:TPU:62 now
where the time goes in v1:
time: 193 us; the launch traced here: 192 us
  waiting for transfers between devices  103 us (53%)
  starting transfers between devices  46.6 us (24%)
  local copies, waits for them, and re-layouts  27.2 us (14%)
  matrix products  9.87 us (5%)
  other arithmetic  4.44 us (2%)
    ppermute x28, waiting for transfers between devices, send(): return lax.ppermute(value, AXES, pairs(move))  103 us
    ppermute x28, starting transfers between devices, send(): return lax.ppermute(value, AXES, pairs(move))  39.3 us
    unnamed x28, local copies, waits for them, and re-layouts  10.8 us
    dot_general x4, matrix products, body(): lax.dot_general(jnp.concatenate(blocks, axis=0), part, CONTRACT, preferre...  9.87 us
    another operation x17, local copies, waits for them, and re-layouts  7.44 us
    all_to_all x1, starting transfers between devices, body(): lax.all_to_all(activations, ('y', 'x'), split_axis=1, concat_axis=0, tile...  7.23 us
  transfers between devices with their start and end apart: 29, of which 19 were waited for; matrix products, arithmetic and copies ran while one was open for 17% of the time, Pallas kernels for 0%

profile of v1, /device:TPU:62, one launch (start us, length us, event | category | flops | bytes accessed | tf_op | source)
XLA Modules:
  0.0 192.5 jit_solution(15541525370810422929)
XLA Ops:
  0.6 4.1 %copy.6 = bf16[128,8192]{0,1:T(8,128)(2,1)} copy(bf16[128,8192]{1,0:T(8,128)(2,1)} %param.4) | data formatting | bytes 4194304 | tf_op args[0]
  4.7 7.2 %all-to-all-start = ((bf16[128,16,512]{0,2,1:T(8,128)(2,1)}), bf16[128,16,512]{0,2,1:T(8,128)(2,1)S(1)}, u32[]{:S(2)}, u32[]{:S(2)}) async-start(bf16[128,16,512]{0,2,1:T(8,128)(2,1)} %bitcast.78), calls=%async_computation | async-start | bytes 4194304 | tf_op jit(solution)/shard_map/all_to_all | solution.py:104
  17.7 26.9 %collective-permute-done.2 = bf16[256,1024]{1,0:T(8,128)(2,1)S(1)} collective-permute-done((bf16[256,1024]{1,0:T(8,128)(2,1)S(1)}, bf16[256,1024]{1,0:T(8,128)(2,1)S(1)}, u32[]{:S(2)}, u32[]{:S(2)}) %collective-permute-start.2) | collective-permute-done | bytes 524320 | tf_op jit(solution)/shard_map/ppermute | solution.py:26
  58.1 2.6 %copy.8 = bf16[16,128,512]{2,1,0:T(8,128)(2,1)} copy(bf16[16,128,512]{1,2,0:T(8,128)(2,1)S(1)} %bitcast.77) | data formatting | bytes 4194304 | tf_op jit(solution)/shard_map/all_to_all | solution.py:104
  68.4 14.1 %collective-permute-done.7 = bf16[1024,1024]{1,0:T(8,128)(2,1)} collective-permute-done((bf16[1024,1024]{1,0:T(8,128)(2,1)}, bf16[1024,1024]{1,0:T(8,128)(2,1)}, u32[]{:S(2)}, u32[]{:S(2)}) %collective-permute-start.7) | collective-permute-done | bytes 2097184 | tf_op jit(solution)/shard_map/ppermute | solution.py:26
  93.4 2.9 %fusion.7 = f32[512,1024]{1,0:T(8,128)S(1)} fusion(bf16[1024,512]{1,0:T(8,128)(2,1)S(1)} %get-tuple-element.17, bf16[1024,1024]{1,0:T(8,128)(2,1)} %constant_dynamic-update-slice_fusion), kind=kOutput, calls=%fused_computation.83 | convolution fusion | flops 1073741824 | bytes 5242880 | tf_op jit(solution)/shard_map/dot_general | solution.py:118
  96.2 2.9 %fusion.9 = f32[512,1024]{1,0:T(8,128)S(1)} fusion(bf16[1024,512]{1,0:T(8,128)(2,1)S(1)} %get-tuple-element.15, bf16[1024,1024]{1,0:T(8,128)(2,1)} %collective-permute-done.7), kind=kOutput, calls=%fused_computation.85 | convolution fusion | flops 1073741824 | bytes 5242880 | tf_op jit(solution)/shard_map/dot_general | solution.py:118
  99.1 2.9 %fusion.8 = f32[512,1024]{1,0:T(8,128)S(1)} fusion(bf16[1024,512]{1,0:T(8,128)(2,1)S(1)} %get-tuple-element.16, bf16[1024,1024]{1,0:T(8,128)(2,1)} %collective-permute-done.6), kind=kOutput, calls=%fused_computation.84 | convolution fusion | flops 1073741824 | bytes 5242880 | tf_op jit(solution)/shard_map/dot_general | solution.py:118
  105.4 4.0 %collective-permute-done.10 = f32[32,1024]{1,0:T(8,128)S(1)} collective-permute-done((f32[32,1024]{1,0:T(8,128)S(1)}, f32[32,1024]{1,0:T(8,128)S(1)}, u32[]{:S(2)}, u32[]{:S(2)}) %collective-permute-start.10) | collective-permute-done | bytes 131104 | tf_op jit(solution)/shard_map/ppermute | solution.py:26
  110.4 3.8 %collective-permute-start.11 = (f32[64,1024]{1,0:T(8,128)S(1)}, f32[64,1024]{1,0:T(8,128)S(1)}, u32[]{:S(2)}, u32[]{:S(2)}) collective-permute-start(f32[64,1024]{1,0:T(8,128)S(1)} %pad_maximum_fusion.1), channel_id=1, source_target_pairs={{0,1},{1,2},{2,3},{3,4},{4,5},{5,6},{6,7},{7,0},{8,9},{9,10},{10,1... | collective-permute-start | bytes 786440 | tf_op jit(solution)/shard_map/ppermute | solution.py:26
  114.3 6.6 %collective-permute-done.11 = f32[64,1024]{1,0:T(8,128)S(1)} collective-permute-done((f32[64,1024]{1,0:T(8,128)S(1)}, f32[64,1024]{1,0:T(8,128)S(1)}, u32[]{:S(2)}, u32[]{:S(2)}) %collective-permute-start.11) | collective-permute-done | bytes 262176 | tf_op jit(solution)/shard_map/ppermute | solution.py:26
  122.6 8.2 %collective-permute-done.12 = f32[64,1024]{1,0:T(8,128)S(1)} collective-permute-done((f32[64,1024]{1,0:T(8,128)S(1)}, f32[64,1024]{1,0:T(8,128)S(1)}, u32[]{:S(2)}, u32[]{:S(2)}) %collective-permute-start.12) | collective-permute-done | bytes 262176 | tf_op jit(solution)/shard_map/ppermute | solution.py:26
  130.8 2.9 %collective-permute-start.16 = (f32[64,1024]{1,0:T(8,128)S(1)}, f32[64,1024]{1,0:T(8,128)S(1)}, u32[]{:S(2)}, u32[]{:S(2)}) collective-permute-start(f32[64,1024]{1,0:T(8,128)S(1)} %get-tuple-element.7), channel_id=1, source_target_pairs={{0,7},{1,0},{2,1},{3,2},{4,3},{5,4},{6,5},{7,6},{8,15},{9,8},{10,9... | collective-permute-start | bytes 786440 | tf_op jit(solution)/shard_map/ppermute | solution.py:26
  133.6 3.9 %collective-permute-done.16 = f32[64,1024]{1,0:T(8,128)S(1)} collective-permute-done((f32[64,1024]{1,0:T(8,128)S(1)}, f32[64,1024]{1,0:T(8,128)S(1)}, u32[]{:S(2)}, u32[]{:S(2)}) %collective-permute-start.16) | collective-permute-done | bytes 262176 | tf_op jit(solution)/shard_map/ppermute | solution.py:26
  137.6 2.6 %collective-permute-start.17 = (f32[64,1024]{1,0:T(8,128)S(1)}, f32[64,1024]{1,0:T(8,128)S(1)}, u32[]{:S(2)}, u32[]{:S(2)}) collective-permute-start(f32[64,1024]{1,0:T(8,128)S(1)} %dynamic-slice_add_fusion.1), channel_id=1, source_target_pairs={{0,7},{1,0},{2,1},{3,2},{4,3},{5,4},{6,5},{7,6},{8,15},{9,8},{10,9... | collective-permute-start | bytes 786440 | tf_op jit(solution)/shard_map/ppermute | solution.py:26
  140.1 3.9 %collective-permute-done.17 = f32[64,1024]{1,0:T(8,128)S(1)} collective-permute-done((f32[64,1024]{1,0:T(8,128)S(1)}, f32[64,1024]{1,0:T(8,128)S(1)}, u32[]{:S(2)}, u32[]{:S(2)}) %collective-permute-start.17) | collective-permute-done | bytes 262176 | tf_op jit(solution)/shard_map/ppermute | solution.py:26
  147.4 3.4 %collective-permute-start.19 = (f32[32,1024]{1,0:T(8,128)S(1)}, f32[32,1024]{1,0:T(8,128)S(1)}, u32[]{:S(2)}, u32[]{:S(2)}) collective-permute-start(f32[32,1024]{1,0:T(8,128)S(1)} %get-tuple-element.49), channel_id=1, source_target_pairs={{0,32},{1,96},{2,160},{3,224},{4,33},{5,97},{6,161},{7,225},{8,40}... | collective-permute-start | bytes 393224 | tf_op jit(solution)/shard_map/ppermute | solution.py:26
  150.8 9.5 %collective-permute-start.18 = (f32[32,1024]{1,0:T(8,128)S(1)}, f32[32,1024]{1,0:T(8,128)S(1)}, u32[]{:S(2)}, u32[]{:S(2)}) collective-permute-start(f32[32,1024]{1,0:T(8,128)S(1)} %get-tuple-element.50), channel_id=1, source_target_pairs={{0,0},{1,64},{2,128},{3,192},{4,1},{5,65},{6,129},{7,193},{8,8},{9... | collective-permute-start | bytes 393224 | tf_op jit(solution)/shard_map/ppermute | solution.py:26
  161.1 5.1 %collective-permute-done.22 = f32[8,128]{1,0:T(8,128)S(1)} collective-permute-done((f32[8,128]{1,0:T(8,128)S(1)}, f32[8,128]{1,0:T(8,128)S(1)}, u32[]{:S(2)}, u32[]{:S(2)}) %collective-permute-start.22) | collective-permute-done | bytes 4128 | tf_op jit(solution)/shard_map/ppermute | solution.py:26
  166.5 3.3 %collective-permute-done.23 = f32[8,128]{1,0:T(8,128)S(1)} collective-permute-done((f32[8,128]{1,0:T(8,128)S(1)}, f32[8,128]{1,0:T(8,128)S(1)}, u32[]{:S(2)}, u32[]{:S(2)}) %collective-permute-start.23) | collective-permute-done | bytes 4128 | tf_op jit(solution)/shard_map/ppermute | solution.py:26
  169.8 5.1 %collective-permute-done.24 = f32[8,128]{1,0:T(8,128)S(1)} collective-permute-done((f32[8,128]{1,0:T(8,128)S(1)}, f32[8,128]{1,0:T(8,128)S(1)}, u32[]{:S(2)}, u32[]{:S(2)}) %collective-permute-start.24) | collective-permute-done | bytes 4128 | tf_op jit(solution)/shard_map/ppermute | solution.py:26
  174.9 3.6 %collective-permute-done.25 = f32[8,128]{1,0:T(8,128)S(1)} collective-permute-done((f32[8,128]{1,0:T(8,128)S(1)}, f32[8,128]{1,0:T(8,128)S(1)}, u32[]{:S(2)}, u32[]{:S(2)}) %collective-permute-start.25) | collective-permute-done | bytes 4128 | tf_op jit(solution)/shard_map/ppermute | solution.py:26
  178.5 4.5 %collective-permute-done.26 = f32[8,128]{1,0:T(8,128)S(1)} collective-permute-done((f32[8,128]{1,0:T(8,128)S(1)}, f32[8,128]{1,0:T(8,128)S(1)}, u32[]{:S(2)}, u32[]{:S(2)}) %collective-permute-start.26) | collective-permute-done | bytes 4128 | tf_op jit(solution)/shard_map/ppermute | solution.py:26
  185.1 5.4 %collective-permute-done.27 = f32[8,128]{1,0:T(8,128)S(1)} collective-permute-done((f32[8,128]{1,0:T(8,128)S(1)}, f32[8,128]{1,0:T(8,128)S(1)}, u32[]{:S(2)}, u32[]{:S(2)}) %collective-permute-start.27) | collective-permute-done | bytes 4128 | tf_op jit(solution)/shard_map/ppermute | solution.py:26
  (114 shorter events, 51.5 us)
Async XLA Ops:
  4.7 53.4 %all-to-all-start = ((bf16[128,16,512]{0,2,1:T(8,128)(2,1)}), bf16[128,16,512]{0,2,1:T(8,128)(2,1)S(1)}, u32[]{:S(2)}, u32[]{:S(2)}) async-start(bf16[128,16,512]{0,2,1:T(8,128)(2,1)} %bitcast.78), calls=%async_computation | async-start | bytes 4194304 | tf_op jit(solution)/shard_map/all_to_all | solution.py:104
  15.6 29.0 %collective-permute-start.2 = (bf16[256,1024]{1,0:T(8,128)(2,1)S(1)}, bf16[256,1024]{1,0:T(8,128)(2,1)S(1)}, u32[]{:S(2)}, u32[]{:S(2)}) collective-permute-start(bf16[256,1024]{1,0:T(8,128)(2,1)S(1)} %pad_maximum_fusion), channel_id=1, source_target_pairs={{0,64},{1,65},{2,66},{3,67},{4,68},{5,69},{6,70},{7,71},{8,72},{9,... | collective-permute-start | bytes 1572872 | tf_op jit(solution)/shard_map/ppermute | solution.py:26
  16.3 30.2 %collective-permute-start.3 = (bf16[256,1024]{1,0:T(8,128)(2,1)S(1)}, bf16[256,1024]{1,0:T(8,128)(2,1)S(1)}, u32[]{:S(2)}, u32[]{:S(2)}) collective-permute-start(bf16[256,1024]{1,0:T(8,128)(2,1)S(1)} %pad_maximum_fusion), channel_id=1, source_target_pairs={{0,192},{1,193},{2,194},{3,195},{4,196},{5,197},{6,198},{7,199},{8... | collective-permute-start | bytes 1572872 | tf_op jit(solution)/shard_map/ppermute | solution.py:26
  44.7 6.4 %collective-permute-start.4 = (bf16[128,1024]{1,0:T(8,128)(2,1)S(1)}, bf16[128,1024]{1,0:T(8,128)(2,1)S(1)}, u32[]{:S(2)}, u32[]{:S(2)}) collective-permute-start(bf16[128,1024]{1,0:T(8,128)(2,1)S(1)} %slice.52), channel_id=1, source_target_pairs={{0,64},{1,65},{2,66},{3,67},{4,68},{5,69},{6,70},{7,71},{8,72},{9,... | collective-permute-start | bytes 786440 | tf_op jit(solution)/shard_map/ppermute | solution.py:26
  46.5 7.7 %collective-permute-start.5 = (bf16[128,1024]{1,0:T(8,128)(2,1)S(1)}, bf16[128,1024]{1,0:T(8,128)(2,1)S(1)}, u32[]{:S(2)}, u32[]{:S(2)}) collective-permute-start(bf16[128,1024]{1,0:T(8,128)(2,1)S(1)} %slice.53), channel_id=1, source_target_pairs={{0,192},{1,193},{2,194},{3,195},{4,196},{5,197},{6,198},{7,199},{8... | collective-permute-start | bytes 786440 | tf_op jit(solution)/shard_map/ppermute | solution.py:26
  54.9 27.6 %collective-permute-start.7 = (bf16[1024,1024]{1,0:T(8,128)(2,1)}, bf16[1024,1024]{1,0:T(8,128)(2,1)}, u32[]{:S(2)}, u32[]{:S(2)}) collective-permute-start(bf16[1024,1024]{1,0:T(8,128)(2,1)} %constant_dynamic-update-slice_fusion), channel_id=1, source_target_pairs={{0,24},{1,25},{2,26},{3,27},{4,28},{5,29},{6,30},{7,31},{8,0},{9,1... | collective-permute-start | bytes 6291464 | tf_op jit(solution)/shard_map/ppermute | solution.py:26
  57.2 27.7 %collective-permute-start.6 = (bf16[1024,1024]{1,0:T(8,128)(2,1)}, bf16[1024,1024]{1,0:T(8,128)(2,1)}, u32[]{:S(2)}, u32[]{:S(2)}) collective-permute-start(bf16[1024,1024]{1,0:T(8,128)(2,1)} %constant_dynamic-update-slice_fusion), channel_id=1, source_target_pairs={{0,8},{1,9},{2,10},{3,11},{4,12},{5,13},{6,14},{7,15},{8,16},{9,17... | collective-permute-start | bytes 6291464 | tf_op jit(solution)/shard_map/ppermute | solution.py:26
  60.7 27.9 %collective-permute-start = (bf16[2048,512]{1,0:T(8,128)(2,1)}, bf16[2048,512]{1,0:T(8,128)(2,1)}, u32[]{:S(2)}, u32[]{:S(2)}) collective-permute-start(bf16[2048,512]{1,0:T(8,128)(2,1)} %bitcast.79), channel_id=1, source_target_pairs={{0,32},{1,33},{2,34},{3,35},{4,36},{5,37},{6,38},{7,39},{8,40},{9,... | collective-permute-start | bytes 6291464 | tf_op jit(solution)/shard_map/ppermute | solution.py:26
  83.7 18.2 %collective-permute-start.9 = (bf16[512,1024]{1,0:T(8,128)(2,1)S(1)}, bf16[512,1024]{1,0:T(8,128)(2,1)S(1)}, u32[]{:S(2)}, u32[]{:S(2)}) collective-permute-start(bf16[512,1024]{1,0:T(8,128)(2,1)S(1)} %slice.55), channel_id=1, source_target_pairs={{0,24},{1,25},{2,26},{3,27},{4,28},{5,29},{6,30},{7,31},{8,0},{9,1... | collective-permute-start | bytes 3145736 | tf_op jit(solution)/shard_map/ppermute | solution.py:26
  86.2 15.8 %collective-permute-start.8 = (bf16[512,1024]{1,0:T(8,128)(2,1)S(1)}, bf16[512,1024]{1,0:T(8,128)(2,1)S(1)}, u32[]{:S(2)}, u32[]{:S(2)}) collective-permute-start(bf16[512,1024]{1,0:T(8,128)(2,1)S(1)} %slice.54), channel_id=1, source_target_pairs={{0,8},{1,9},{2,10},{3,11},{4,12},{5,13},{6,14},{7,15},{8,16},{9,17... | collective-permute-start | bytes 3145736 | tf_op jit(solution)/shard_map/ppermute | solution.py:26
  103.3 6.1 %collective-permute-start.10 = (f32[32,1024]{1,0:T(8,128)S(1)}, f32[32,1024]{1,0:T(8,128)S(1)}, u32[]{:S(2)}, u32[]{:S(2)}) collective-permute-start(f32[32,1024]{1,0:T(8,128)S(1)} %get-tuple-element.12), channel_id=1, source_target_pairs={{0,1},{1,2},{2,3},{3,4},{4,5},{5,6},{6,7},{7,0},{8,9},{9,10},{10,1... | collective-permute-start | bytes 393224 | tf_op jit(solution)/shard_map/ppermute | solution.py:26
  105.3 5.0 %collective-permute-start.14 = (f32[32,1024]{1,0:T(8,128)S(1)}, f32[32,1024]{1,0:T(8,128)S(1)}, u32[]{:S(2)}, u32[]{:S(2)}) collective-permute-start(f32[32,1024]{1,0:T(8,128)S(1)} %get-tuple-element.13), channel_id=1, source_target_pairs={{0,7},{1,0},{2,1},{3,2},{4,3},{5,4},{6,5},{7,6},{8,15},{9,8},{10,9... | collective-permute-start | bytes 393224 | tf_op jit(solution)/shard_map/ppermute | solution.py:26
  110.4 10.5 %collective-permute-start.11 = (f32[64,1024]{1,0:T(8,128)S(1)}, f32[64,1024]{1,0:T(8,128)S(1)}, u32[]{:S(2)}, u32[]{:S(2)}) collective-permute-start(f32[64,1024]{1,0:T(8,128)S(1)} %pad_maximum_fusion.1), channel_id=1, source_target_pairs={{0,1},{1,2},{2,3},{3,4},{4,5},{5,6},{6,7},{7,0},{8,9},{9,10},{10,1... | collective-permute-start | bytes 786440 | tf_op jit(solution)/shard_map/ppermute | solution.py:26
  114.2 8.3 %collective-permute-start.15 = (f32[64,1024]{1,0:T(8,128)S(1)}, f32[64,1024]{1,0:T(8,128)S(1)}, u32[]{:S(2)}, u32[]{:S(2)}) collective-permute-start(f32[64,1024]{1,0:T(8,128)S(1)} %pad_maximum_fusion.2), channel_id=1, source_target_pairs={{0,7},{1,0},{2,1},{3,2},{4,3},{5,4},{6,5},{7,6},{8,15},{9,8},{10,9... | collective-permute-start | bytes 786440 | tf_op jit(solution)/shard_map/ppermute | solution.py:26
  120.9 9.8 %collective-permute-start.12 = (f32[64,1024]{1,0:T(8,128)S(1)}, f32[64,1024]{1,0:T(8,128)S(1)}, u32[]{:S(2)}, u32[]{:S(2)}) collective-permute-start(f32[64,1024]{1,0:T(8,128)S(1)} %dynamic-slice_add_fusion.2), channel_id=1, source_target_pairs={{0,1},{1,2},{2,3},{3,4},{4,5},{5,6},{6,7},{7,0},{8,9},{9,10},{10,1... | collective-permute-start | bytes 786440 | tf_op jit(solution)/shard_map/ppermute | solution.py:26
  130.8 6.7 %collective-permute-start.16 = (f32[64,1024]{1,0:T(8,128)S(1)}, f32[64,1024]{1,0:T(8,128)S(1)}, u32[]{:S(2)}, u32[]{:S(2)}) collective-permute-start(f32[64,1024]{1,0:T(8,128)S(1)} %get-tuple-element.7), channel_id=1, source_target_pairs={{0,7},{1,0},{2,1},{3,2},{4,3},{5,4},{6,5},{7,6},{8,15},{9,8},{10,9... | collective-permute-start | bytes 786440 | tf_op jit(solution)/shard_map/ppermute | solution.py:26
  133.6 6.5 %collective-permute-start.13 = (f32[64,1024]{1,0:T(8,128)S(1)}, f32[64,1024]{1,0:T(8,128)S(1)}, u32[]{:S(2)}, u32[]{:S(2)}) collective-permute-start(f32[64,1024]{1,0:T(8,128)S(1)} %get-tuple-element.6), channel_id=1, source_target_pairs={{0,1},{1,2},{2,3},{3,4},{4,5},{5,6},{6,7},{7,0},{8,9},{9,10},{10,1... | collective-permute-start | bytes 786440 | tf_op jit(solution)/shard_map/ppermute | solution.py:26
  137.6 6.5 %collective-permute-start.17 = (f32[64,1024]{1,0:T(8,128)S(1)}, f32[64,1024]{1,0:T(8,128)S(1)}, u32[]{:S(2)}, u32[]{:S(2)}) collective-permute-start(f32[64,1024]{1,0:T(8,128)S(1)} %dynamic-slice_add_fusion.1), channel_id=1, source_target_pairs={{0,7},{1,0},{2,1},{3,2},{4,3},{5,4},{6,5},{7,6},{8,15},{9,8},{10,9... | collective-permute-start | bytes 786440 | tf_op jit(solution)/shard_map/ppermute | solution.py:26
  147.3 13.1 %collective-permute-start.21 = (f32[8,128]{1,0:T(8,128)S(1)}, f32[8,128]{1,0:T(8,128)S(1)}, u32[]{:S(2)}, u32[]{:S(2)}) collective-permute-start(f32[8,128]{1,0:T(8,128)S(1)} %broadcast_add_fusion), channel_id=1, source_target_pairs={{0,64},{1,65},{2,66},{3,67},{4,68},{5,69},{6,70},{7,71},{8,72},{9,... | collective-permute-start | bytes 12296 | tf_op jit(solution)/shard_map/ppermute | solution.py:26
  147.4 44.4 %collective-permute-start.19 = (f32[32,1024]{1,0:T(8,128)S(1)}, f32[32,1024]{1,0:T(8,128)S(1)}, u32[]{:S(2)}, u32[]{:S(2)}) collective-permute-start(f32[32,1024]{1,0:T(8,128)S(1)} %get-tuple-element.49), channel_id=1, source_target_pairs={{0,32},{1,96},{2,160},{3,224},{4,33},{5,97},{6,161},{7,225},{8,40}... | collective-permute-start | bytes 393224 | tf_op jit(solution)/shard_map/ppermute | solution.py:26
  150.8 41.0 %collective-permute-start.18 = (f32[32,1024]{1,0:T(8,128)S(1)}, f32[32,1024]{1,0:T(8,128)S(1)}, u32[]{:S(2)}, u32[]{:S(2)}) collective-permute-start(f32[32,1024]{1,0:T(8,128)S(1)} %get-tuple-element.50), channel_id=1, source_target_pairs={{0,0},{1,64},{2,128},{3,192},{4,1},{5,65},{6,129},{7,193},{8,8},{9... | collective-permute-start | bytes 393224 | tf_op jit(solution)/shard_map/ppermute | solution.py:26
  161.0 5.2 %collective-permute-start.22 = (f32[8,128]{1,0:T(8,128)S(1)}, f32[8,128]{1,0:T(8,128)S(1)}, u32[]{:S(2)}, u32[]{:S(2)}) collective-permute-start(f32[8,128]{1,0:T(8,128)S(1)} %fusion.17), channel_id=1, source_target_pairs={{0,128},{1,129},{2,130},{3,131},{4,132},{5,133},{6,134},{7,135},{8... | collective-permute-start | bytes 12296 | tf_op jit(solution)/shard_map/ppermute | solution.py:26
  169.8 5.1 %collective-permute-start.24 = (f32[8,128]{1,0:T(8,128)S(1)}, f32[8,128]{1,0:T(8,128)S(1)}, u32[]{:S(2)}, u32[]{:S(2)}) collective-permute-start(f32[8,128]{1,0:T(8,128)S(1)} %add.488), channel_id=1, source_target_pairs={{0,16},{1,17},{2,18},{3,19},{4,20},{5,21},{6,22},{7,23},{8,24},{9,... | collective-permute-start | bytes 12296 | tf_op jit(solution)/shard_map/ppermute | solution.py:26
  183.0 7.5 %collective-permute-start.27 = (f32[8,128]{1,0:T(8,128)S(1)}, f32[8,128]{1,0:T(8,128)S(1)}, u32[]{:S(2)}, u32[]{:S(2)}) collective-permute-start(f32[8,128]{1,0:T(8,128)S(1)} %add.491), channel_id=1, source_target_pairs={{0,4},{1,5},{2,6},{3,7},{4,0},{5,1},{6,2},{7,3},{8,12},{9,13},{10,... | collective-permute-start | bytes 12296 | tf_op jit(solution)/shard_map/ppermute | solution.py:26
  (8 other events, 38.7 us)

commit v2 on v1

v2 whole, which is shorter than its diff:
```python
import itertools
import math

import jax
import jax.numpy as jnp
from jax import lax
from jax.experimental import pallas as pl
from jax.experimental.pallas import tpu as pltpu
from jax.sharding import Mesh, PartitionSpec as P

CH = 512
AXES = ("x", "c", "y", "z")
NX, NC, NY, NZ = 4, 2, 4, 8
DEVICES = NX * NC * NY * NZ
OFFSETS = (0, -1, 1, 2)
SPLITS = (512, 512)


def pairs(move):
    out = []
    for x, c, y, z in itertools.product(range(NX), range(NC), range(NY), range(NZ)):
        tx, tc, ty, tz = move(x, c, y, z)
        source = ((x * NC + c) * NY + y) * NZ + z
        target = (((tx % NX) * NC + tc % NC) * NY + ty % NY) * NZ + tz % NZ
        out.append((source, target))
    return out


def send(value, move):
    return lax.ppermute(value, AXES, pairs(move))


def swap_cores(value):
    return send(value, lambda x, c, y, z: (x, 1 - c, y, z))


def first_ring(value, step):
    return send(value, lambda x, c, y, z: (x + step, c, y, z) if c == 0 else (x, c, y + step, z))


def second_ring(value, step):
    return send(value, lambda x, c, y, z: (x, c, y + step, z) if c == 0 else (x + step, c, y, z))


def z_ring(value, step):
    return send(value, lambda x, c, y, z: (x, c, y, z + step))


def dot_kernel(offsets, has_start, index_ref, acts_ref, other_ref, *refs):
    out_ref = refs[-1]
    start_ref = refs[0] if has_start else None
    parts = refs[1:-1] if has_start else refs[:-1]
    total = start_ref[...] if has_start else None
    at = 0
    for part_ref in parts:
        for piece in range(part_ref.shape[0]):
            block = index_ref[offsets[at]]
            lhs = jnp.concatenate((acts_ref[block], other_ref[block]), axis=1)
            product = jnp.dot(lhs, part_ref[piece], preferred_element_type=jnp.float32)
            total = product if total is None else total + product
            at += 1
    out_ref[...] = total


def multiply(index, acts, other, parts, offsets, start=None):
    width, n = acts.shape[1], parts[0].shape[2]
    operands = [acts, other] + ([] if start is None else [start]) + list(parts)
    depth = sum(part.shape[0] * part.shape[1] for part in parts)
    vmem = pl.BlockSpec(memory_space=pltpu.VMEM)
    return pl.pallas_call(
        lambda *refs: dot_kernel(offsets, start is not None, *refs),
        out_shape=jax.ShapeDtypeStruct((width, n), jnp.float32),
        in_specs=[pl.BlockSpec(memory_space=pltpu.SMEM)] + [vmem] * len(operands),
        out_specs=vmem,
        compiler_params=pltpu.CompilerParams(vmem_limit_bytes=40 * 1024 * 1024),
        cost_estimate=pl.CostEstimate(
            flops=2 * width * n * depth, bytes_accessed=2 * depth * (n + width), transcendentals=0
        ),
    )(index, *operands)


def reduce_z(partial, z):
    rows = partial.shape[0] // NZ
    half = rows // 2

    def block(offset):
        return lax.dynamic_slice_in_dim(partial, lax.rem(z + offset + NZ, NZ) * rows, rows, axis=0)

    far = block(4)
    up = z_ring(far[:half], 1)
    down = z_ring(far[half:], -1)
    near_up, near_down = block(3), block(-3)
    up = z_ring(jnp.concatenate((near_up[:half] + up, near_up[half:]), axis=0), 1)
    down = z_ring(jnp.concatenate((near_down[:half], near_down[half:] + down), axis=0), -1)
    for offset in (2, 1):
        up = z_ring(block(offset) + up, 1)
        down = z_ring(block(-offset) + down, -1)
    return block(0) + up + down


def sum_all(value):
    rows = jnp.broadcast_to(value, (DEVICES, 1, 128))
    return jnp.sum(lax.all_to_all(rows, AXES, split_axis=0, concat_axis=0, tiled=True)[:, 0, 0])


def body(activations, key_grads, value_grads, block_lengths):
    tok_count, model_width = activations.shape
    head_width = key_grads.shape[1]
    x, c, y, z = (lax.axis_index(axis) for axis in AXES)
    is_keys = c == 0
    position = (((x * NC + c) * NY + y) * NZ + z) * tok_count
    limit_len = lax.dynamic_index_in_dim(block_lengths, position // CH, keepdims=False)
    rows = lax.broadcasted_iota(jnp.int32, (tok_count, 1), 0)
    is_real = rows + lax.rem(position, CH) < limit_len
    clip_norm = math.sqrt(2.0 * model_width * head_width)

    zero = jnp.zeros((), key_grads.dtype)
    mine = jnp.where(is_real, jnp.where(is_keys, key_grads, value_grads), zero)
    theirs = jnp.where(is_real, jnp.where(is_keys, value_grads, key_grads), zero)
    received = swap_cores(theirs)

    grads = jnp.stack((mine, received))
    before = first_ring(grads, 1)
    after = first_ring(grads, -1)
    opposite = (first_ring(before[:1], 1), first_ring(after[1:], -1))

    owner_rows = model_width // (NX * NY * NZ)
    across = activations.T.reshape(NY, NZ, NX, owner_rows, tok_count)
    across = across.transpose(0, 2, 1, 3, 4).reshape(NY * NX, NZ * owner_rows, tok_count)
    acts = lax.all_to_all(across, ("y", "x"), split_axis=0, concat_axis=0, tiled=True)
    other = swap_cores(acts)

    first, second = jnp.where(is_keys, x, y), jnp.where(is_keys, y, x)
    index = []
    for offset2 in OFFSETS:
        for offset1 in OFFSETS:
            at1, at2 = lax.rem(first + offset1 + 4, 4), lax.rem(second + offset2 + 4, 4)
            index.append(jnp.where(is_keys, at2 * NX + at1, at1 * NX + at2))
    index = jnp.stack(index).astype(jnp.int32)

    owned = []
    low = 0
    for columns in SPLITS:
        cut = slice(low, low + columns)
        low += columns
        lump = jnp.stack(
            (
                grads[:, :, cut],
                before[:, :, cut],
                after[:, :, cut],
                jnp.concatenate((opposite[0][:, :, cut], opposite[1][:, :, cut])),
            )
        ).reshape(4, 2 * tok_count, columns)
        lump_before = second_ring(lump, 1)
        lump_after = second_ring(lump, -1)
        opposite_a = second_ring(lump_before[:2], 1)
        opposite_b = second_ring(lump_after[2:], -1)
        weight = multiply(index, acts, other, [lump, lump_before, lump_after], range(12))
        weight = multiply(index, acts, other, [opposite_a, opposite_b], range(12, 16), weight)
        owned.append(reduce_z(weight, z))

    total = sum_all(sum(jnp.sum(part * part) for part in owned))
    owned = jnp.concatenate(owned, axis=1)
    half = owned.shape[0] // 2
    upper, lower = owned[:half], owned[half:]
    kept = jnp.where(is_keys, upper, lower)
    swapped = swap_cores(jnp.where(is_keys, lower, upper))
    factor = jnp.minimum(1.0, clip_norm / jnp.sqrt(total))
    key_clipped = (jnp.where(is_keys, kept, swapped) * factor).astype(jnp.bfloat16)
    value_clipped = (jnp.where(is_keys, swapped, kept) * factor).astype(jnp.bfloat16)
    return key_clipped, value_clipped


def solution(mesh):
    fine = Mesh(mesh.devices.reshape(NX, NC, NY, NZ), AXES)
    tokens = P(AXES, None)
    owners = P(("y", "z", "x", "c"), None)
    return jax.shard_map(
        body,
        mesh=fine,
        in_specs=(tokens, tokens, tokens, P()),
        out_specs=(owners, owners),
        check_vma=False,
    )
```

time: 193 us -> 174 us (0.902)
  the two profiles are of different devices: /device:TPU:62 before, /device:TPU:1 now
where the time goes in v2:
time: 174 us; the launch traced here: 173 us
  starting transfers between devices  72.4 us (42%)
  waiting for transfers between devices  61.9 us (36%)
  local copies, waits for them, and re-layouts  19 us (11%)
  Pallas kernels  12 us (7%)
  other arithmetic  4.96 us (3%)
  between operations  3.05 us (2%)
    ppermute x31, waiting for transfers between devices, send(): return lax.ppermute(value, AXES, pairs(move))  51.1 us
    ppermute x31, starting transfers between devices, send(): return lax.ppermute(value, AXES, pairs(move))  45.3 us
    all_to_all x1, starting transfers between devices, sum_all(): lax.all_to_all(rows, AXES, split_axis=0, concat_axis=0, tiled=True)[:, 0, 0]  19.4 us
    pallas_call x4, Pallas kernels, multiply(): pl.pallas_call(lambda *refs: dot_kernel(offsets, start is not None, *refs...  12 us
    all_to_all x1, waiting for transfers between devices, sum_all(): lax.all_to_all(rows, AXES, split_axis=0, concat_axis=0, tiled=True)[:, 0, 0]  10.8 us
    all_to_all x1, starting transfers between devices, body(): lax.all_to_all(across, ('y', 'x'), split_axis=0, concat_axis=0, tiled=True)  7.72 us
    unnamed x33, local copies, waits for them, and re-layouts  7.51 us
  transfers between devices with their start and end apart: 33, of which 12 were waited for; matrix products, arithmetic and copies ran while one was open for 7% of the time, Pallas kernels for 7%

profile of v2, /device:TPU:1, one launch (start us, length us, event | category | flops | bytes accessed | tf_op | source)
XLA Modules:
  0.0 173.4 jit_solution(15524678918938730037)
XLA Ops:
  0.6 3.2 %copy.11 = bf16[128,8192]{0,1:T(8,128)(2,1)S(1)} copy(bf16[128,8192]{1,0:T(8,128)(2,1)} %param.4) | data formatting | bytes 4194304 | tf_op args[0]
  5.5 7.7 %all-to-all-start = ((bf16[16,512,128]{2,1,0:T(8,128)(2,1)}), bf16[16,512,128]{2,1,0:T(8,128)(2,1)S(1)}, u32[]{:S(2)}, u32[]{:S(2)}) async-start(bf16[16,512,128]{2,1,0:T(8,128)(2,1)} %bitcast.34), calls=%async_computation | async-start | bytes 4194304 | tf_op jit(solution)/shard_map/all_to_all | solution.py:130
  20.6 23.1 %collective-permute-done.2 = bf16[2,128,1024]{2,1,0:T(8,128)(2,1)S(1)} collective-permute-done((bf16[2,128,1024]{2,1,0:T(8,128)(2,1)S(1)}, bf16[2,128,1024]{2,1,0:T(8,128)(2,1)S(1)}, u32[]{:S(2)}, u32[]{:S(2)}) %collective-permute-start.2) | collective-permute-done | bytes 524320 | tf_op jit(solution)/shard_map/ppermute | solution.py:30
  45.2 2.7 %collective-permute-start.5 = (bf16[1,128,1024]{2,1,0:T(8,128)(2,1)}, bf16[1,128,1024]{2,1,0:T(8,128)(2,1)}, u32[]{:S(2)}, u32[]{:S(2)}) collective-permute-start(bf16[1,128,1024]{2,1,0:T(8,128)(2,1)} %slice.130), channel_id=1, source_target_pairs={{0,192},{1,193},{2,194},{3,195},{4,196},{5,197},{6,198},{7,199},{8... | collective-permute-start | bytes 786440 | tf_op jit(solution)/shard_map/ppermute | solution.py:30
  49.3 5.0 %collective-permute-start = (bf16[16,512,128]{2,1,0:T(8,128)(2,1)S(1)}, bf16[16,512,128]{2,1,0:T(8,128)(2,1)}, u32[]{:S(2)}, u32[]{:S(2)}) collective-permute-start(bf16[16,512,128]{2,1,0:T(8,128)(2,1)S(1)} %all-to-all-done.refs_1_), channel_id=1, source_target_pairs={{0,32},{1,33},{2,34},{3,35},{4,36},{5,37},{6,38},{7,39},{8,40},{9,... | collective-permute-start | bytes 6291464 | tf_op jit(solution)/shard_map/ppermute | solution.py:30
  56.7 2.7 %collective-permute-start.7 = (bf16[4,256,512]{2,1,0:T(8,128)(2,1)S(1)}, bf16[4,256,512]{2,1,0:T(8,128)(2,1)S(1)}, u32[]{:S(2)}, u32[]{:S(2)}) collective-permute-start(bf16[4,256,512]{2,1,0:T(8,128)(2,1)S(1)} %pad_maximum_fusion.refs_3_), channel_id=1, source_target_pairs={{0,24},{1,25},{2,26},{3,27},{4,28},{5,29},{6,30},{7,31},{8,0},{9,1... | collective-permute-start | bytes 3145736 | tf_op jit(solution)/shard_map/ppermute | solution.py:30
  59.6 2.7 %collective-permute-start.19 = (bf16[4,256,512]{2,1,0:T(8,128)(2,1)S(1)}, bf16[4,256,512]{2,1,0:T(8,128)(2,1)S(1)}, u32[]{:S(2)}, u32[]{:S(2)}) collective-permute-start(bf16[4,256,512]{2,1,0:T(8,128)(2,1)S(1)} %pad_maximum_fusion.1.refs_3_), channel_id=1, source_target_pairs={{0,24},{1,25},{2,26},{3,27},{4,28},{5,29},{6,30},{7,31},{8,0},{9,1... | collective-permute-start | bytes 3145736 | tf_op jit(solution)/shard_map/ppermute | solution.py:30
  62.2 9.6 %collective-permute-done.6.refs_4_ = bf16[4,256,512]{2,1,0:T(8,128)(2,1)S(1)} collective-permute-done((bf16[4,256,512]{2,1,0:T(8,128)(2,1)S(1)}, bf16[4,256,512]{2,1,0:T(8,128)(2,1)S(1)}, u32[]{:S(2)}, u32[]{:S(2)}) %collective-permute-start.6) | collective-permute-done | bytes 1048608 | tf_op jit(solution)/shard_map/ppermute | solution.py:30
  73.6 2.7 %collective-permute-start.9 = (bf16[2,256,512]{2,1,0:T(8,128)(2,1)}, bf16[2,256,512]{2,1,0:T(8,128)(2,1)}, u32[]{:S(2)}, u32[]{:S(2)}) collective-permute-start(bf16[2,256,512]{2,1,0:T(8,128)(2,1)} %slice.133), channel_id=1, source_target_pairs={{0,24},{1,25},{2,26},{3,27},{4,28},{5,29},{6,30},{7,31},{8,0},{9,1... | collective-permute-start | bytes 1572872 | tf_op jit(solution)/shard_map/ppermute | solution.py:30
  76.3 6.7 %collective-permute-done.18.refs_4_ = bf16[4,256,512]{2,1,0:T(8,128)(2,1)S(1)} collective-permute-done((bf16[4,256,512]{2,1,0:T(8,128)(2,1)S(1)}, bf16[4,256,512]{2,1,0:T(8,128)(2,1)S(1)}, u32[]{:S(2)}, u32[]{:S(2)}) %collective-permute-start.18) | collective-permute-done | bytes 1048608 | tf_op jit(solution)/shard_map/ppermute | solution.py:30
  85.4 2.4 %collective-permute-start.21 = (bf16[2,256,512]{2,1,0:T(8,128)(2,1)}, bf16[2,256,512]{2,1,0:T(8,128)(2,1)}, u32[]{:S(2)}, u32[]{:S(2)}) collective-permute-start(bf16[2,256,512]{2,1,0:T(8,128)(2,1)} %slice.141), channel_id=1, source_target_pairs={{0,24},{1,25},{2,26},{3,27},{4,28},{5,29},{6,30},{7,31},{8,0},{9,1... | collective-permute-start | bytes 1572872 | tf_op jit(solution)/shard_map/ppermute | solution.py:30
  91.6 3.4 %shard_map.59.refs_3_ = f32[512,512]{1,0:T(8,128)S(1)} custom-call(s32[16]{0:T(128)S(1)} %stack.106.refs_0_, bf16[16,512,128]{2,1,0:T(8,128)(2,1)S(1)} %all-to-all-done.refs_1_, bf16[16,512,128]{2,1,0:T(8,128)(2,1)} %collective-permute-done.refs_2_, bf16[4,256,512]{2,1,0:T(8,128)(2,1)S(1)} %copy-done.1, bf16[4,256,512]{2,1,0:T(8,128)(2,1)S(1)} %copy-done.7, ...), custom_call_target="tpu_custom_call" | custom-call | flops 1610612736 | bytes 6291456 | tf_op jit(solution)/shard_map/pallas_call | solution.py:70
  95.0 2.7 %shard_map.60 = f32[512,512]{1,0:T(8,128)S(1)} custom-call(s32[16]{0:T(128)S(1)} %stack.106.refs_0_, bf16[16,512,128]{2,1,0:T(8,128)(2,1)S(1)} %all-to-all-done.refs_1_, bf16[16,512,128]{2,1,0:T(8,128)(2,1)} %collective-permute-done.refs_2_, f32[512,512]{1,0:T(8,128)S(1)} %shard_map.59.refs_3_, bf16[2,256,512]{2,1,0:T(8,128)(2,1)} %collective-permute-done.8.refs_4_, ...), custom_call_target="tpu_custom_call" | custom-call | flops 536870912 | bytes 2097152 | tf_op jit(solution)/shard_map/pallas_call | solution.py:70
  99.5 4.0 %collective-permute-start.14 = (f32[32,512]{1,0:T(8,128)S(1)}, f32[32,512]{1,0:T(8,128)S(1)}, u32[]{:S(2)}, u32[]{:S(2)}) collective-permute-start(f32[32,512]{1,0:T(8,128)S(1)} %get-tuple-element.13), channel_id=1, source_target_pairs={{0,7},{1,0},{2,1},{3,2},{4,3},{5,4},{6,5},{7,6},{8,15},{9,8},{10,9... | collective-permute-start | bytes 196616 | tf_op jit(solution)/shard_map/ppermute | solution.py:30
  103.5 3.4 %shard_map.61.refs_3_ = f32[512,512]{1,0:T(8,128)S(1)} custom-call(s32[16]{0:T(128)S(1)} %stack.106.refs_0_, bf16[16,512,128]{2,1,0:T(8,128)(2,1)S(1)} %all-to-all-done.refs_1_, bf16[16,512,128]{2,1,0:T(8,128)(2,1)} %collective-permute-done.refs_2_, bf16[4,256,512]{2,1,0:T(8,128)(2,1)S(1)} %pad_maximum_fusion.1.refs_3_, bf16[4,256,512]{2,1,0:T(8,128)(2,1)S(1)} %copy-done.3, ...), custom_call_target="tpu_custom_call" | custom-call | flops 1610612736 | bytes 6291456 | tf_op jit(solution)/shard_map/pallas_call | solution.py:70
  106.9 2.5 %shard_map.62 = f32[512,512]{1,0:T(8,128)S(1)} custom-call(s32[16]{0:T(128)S(1)} %stack.106.refs_0_, bf16[16,512,128]{2,1,0:T(8,128)(2,1)S(1)} %all-to-all-done.refs_1_, bf16[16,512,128]{2,1,0:T(8,128)(2,1)} %collective-permute-done.refs_2_, f32[512,512]{1,0:T(8,128)S(1)} %shard_map.61.refs_3_, bf16[2,256,512]{2,1,0:T(8,128)(2,1)} %collective-permute-done.20.refs_4_, ...), custom_call_target="tpu_custom_call" | custom-call | flops 536870912 | bytes 2097152 | tf_op jit(solution)/shard_map/pallas_call | solution.py:70
  109.6 2.7 %collective-permute-start.26 = (f32[32,512]{1,0:T(8,128)S(1)}, f32[32,512]{1,0:T(8,128)S(1)}, u32[]{:S(2)}, u32[]{:S(2)}) collective-permute-start(f32[32,512]{1,0:T(8,128)S(1)} %get-tuple-element.21), channel_id=1, source_target_pairs={{0,7},{1,0},{2,1},{3,2},{4,3},{5,4},{6,5},{7,6},{8,15},{9,8},{10,9... | collective-permute-start | bytes 196616 | tf_op jit(solution)/shard_map/ppermute | solution.py:30
  114.0 2.7 %collective-permute-start.27 = (f32[64,512]{1,0:T(8,128)S(1)}, f32[64,512]{1,0:T(8,128)S(1)}, u32[]{:S(2)}, u32[]{:S(2)}) collective-permute-start(f32[64,512]{1,0:T(8,128)S(1)} %pad_maximum_fusion.9), channel_id=1, source_target_pairs={{0,7},{1,0},{2,1},{3,2},{4,3},{5,4},{6,5},{7,6},{8,15},{9,8},{10,9... | collective-permute-start | bytes 393224 | tf_op jit(solution)/shard_map/ppermute | solution.py:30
  118.8 3.0 %collective-permute-done.23 = f32[64,512]{1,0:T(8,128)S(1)} collective-permute-done((f32[64,512]{1,0:T(8,128)S(1)}, f32[64,512]{1,0:T(8,128)S(1)}, u32[]{:S(2)}, u32[]{:S(2)}) %collective-permute-start.23) | collective-permute-done | bytes 131104 | tf_op jit(solution)/shard_map/ppermute | solution.py:30
  121.9 2.7 %collective-permute-done.12 = f32[64,512]{1,0:T(8,128)S(1)} collective-permute-done((f32[64,512]{1,0:T(8,128)S(1)}, f32[64,512]{1,0:T(8,128)S(1)}, u32[]{:S(2)}, u32[]{:S(2)}) %collective-permute-start.12) | collective-permute-done | bytes 131104 | tf_op jit(solution)/shard_map/ppermute | solution.py:30
  133.7 2.4 %collective-permute-done.29 = f32[64,512]{1,0:T(8,128)S(1)} collective-permute-done((f32[64,512]{1,0:T(8,128)S(1)}, f32[64,512]{1,0:T(8,128)S(1)}, u32[]{:S(2)}, u32[]{:S(2)}) %collective-permute-start.29) | collective-permute-done | bytes 131104 | tf_op jit(solution)/shard_map/ppermute | solution.py:30
  138.7 19.4 %all-to-all-start.1 = ((f32[256,1,128]{2,1,0:T(1,128)}), f32[256,1,128]{2,1,0:T(1,128)S(1)}, u32[]{:S(2)}, u32[]{:S(2)}) async-start(f32[256,1,128]{2,1,0:T(1,128)} %broadcast_in_dim.21), calls=%async_computation.1 | async-start | bytes 262144 | tf_op jit(solution)/shard_map/all_to_all | solution.py:103
  158.1 2.2 %collective-permute-start.30 = (f32[32,1024]{1,0:T(8,128)S(1)}, f32[32,1024]{1,0:T(8,128)S(1)}, u32[]{:S(2)}, u32[]{:S(2)}) collective-permute-start(f32[32,1024]{1,0:T(8,128)S(1)} %broadcast_select_fusion), channel_id=1, source_target_pairs={{0,32},{1,33},{2,34},{3,35},{4,36},{5,37},{6,38},{7,39},{8,40},{9,... | collective-permute-start | bytes 393224 | tf_op jit(solution)/shard_map/ppermute | solution.py:30
  160.3 10.8 %all-to-all-done.1 = f32[256,1,128]{2,1,0:T(1,128)S(1)} async-done(((f32[256,1,128]{2,1,0:T(1,128)}), f32[256,1,128]{2,1,0:T(1,128)S(1)}, u32[]{:S(2)}, u32[]{:S(2)}) %all-to-all-start.1) | async-done | bytes 131104 | tf_op jit(solution)/shard_map/all_to_all | solution.py:103
  (119 shorter events, 40.0 us)
Async XLA Ops:
  5.5 43.9 %all-to-all-start = ((bf16[16,512,128]{2,1,0:T(8,128)(2,1)}), bf16[16,512,128]{2,1,0:T(8,128)(2,1)S(1)}, u32[]{:S(2)}, u32[]{:S(2)}) async-start(bf16[16,512,128]{2,1,0:T(8,128)(2,1)} %bitcast.34), calls=%async_computation | async-start | bytes 4194304 | tf_op jit(solution)/shard_map/all_to_all | solution.py:130
  16.9 26.9 %collective-permute-start.2 = (bf16[2,128,1024]{2,1,0:T(8,128)(2,1)S(1)}, bf16[2,128,1024]{2,1,0:T(8,128)(2,1)S(1)}, u32[]{:S(2)}, u32[]{:S(2)}) collective-permute-start(bf16[2,128,1024]{2,1,0:T(8,128)(2,1)S(1)} %pad_maximum_fusion.2), channel_id=1, source_target_pairs={{0,64},{1,65},{2,66},{3,67},{4,68},{5,69},{6,70},{7,71},{8,72},{9,... | collective-permute-start | bytes 1572872 | tf_op jit(solution)/shard_map/ppermute | solution.py:30
  18.6 25.9 %collective-permute-start.3 = (bf16[2,128,1024]{2,1,0:T(8,128)(2,1)S(1)}, bf16[2,128,1024]{2,1,0:T(8,128)(2,1)S(1)}, u32[]{:S(2)}, u32[]{:S(2)}) collective-permute-start(bf16[2,128,1024]{2,1,0:T(8,128)(2,1)S(1)} %pad_maximum_fusion.2), channel_id=1, source_target_pairs={{0,192},{1,193},{2,194},{3,195},{4,196},{5,197},{6,198},{7,199},{8... | collective-permute-start | bytes 1572872 | tf_op jit(solution)/shard_map/ppermute | solution.py:30
  44.5 9.9 %collective-permute-start.4 = (bf16[1,128,1024]{2,1,0:T(8,128)(2,1)}, bf16[1,128,1024]{2,1,0:T(8,128)(2,1)}, u32[]{:S(2)}, u32[]{:S(2)}) collective-permute-start(bf16[1,128,1024]{2,1,0:T(8,128)(2,1)} %slice.128), channel_id=1, source_target_pairs={{0,64},{1,65},{2,66},{3,67},{4,68},{5,69},{6,70},{7,71},{8,72},{9,... | collective-permute-start | bytes 786440 | tf_op jit(solution)/shard_map/ppermute | solution.py:30
  45.2 10.2 %collective-permute-start.5 = (bf16[1,128,1024]{2,1,0:T(8,128)(2,1)}, bf16[1,128,1024]{2,1,0:T(8,128)(2,1)}, u32[]{:S(2)}, u32[]{:S(2)}) collective-permute-start(bf16[1,128,1024]{2,1,0:T(8,128)(2,1)} %slice.130), channel_id=1, source_target_pairs={{0,192},{1,193},{2,194},{3,195},{4,196},{5,197},{6,198},{7,199},{8... | collective-permute-start | bytes 786440 | tf_op jit(solution)/shard_map/ppermute | solution.py:30
  49.3 38.6 %collective-permute-start = (bf16[16,512,128]{2,1,0:T(8,128)(2,1)S(1)}, bf16[16,512,128]{2,1,0:T(8,128)(2,1)}, u32[]{:S(2)}, u32[]{:S(2)}) collective-permute-start(bf16[16,512,128]{2,1,0:T(8,128)(2,1)S(1)} %all-to-all-done.refs_1_), channel_id=1, source_target_pairs={{0,32},{1,33},{2,34},{3,35},{4,36},{5,37},{6,38},{7,39},{8,40},{9,... | collective-permute-start | bytes 6291464 | tf_op jit(solution)/shard_map/ppermute | solution.py:30
  56.6 15.2 %collective-permute-start.6 = (bf16[4,256,512]{2,1,0:T(8,128)(2,1)S(1)}, bf16[4,256,512]{2,1,0:T(8,128)(2,1)S(1)}, u32[]{:S(2)}, u32[]{:S(2)}) collective-permute-start(bf16[4,256,512]{2,1,0:T(8,128)(2,1)S(1)} %pad_maximum_fusion.refs_3_), channel_id=1, source_target_pairs={{0,8},{1,9},{2,10},{3,11},{4,12},{5,13},{6,14},{7,15},{8,16},{9,17... | collective-permute-start | bytes 3145736 | tf_op jit(solution)/shard_map/ppermute | solution.py:30
  56.7 16.1 %collective-permute-start.7 = (bf16[4,256,512]{2,1,0:T(8,128)(2,1)S(1)}, bf16[4,256,512]{2,1,0:T(8,128)(2,1)S(1)}, u32[]{:S(2)}, u32[]{:S(2)}) collective-permute-start(bf16[4,256,512]{2,1,0:T(8,128)(2,1)S(1)} %pad_maximum_fusion.refs_3_), channel_id=1, source_target_pairs={{0,24},{1,25},{2,26},{3,27},{4,28},{5,29},{6,30},{7,31},{8,0},{9,1... | collective-permute-start | bytes 3145736 | tf_op jit(solution)/shard_map/ppermute | solution.py:30
  59.5 23.6 %collective-permute-start.18 = (bf16[4,256,512]{2,1,0:T(8,128)(2,1)S(1)}, bf16[4,256,512]{2,1,0:T(8,128)(2,1)S(1)}, u32[]{:S(2)}, u32[]{:S(2)}) collective-permute-start(bf16[4,256,512]{2,1,0:T(8,128)(2,1)S(1)} %pad_maximum_fusion.1.refs_3_), channel_id=1, source_target_pairs={{0,8},{1,9},{2,10},{3,11},{4,12},{5,13},{6,14},{7,15},{8,16},{9,17... | collective-permute-start | bytes 3145736 | tf_op jit(solution)/shard_map/ppermute | solution.py:30
  59.6 24.4 %collective-permute-start.19 = (bf16[4,256,512]{2,1,0:T(8,128)(2,1)S(1)}, bf16[4,256,512]{2,1,0:T(8,128)(2,1)S(1)}, u32[]{:S(2)}, u32[]{:S(2)}) collective-permute-start(bf16[4,256,512]{2,1,0:T(8,128)(2,1)S(1)} %pad_maximum_fusion.1.refs_3_), channel_id=1, source_target_pairs={{0,24},{1,25},{2,26},{3,27},{4,28},{5,29},{6,30},{7,31},{8,0},{9,1... | collective-permute-start | bytes 3145736 | tf_op jit(solution)/shard_map/ppermute | solution.py:30
  72.7 22.3 %collective-permute-start.8 = (bf16[2,256,512]{2,1,0:T(8,128)(2,1)}, bf16[2,256,512]{2,1,0:T(8,128)(2,1)}, u32[]{:S(2)}, u32[]{:S(2)}) collective-permute-start(bf16[2,256,512]{2,1,0:T(8,128)(2,1)} %slice.132), channel_id=1, source_target_pairs={{0,8},{1,9},{2,10},{3,11},{4,12},{5,13},{6,14},{7,15},{8,16},{9,17... | collective-permute-start | bytes 1572872 | tf_op jit(solution)/shard_map/ppermute | solution.py:30
  73.6 21.4 %collective-permute-start.9 = (bf16[2,256,512]{2,1,0:T(8,128)(2,1)}, bf16[2,256,512]{2,1,0:T(8,128)(2,1)}, u32[]{:S(2)}, u32[]{:S(2)}) collective-permute-start(bf16[2,256,512]{2,1,0:T(8,128)(2,1)} %slice.133), channel_id=1, source_target_pairs={{0,24},{1,25},{2,26},{3,27},{4,28},{5,29},{6,30},{7,31},{8,0},{9,1... | collective-permute-start | bytes 1572872 | tf_op jit(solution)/shard_map/ppermute | solution.py:30
  84.0 22.9 %collective-permute-start.20 = (bf16[2,256,512]{2,1,0:T(8,128)(2,1)}, bf16[2,256,512]{2,1,0:T(8,128)(2,1)}, u32[]{:S(2)}, u32[]{:S(2)}) collective-permute-start(bf16[2,256,512]{2,1,0:T(8,128)(2,1)} %slice.140), channel_id=1, source_target_pairs={{0,8},{1,9},{2,10},{3,11},{4,12},{5,13},{6,14},{7,15},{8,16},{9,17... | collective-permute-start | bytes 1572872 | tf_op jit(solution)/shard_map/ppermute | solution.py:30
  85.4 21.5 %collective-permute-start.21 = (bf16[2,256,512]{2,1,0:T(8,128)(2,1)}, bf16[2,256,512]{2,1,0:T(8,128)(2,1)}, u32[]{:S(2)}, u32[]{:S(2)}) collective-permute-start(bf16[2,256,512]{2,1,0:T(8,128)(2,1)} %slice.141), channel_id=1, source_target_pairs={{0,24},{1,25},{2,26},{3,27},{4,28},{5,29},{6,30},{7,31},{8,0},{9,1... | collective-permute-start | bytes 1572872 | tf_op jit(solution)/shard_map/ppermute | solution.py:30
  97.7 14.5 %collective-permute-start.10 = (f32[32,512]{1,0:T(8,128)S(1)}, f32[32,512]{1,0:T(8,128)S(1)}, u32[]{:S(2)}, u32[]{:S(2)}) collective-permute-start(f32[32,512]{1,0:T(8,128)S(1)} %get-tuple-element.12), channel_id=1, source_target_pairs={{0,1},{1,2},{2,3},{3,4},{4,5},{5,6},{6,7},{7,0},{8,9},{9,10},{10,1... | collective-permute-start | bytes 196616 | tf_op jit(solution)/shard_map/ppermute | solution.py:30
  99.5 12.8 %collective-permute-start.14 = (f32[32,512]{1,0:T(8,128)S(1)}, f32[32,512]{1,0:T(8,128)S(1)}, u32[]{:S(2)}, u32[]{:S(2)}) collective-permute-start(f32[32,512]{1,0:T(8,128)S(1)} %get-tuple-element.13), channel_id=1, source_target_pairs={{0,7},{1,0},{2,1},{3,2},{4,3},{5,4},{6,5},{7,6},{8,15},{9,8},{10,9... | collective-permute-start | bytes 196616 | tf_op jit(solution)/shard_map/ppermute | solution.py:30
  112.3 9.6 %collective-permute-start.15 = (f32[64,512]{1,0:T(8,128)S(1)}, f32[64,512]{1,0:T(8,128)S(1)}, u32[]{:S(2)}, u32[]{:S(2)}) collective-permute-start(f32[64,512]{1,0:T(8,128)S(1)} %pad_maximum_fusion.7), channel_id=1, source_target_pairs={{0,7},{1,0},{2,1},{3,2},{4,3},{5,4},{6,5},{7,6},{8,15},{9,8},{10,9... | collective-permute-start | bytes 393224 | tf_op jit(solution)/shard_map/ppermute | solution.py:30
  112.5 5.1 %collective-permute-start.11 = (f32[64,512]{1,0:T(8,128)S(1)}, f32[64,512]{1,0:T(8,128)S(1)}, u32[]{:S(2)}, u32[]{:S(2)}) collective-permute-start(f32[64,512]{1,0:T(8,128)S(1)} %pad_maximum_fusion.6), channel_id=1, source_target_pairs={{0,1},{1,2},{2,3},{3,4},{4,5},{5,6},{6,7},{7,0},{8,9},{9,10},{10,1... | collective-permute-start | bytes 393224 | tf_op jit(solution)/shard_map/ppermute | solution.py:30
  114.0 12.3 %collective-permute-start.27 = (f32[64,512]{1,0:T(8,128)S(1)}, f32[64,512]{1,0:T(8,128)S(1)}, u32[]{:S(2)}, u32[]{:S(2)}) collective-permute-start(f32[64,512]{1,0:T(8,128)S(1)} %pad_maximum_fusion.9), channel_id=1, source_target_pairs={{0,7},{1,0},{2,1},{3,2},{4,3},{5,4},{6,5},{7,6},{8,15},{9,8},{10,9... | collective-permute-start | bytes 393224 | tf_op jit(solution)/shard_map/ppermute | solution.py:30
  117.7 7.0 %collective-permute-start.12 = (f32[64,512]{1,0:T(8,128)S(1)}, f32[64,512]{1,0:T(8,128)S(1)}, u32[]{:S(2)}, u32[]{:S(2)}) collective-permute-start(f32[64,512]{1,0:T(8,128)S(1)} %dynamic-slice_add_fusion.6), channel_id=1, source_target_pairs={{0,1},{1,2},{2,3},{3,4},{4,5},{5,6},{6,7},{7,0},{8,9},{9,10},{10,1... | collective-permute-start | bytes 393224 | tf_op jit(solution)/shard_map/ppermute | solution.py:30
  124.8 8.2 %collective-permute-start.13 = (f32[64,512]{1,0:T(8,128)S(1)}, f32[64,512]{1,0:T(8,128)S(1)}, u32[]{:S(2)}, u32[]{:S(2)}) collective-permute-start(f32[64,512]{1,0:T(8,128)S(1)} %get-tuple-element.6), channel_id=1, source_target_pairs={{0,1},{1,2},{2,3},{3,4},{4,5},{5,6},{6,7},{7,0},{8,9},{9,10},{10,1... | collective-permute-start | bytes 393224 | tf_op jit(solution)/shard_map/ppermute | solution.py:30
  127.9 5.8 %collective-permute-start.25 = (f32[64,512]{1,0:T(8,128)S(1)}, f32[64,512]{1,0:T(8,128)S(1)}, u32[]{:S(2)}, u32[]{:S(2)}) collective-permute-start(f32[64,512]{1,0:T(8,128)S(1)} %get-tuple-element.14), channel_id=1, source_target_pairs={{0,1},{1,2},{2,3},{3,4},{4,5},{5,6},{6,7},{7,0},{8,9},{9,10},{10,1... | collective-permute-start | bytes 393224 | tf_op jit(solution)/shard_map/ppermute | solution.py:30
  138.7 32.4 %all-to-all-start.1 = ((f32[256,1,128]{2,1,0:T(1,128)}), f32[256,1,128]{2,1,0:T(1,128)S(1)}, u32[]{:S(2)}, u32[]{:S(2)}) async-start(f32[256,1,128]{2,1,0:T(1,128)} %broadcast_in_dim.21), calls=%async_computation.1 | async-start | bytes 262144 | tf_op jit(solution)/shard_map/all_to_all | solution.py:103
  158.1 14.6 %collective-permute-start.30 = (f32[32,1024]{1,0:T(8,128)S(1)}, f32[32,1024]{1,0:T(8,128)S(1)}, u32[]{:S(2)}, u32[]{:S(2)}) collective-permute-start(f32[32,1024]{1,0:T(8,128)S(1)} %broadcast_select_fusion), channel_id=1, source_target_pairs={{0,32},{1,33},{2,34},{3,35},{4,36},{5,37},{6,38},{7,39},{8,40},{9,... | collective-permute-start | bytes 393224 | tf_op jit(solution)/shard_map/ppermute | solution.py:30
  (25 other events, 161.5 us)

commit v3 on v2

--- a/solution.py
+++ b/solution.py
@@ -1,3 +1,4 @@
+import functools
 import itertools
 import math
 
@@ -46,37 +47,112 @@
     return send(value, lambda x, c, y, z: (x, c, y, z + step))
 
 
+def mask_kernel(splits, place_ref, lengths_ref, keys_ref, values_ref, *out_refs):
+    is_keys = place_ref[0] == 0
+    limit = lengths_ref[place_ref[1]] - place_ref[2]
+    low = 0
+    for i, columns in enumerate(splits):
+        cut = pl.ds(low, columns)
+        low += columns
+        keys, values = keys_ref[:, cut], values_ref[:, cut]
+        rows = lax.broadcasted_iota(jnp.int32, keys.shape, 0)
+        zero = jnp.zeros_like(keys)
+        keys = jnp.where(rows < limit, keys, zero)
+        values = jnp.where(rows < limit, values, zero)
+        out_refs[2 * i][...] = jnp.where(is_keys, keys, values)
+        out_refs[2 * i + 1][...] = jnp.where(is_keys, values, keys)
+
+
+def mask(place, block_lengths, key_grads, value_grads):
+    tok_count = key_grads.shape[0]
+    smem = pl.BlockSpec(memory_space=pltpu.SMEM)
+    vmem = pl.BlockSpec(memory_space=pltpu.VMEM)
+    return pl.pallas_call(
+        functools.partial(mask_kernel, SPLITS),
+        out_shape=[
+            jax.ShapeDtypeStruct((tok_count, columns), key_grads.dtype)
+            for columns in SPLITS
+            for _ in range(2)
+        ],
+        in_specs=[smem, smem, vmem, vmem],
+        out_specs=[vmem] * (2 * len(SPLITS)),
+        cost_estimate=pl.CostEstimate(
+            flops=key_grads.size, bytes_accessed=8 * key_grads.size, transcendentals=0
+        ),
+    )(place, block_lengths, key_grads, value_grads)
+
+
+def transpose_kernel(acts_ref, after_ref, out_ref):
+    owner_rows = out_ref.shape[1] // NZ
+    for at in range(0, acts_ref.shape[1], 128):
+        turned = acts_ref[:, at : at + 128].T
+        for low in range(0, 128, owner_rows):
+            piece = (at + low) // owner_rows
+            y, z, x = piece // (NZ * NX), piece // NX % NZ, piece % NX
+            out_ref[y * NX + x, z * owner_rows : (z + 1) * owner_rows, :] = turned[
+                low : low + owner_rows
+            ]
+
+
+def transpose(acts, after):
+    tok_count, model_width = acts.shape
+    vmem = pl.BlockSpec(memory_space=pltpu.VMEM)
+    return pl.pallas_call(
+        transpose_kernel,
+        out_shape=jax.ShapeDtypeStruct(
+            (NX * NY, model_width // (NX * NY), tok_count), acts.dtype
+        ),
+        in_specs=[vmem, pl.BlockSpec(memory_space=pl.ANY)],
+        out_specs=vmem,
+        compiler_params=pltpu.CompilerParams(vmem_limit_bytes=24 * 1024 * 1024),
+        cost_estimate=pl.CostEstimate(
+            flops=acts.size, bytes_accessed=4 * acts.size, transcendentals=0
+        ),
+    )(acts, after)
+
+
 def dot_kernel(offsets, has_start, index_ref, acts_ref, other_ref, *refs):
     out_ref = refs[-1]
     start_ref = refs[0] if has_start else None
     parts = refs[1:-1] if has_start else refs[:-1]
-    total = start_ref[...] if has_start else None
-    at = 0
-    for part_ref in parts:
-        for piece in range(part_ref.shape[0]):
-            block = index_ref[offsets[at]]
-            lhs = jnp.concatenate((acts_ref[block], other_ref[block]), axis=1)
-            product = jnp.dot(lhs, part_ref[piece], preferred_element_type=jnp.float32)
+    tile = 128
+    for row in range(0, out_ref.shape[0], tile):
+        cut = pl.ds(row, tile)
+        total = start_ref[cut, :] if has_start else None
+        for part_ref, places in zip(parts, offsets):
+            blocks = []
+            for place in places:
+                block = index_ref[place]
+                blocks += [acts_ref[block, cut, :], other_ref[block, cut, :]]
+            product = jnp.dot(
+                jnp.concatenate(blocks, axis=1), part_ref[...], preferred_element_type=jnp.float32
+            )
             total = product if total is None else total + product
-            at += 1
-    out_ref[...] = total
-
-
-def multiply(index, acts, other, parts, offsets, start=None):
-    width, n = acts.shape[1], parts[0].shape[2]
+        out_ref[cut, :] = total
+
+
+def multiply(index, acts, other, parts, offsets, start=None, after=()):
+    width, n = acts.shape[1], parts[0].shape[1]
     operands = [acts, other] + ([] if start is None else [start]) + list(parts)
-    depth = sum(part.shape[0] * part.shape[1] for part in parts)
+    depth = sum(part.shape[0] for part in parts)
     vmem = pl.BlockSpec(memory_space=pltpu.VMEM)
+
+    def kernel(*refs):
+        read = refs[: 1 + len(operands)]
+        dot_kernel(offsets, start is not None, *read, refs[-1])
+
     return pl.pallas_call(
-        lambda *refs: dot_kernel(offsets, start is not None, *refs),
+        kernel,
         out_shape=jax.ShapeDtypeStruct((width, n), jnp.float32),
-        in_specs=[pl.BlockSpec(memory_space=pltpu.SMEM)] + [vmem] * len(operands),
+        in_specs=[pl.BlockSpec(memory_space=pltpu.SMEM)]
+        + [vmem] * len(operands)
+        + [pl.BlockSpec(memory_space=pl.ANY)] * len(after),
         out_specs=vmem,
         compiler_params=pltpu.CompilerParams(vmem_limit_bytes=40 * 1024 * 1024),
         cost_estimate=pl.CostEstimate(
             flops=2 * width * n * depth, bytes_accessed=2 * depth * (n + width), transcendentals=0
         ),
-    )(index, *operands)
+    )(index, *operands, *after)
 
 
 def reduce_z(partial, z):
@@ -109,24 +185,16 @@
     x, c, y, z = (lax.axis_index(axis) for axis in AXES)
     is_keys = c == 0
     position = (((x * NC + c) * NY + y) * NZ + z) * tok_count
-    limit_len = lax.dynamic_index_in_dim(block_lengths, position // CH, keepdims=False)
-    rows = lax.broadcasted_iota(jnp.int32, (tok_count, 1), 0)
-    is_real = rows + lax.rem(position, CH) < limit_len
     clip_norm = math.sqrt(2.0 * model_width * head_width)
 
-    zero = jnp.zeros((), key_grads.dtype)
-    mine = jnp.where(is_real, jnp.where(is_keys, key_grads, value_grads), zero)
-    theirs = jnp.where(is_real, jnp.where(is_keys, value_grads, key_grads), zero)
-    received = swap_cores(theirs)
-
-    grads = jnp.stack((mine, received))
-    before = first_ring(grads, 1)
-    after = first_ring(grads, -1)
-    opposite = (first_ring(before[:1], 1), first_ring(after[1:], -1))
-
-    owner_rows = model_width // (NX * NY * NZ)
-    across = activations.T.reshape(NY, NZ, NX, owner_rows, tok_count)
-    across = across.transpose(0, 2, 1, 3, 4).reshape(NY * NX, NZ * owner_rows, tok_count)
+    place = jnp.stack((c, lax.div(position, CH), lax.rem(position, CH))).astype(jnp.int32)
+    masked = mask(place, block_lengths, key_grads, value_grads)
+    grads, rings = [], []
+    for mine, theirs in zip(masked[0::2], masked[1::2]):
+        grads.append(jnp.concatenate((mine, swap_cores(theirs)), axis=0))
+        rings.append((first_ring(grads[-1], 1), first_ring(grads[-1], -1)))
+
+    across = transpose(activations, grads[-1])
     acts = lax.all_to_all(across, ("y", "x"), split_axis=0, concat_axis=0, tiled=True)
     other = swap_cores(acts)
 
@@ -137,26 +205,20 @@
             at1, at2 = lax.rem(first + offset1 + 4, 4), lax.rem(second + offset2 + 4, 4)
             index.append(jnp.where(is_keys, at2 * NX + at1, at1 * NX + at2))
     index = jnp.stack(index).astype(jnp.int32)
+    own, minus, plus, across_ring = (tuple(range(4 * i, 4 * i + 4)) for i in range(4))
 
     owned = []
-    low = 0
-    for columns in SPLITS:
-        cut = slice(low, low + columns)
-        low += columns
-        lump = jnp.stack(
-            (
-                grads[:, :, cut],
-                before[:, :, cut],
-                after[:, :, cut],
-                jnp.concatenate((opposite[0][:, :, cut], opposite[1][:, :, cut])),
-            )
-        ).reshape(4, 2 * tok_count, columns)
+    for part, (grad, (before, after)) in enumerate(zip(grads, rings)):
+        step = 1 if part % 2 == 0 else -1
+        opposite = first_ring(before if step == 1 else after, step)
+        lump = jnp.concatenate((grad, before, after, opposite), axis=0)
         lump_before = second_ring(lump, 1)
         lump_after = second_ring(lump, -1)
-        opposite_a = second_ring(lump_before[:2], 1)
-        opposite_b = second_ring(lump_after[2:], -1)
-        weight = multiply(index, acts, other, [lump, lump_before, lump_after], range(12))
-        weight = multiply(index, acts, other, [opposite_a, opposite_b], range(12, 16), weight)
+        lump_opposite = second_ring(lump_before if step == 1 else lump_after, step)
+        weight = multiply(
+            index, acts, other, [lump, lump_before, lump_after], [own, minus, plus]
+        )
+        weight = multiply(index, acts, other, [lump_opposite], [across_ring], weight)
         owned.append(reduce_z(weight, z))
 
     total = sum_all(sum(jnp.sum(part * part) for part in owned))

time: 174 us -> 175 us (level)
  waiting for transfers between devices: 61.9 us -> 67.4 us
  local copies, waits for them, and re-layouts: 19 us -> 13.9 us
  Pallas kernels: 12 us -> 15.6 us
    slice x10 -> x0, local copies, waits for them, and re-layouts: 8.48 us -> none  [the longest x2 1.81 us: body(): opposite_a = second_ring(lump_before[:2], 1)]
    pallas_call x4 -> x6, Pallas kernels: 12 us -> 15.6 us  [the longest x4 13.2 us: multiply(): pl.pallas_call(kernel, out_shape=jax.ShapeDtypeStruct((width, n), jnp.flo...]
    concatenate x0 -> x3, local copies, waits for them, and re-layouts: none -> 3.32 us  [the longest x2 2.65 us: body(): lump = jnp.concatenate((grad, before, after, opposite), axis=0)]
    all_to_all x1, waiting for transfers between devices: 0.01 us -> 2.79 us  [body(): lax.all_to_all(across, ('y', 'x'), split_axis=0, concat_axis=0, tiled=True)]
    ppermute x31 -> x32, waiting for transfers between devices: 51.1 us -> 53.8 us  [send(): return lax.ppermute(value, AXES, pairs(move))]
    all_to_all x1, starting transfers between devices: 7.72 us -> 5.15 us  [body(): lax.all_to_all(across, ('y', 'x'), split_axis=0, concat_axis=0, tiled=True)]
    unnamed x33 -> x14, local copies, waits for them, and re-layouts: 7.51 us -> 9.69 us
    ppermute x31 -> x32, starting transfers between devices: 45.3 us -> 46.1 us  [send(): return lax.ppermute(value, AXES, pairs(move))]
  transfers between devices with their start and end apart: 33 -> 34, of which waited for: 12 -> 15; matrix products, arithmetic and copies ran while one was open for 7% -> 6% of each run, Pallas kernels for 7% -> 8%
where the time goes in v3:
time: 175 us
  starting transfers between devices  71 us (41%)
  waiting for transfers between devices  67.4 us (39%)
  Pallas kernels  15.6 us (9%)
  local copies, waits for them, and re-layouts  13.9 us (8%)
  other arithmetic  3.75 us (2%)
  between operations  2.92 us (2%)
    ppermute x32, waiting for transfers between devices, send(): return lax.ppermute(value, AXES, pairs(move))  53.8 us
    ppermute x32, starting transfers between devices, send(): return lax.ppermute(value, AXES, pairs(move))  46.1 us
    all_to_all x1, starting transfers between devices, sum_all(): lax.all_to_all(rows, AXES, split_axis=0, concat_axis=0, tiled=True)[:, 0, 0]  19.7 us
    pallas_call x4, Pallas kernels, multiply(): pl.pallas_call(kernel, out_shape=jax.ShapeDtypeStruct((width, n), jnp.flo...  13.2 us
    all_to_all x1, waiting for transfers between devices, sum_all(): lax.all_to_all(rows, AXES, split_axis=0, concat_axis=0, tiled=True)[:, 0, 0]  10.8 us
    unnamed x14, local copies, waits for them, and re-layouts  9.69 us
    all_to_all x1, starting transfers between devices, body(): lax.all_to_all(across, ('y', 'x'), split_axis=0, concat_axis=0, tiled=True)  5.15 us
  transfers between devices with their start and end apart: 34, of which 15 were waited for; matrix products, arithmetic and copies ran while one was open for 6% of the time, Pallas kernels for 8%

profile of v3, /device:TPU:1, one launch (start us, length us, event | category | flops | bytes accessed | tf_op | source)
XLA Modules:
  0.0 174.6 jit_solution(4436237390453384759)
XLA Ops:
  3.2 3.2 %collective-permute-start = (bf16[128,512]{1,0:T(8,128)(2,1)}, bf16[128,512]{1,0:T(8,128)(2,1)S(1)}, u32[]{:S(2)}, u32[]{:S(2)}) collective-permute-start(bf16[128,512]{1,0:T(8,128)(2,1)} %get-tuple-element.7), channel_id=1, source_target_pairs={{0,32},{1,33},{2,34},{3,35},{4,36},{5,37},{6,38},{7,39},{8,40},{9,... | collective-permute-start | bytes 393224 | tf_op jit(solution)/shard_map/ppermute | solution.py:31
  12.4 5.2 %all-to-all-start = ((bf16[16,512,128]{2,1,0:T(8,128)(2,1)}), bf16[16,512,128]{2,1,0:T(8,128)(2,1)S(1)}, u32[]{:S(2)}, u32[]{:S(2)}) async-start(bf16[16,512,128]{2,1,0:T(8,128)(2,1)} %copy-done), calls=%async_computation | async-start | bytes 4194304 | tf_op jit(solution)/shard_map/all_to_all | solution.py:198
  23.9 20.2 %collective-permute-done.3 = bf16[256,512]{1,0:T(8,128)(2,1)} collective-permute-done((bf16[256,512]{1,0:T(8,128)(2,1)}, bf16[256,512]{1,0:T(8,128)(2,1)}, u32[]{:S(2)}, u32[]{:S(2)}) %collective-permute-start.3) | collective-permute-done | bytes 262176 | tf_op jit(solution)/shard_map/ppermute | solution.py:31
  45.8 2.1 %collective-permute-start.19 = (bf16[256,512]{1,0:T(8,128)(2,1)}, bf16[256,512]{1,0:T(8,128)(2,1)}, u32[]{:S(2)}, u32[]{:S(2)}) collective-permute-start(bf16[256,512]{1,0:T(8,128)(2,1)} %collective-permute-done.18), channel_id=1, source_target_pairs={{0,192},{1,193},{2,194},{3,195},{4,196},{5,197},{6,198},{7,199},{8... | collective-permute-start | bytes 786440 | tf_op jit(solution)/shard_map/ppermute | solution.py:31
  48.2 2.8 %all-to-all-done.refs_1_ = bf16[16,512,128]{2,1,0:T(8,128)(2,1)S(1)} async-done(((bf16[16,512,128]{2,1,0:T(8,128)(2,1)}), bf16[16,512,128]{2,1,0:T(8,128)(2,1)S(1)}, u32[]{:S(2)}, u32[]{:S(2)}) %all-to-all-start) | async-done | bytes 2097184 | tf_op jit(solution)/shard_map/all_to_all | solution.py:198
  51.0 5.1 %collective-permute-start.1 = (bf16[16,512,128]{2,1,0:T(8,128)(2,1)S(1)}, bf16[16,512,128]{2,1,0:T(8,128)(2,1)}, u32[]{:S(2)}, u32[]{:S(2)}) collective-permute-start(bf16[16,512,128]{2,1,0:T(8,128)(2,1)S(1)} %all-to-all-done.refs_1_), channel_id=1, source_target_pairs={{0,32},{1,33},{2,34},{3,35},{4,36},{5,37},{6,38},{7,39},{8,40},{9,... | collective-permute-start | bytes 6291464 | tf_op jit(solution)/shard_map/ppermute | solution.py:31
  65.1 7.5 %collective-permute-done.6.refs_4_ = bf16[1024,512]{1,0:T(8,128)(2,1)} collective-permute-done((bf16[1024,512]{1,0:T(8,128)(2,1)S(1)}, bf16[1024,512]{1,0:T(8,128)(2,1)}, u32[]{:S(2)}, u32[]{:S(2)}) %collective-permute-start.6) | collective-permute-done | bytes 1048608 | tf_op jit(solution)/shard_map/ppermute | solution.py:31
  73.7 3.6 %collective-permute-done.21.refs_5_ = bf16[1024,512]{1,0:T(8,128)(2,1)} collective-permute-done((bf16[1024,512]{1,0:T(8,128)(2,1)}, bf16[1024,512]{1,0:T(8,128)(2,1)}, u32[]{:S(2)}, u32[]{:S(2)}) %collective-permute-start.21) | collective-permute-done | bytes 1048608 | tf_op jit(solution)/shard_map/ppermute | solution.py:31
  77.3 2.8 %collective-permute-start.22 = (bf16[1024,512]{1,0:T(8,128)(2,1)}, bf16[1024,512]{1,0:T(8,128)(2,1)}, u32[]{:S(2)}, u32[]{:S(2)}) collective-permute-start(bf16[1024,512]{1,0:T(8,128)(2,1)} %collective-permute-done.21.refs_5_), channel_id=1, source_target_pairs={{0,24},{1,25},{2,26},{3,27},{4,28},{5,29},{6,30},{7,31},{8,0},{9,1... | collective-permute-start | bytes 3145736 | tf_op jit(solution)/shard_map/ppermute | solution.py:31
  80.2 8.3 %collective-permute-done.7.refs_5_ = bf16[1024,512]{1,0:T(8,128)(2,1)} collective-permute-done((bf16[1024,512]{1,0:T(8,128)(2,1)S(1)}, bf16[1024,512]{1,0:T(8,128)(2,1)}, u32[]{:S(2)}, u32[]{:S(2)}) %collective-permute-start.7) | collective-permute-done | bytes 1048608 | tf_op jit(solution)/shard_map/ppermute | solution.py:31
  88.5 4.0 %shard_map.61.refs_3_ = f32[512,512]{1,0:T(8,128)S(1)} custom-call(s32[16]{0:T(128)S(1)} %stack.79.refs_0_, bf16[16,512,128]{2,1,0:T(8,128)(2,1)S(1)} %all-to-all-done.refs_1_, bf16[16,512,128]{2,1,0:T(8,128)(2,1)} %collective-permute-done.1.refs_2_, bf16[1024,512]{1,0:T(8,128)(2,1)S(1)} %constant_dynamic-update-slice_fusion.4.refs_3_, ...), custom_call_target="tpu_custom_call" | custom-call | flops 1610612736 | bytes 6291456 | tf_op jit(solution)/shard_map/pallas_call | solution.py:144
  92.5 2.7 %shard_map.62 = f32[512,512]{1,0:T(8,128)S(1)} custom-call(s32[16]{0:T(128)S(1)} %stack.79.refs_0_, bf16[16,512,128]{2,1,0:T(8,128)(2,1)S(1)} %all-to-all-done.refs_1_, bf16[16,512,128]{2,1,0:T(8,128)(2,1)} %collective-permute-done.1.refs_2_, f32[512,512]{1,0:T(8,128)S(1)} %shard_map.61.refs_3_, bf16[1024,512]{1,0:T(8,128)(2,1)} %collective-permute-done.8.refs_4_), custom_call_target="tpu_custom_call" | custom-call | flops 536870912 | bytes 2097152 | tf_op jit(solution)/shard_map/pallas_call | solution.py:144
  95.2 5.7 %collective-permute-start.13 = (f32[32,512]{1,0:T(8,128)S(1)}, f32[32,512]{1,0:T(8,128)S(1)}, u32[]{:S(2)}, u32[]{:S(2)}) collective-permute-start(f32[32,512]{1,0:T(8,128)S(1)} %get-tuple-element.21), channel_id=1, source_target_pairs={{0,7},{1,0},{2,1},{3,2},{4,3},{5,4},{6,5},{7,6},{8,15},{9,8},{10,9... | collective-permute-start | bytes 196616 | tf_op jit(solution)/shard_map/ppermute | solution.py:31
  100.9 4.0 %shard_map.63.refs_3_ = f32[512,512]{1,0:T(8,128)S(1)} custom-call(s32[16]{0:T(128)S(1)} %stack.79.refs_0_, bf16[16,512,128]{2,1,0:T(8,128)(2,1)S(1)} %all-to-all-done.refs_1_, bf16[16,512,128]{2,1,0:T(8,128)(2,1)} %collective-permute-done.1.refs_2_, bf16[1024,512]{1,0:T(8,128)(2,1)S(1)} %copy-done.2, bf16[1024,512]{1,0:T(8,128)(2,1)} %collective-permute-done.20.refs_4_, ...), custom_call_target="tpu_custom_call" | custom-call | flops 1610612736 | bytes 6291456 | tf_op jit(solution)/shard_map/pallas_call | solution.py:144
  104.8 2.6 %shard_map.64 = f32[512,512]{1,0:T(8,128)S(1)} custom-call(s32[16]{0:T(128)S(1)} %stack.79.refs_0_, bf16[16,512,128]{2,1,0:T(8,128)(2,1)S(1)} %all-to-all-done.refs_1_, bf16[16,512,128]{2,1,0:T(8,128)(2,1)} %collective-permute-done.1.refs_2_, f32[512,512]{1,0:T(8,128)S(1)} %shard_map.63.refs_3_, bf16[1024,512]{1,0:T(8,128)(2,1)} %collective-permute-done.22.refs_4_), custom_call_target="tpu_custom_call" | custom-call | flops 536870912 | bytes 2097152 | tf_op jit(solution)/shard_map/pallas_call | solution.py:144
  107.6 4.0 %collective-permute-start.27 = (f32[32,512]{1,0:T(8,128)S(1)}, f32[32,512]{1,0:T(8,128)S(1)}, u32[]{:S(2)}, u32[]{:S(2)}) collective-permute-start(f32[32,512]{1,0:T(8,128)S(1)} %get-tuple-element.29), channel_id=1, source_target_pairs={{0,7},{1,0},{2,1},{3,2},{4,3},{5,4},{6,5},{7,6},{8,15},{9,8},{10,9... | collective-permute-start | bytes 196616 | tf_op jit(solution)/shard_map/ppermute | solution.py:31
  113.4 2.7 %collective-permute-start.28 = (f32[64,512]{1,0:T(8,128)S(1)}, f32[64,512]{1,0:T(8,128)S(1)}, u32[]{:S(2)}, u32[]{:S(2)}) collective-permute-start(f32[64,512]{1,0:T(8,128)S(1)} %pad_maximum_fusion.4), channel_id=1, source_target_pairs={{0,7},{1,0},{2,1},{3,2},{4,3},{5,4},{6,5},{7,6},{8,15},{9,8},{10,9... | collective-permute-start | bytes 393224 | tf_op jit(solution)/shard_map/ppermute | solution.py:31
  116.2 2.8 %collective-permute-done.10 = f32[64,512]{1,0:T(8,128)S(1)} collective-permute-done((f32[64,512]{1,0:T(8,128)S(1)}, f32[64,512]{1,0:T(8,128)S(1)}, u32[]{:S(2)}, u32[]{:S(2)}) %collective-permute-start.10) | collective-permute-done | bytes 131104 | tf_op jit(solution)/shard_map/ppermute | solution.py:31
  119.1 2.1 %collective-permute-done.24 = f32[64,512]{1,0:T(8,128)S(1)} collective-permute-done((f32[64,512]{1,0:T(8,128)S(1)}, f32[64,512]{1,0:T(8,128)S(1)}, u32[]{:S(2)}, u32[]{:S(2)}) %collective-permute-start.24) | collective-permute-done | bytes 131104 | tf_op jit(solution)/shard_map/ppermute | solution.py:31
  121.3 4.1 %collective-permute-done.11 = f32[64,512]{1,0:T(8,128)S(1)} collective-permute-done((f32[64,512]{1,0:T(8,128)S(1)}, f32[64,512]{1,0:T(8,128)S(1)}, u32[]{:S(2)}, u32[]{:S(2)}) %collective-permute-start.11) | collective-permute-done | bytes 131104 | tf_op jit(solution)/shard_map/ppermute | solution.py:31
  131.5 2.3 %collective-permute-start.30 = (f32[64,512]{1,0:T(8,128)S(1)}, f32[64,512]{1,0:T(8,128)S(1)}, u32[]{:S(2)}, u32[]{:S(2)}) collective-permute-start(f32[64,512]{1,0:T(8,128)S(1)} %dynamic-slice_add_fusion.1), channel_id=1, source_target_pairs={{0,7},{1,0},{2,1},{3,2},{4,3},{5,4},{6,5},{7,6},{8,15},{9,8},{10,9... | collective-permute-start | bytes 393224 | tf_op jit(solution)/shard_map/ppermute | solution.py:31
  139.5 19.7 %all-to-all-start.1 = ((f32[256,1,128]{2,1,0:T(1,128)}), f32[256,1,128]{2,1,0:T(1,128)S(1)}, u32[]{:S(2)}, u32[]{:S(2)}) async-start(f32[256,1,128]{2,1,0:T(1,128)} %broadcast_in_dim.3), calls=%async_computation.1 | async-start | bytes 262144 | tf_op jit(solution)/shard_map/all_to_all | solution.py:179
  159.3 2.2 %collective-permute-start.31 = (f32[32,1024]{1,0:T(8,128)S(1)}, f32[32,1024]{1,0:T(8,128)S(1)}, u32[]{:S(2)}, u32[]{:S(2)}) collective-permute-start(f32[32,1024]{1,0:T(8,128)S(1)} %broadcast_select_fusion), channel_id=1, source_target_pairs={{0,32},{1,33},{2,34},{3,35},{4,36},{5,37},{6,38},{7,39},{8,40},{9,... | collective-permute-start | bytes 393224 | tf_op jit(solution)/shard_map/ppermute | solution.py:31
  161.5 10.8 %all-to-all-done.1 = f32[256,1,128]{2,1,0:T(1,128)S(1)} async-done(((f32[256,1,128]{2,1,0:T(1,128)}), f32[256,1,128]{2,1,0:T(1,128)S(1)}, u32[]{:S(2)}, u32[]{:S(2)}) %all-to-all-start.1) | async-done | bytes 131104 | tf_op jit(solution)/shard_map/all_to_all | solution.py:179
  (89 shorter events, 41.1 us)
Async XLA Ops:
  12.4 38.6 %all-to-all-start = ((bf16[16,512,128]{2,1,0:T(8,128)(2,1)}), bf16[16,512,128]{2,1,0:T(8,128)(2,1)S(1)}, u32[]{:S(2)}, u32[]{:S(2)}) async-start(bf16[16,512,128]{2,1,0:T(8,128)(2,1)} %copy-done), calls=%async_computation | async-start | bytes 4194304 | tf_op jit(solution)/shard_map/all_to_all | solution.py:198
  19.6 24.5 %collective-permute-start.3 = (bf16[256,512]{1,0:T(8,128)(2,1)}, bf16[256,512]{1,0:T(8,128)(2,1)}, u32[]{:S(2)}, u32[]{:S(2)}) collective-permute-start(bf16[256,512]{1,0:T(8,128)(2,1)} %get-tuple-element.32), channel_id=1, source_target_pairs={{0,64},{1,65},{2,66},{3,67},{4,68},{5,69},{6,70},{7,71},{8,72},{9,... | collective-permute-start | bytes 786440 | tf_op jit(solution)/shard_map/ppermute | solution.py:31
  21.2 24.6 %collective-permute-start.18 = (bf16[256,512]{1,0:T(8,128)(2,1)S(1)}, bf16[256,512]{1,0:T(8,128)(2,1)}, u32[]{:S(2)}, u32[]{:S(2)}) collective-permute-start(bf16[256,512]{1,0:T(8,128)(2,1)S(1)} %get-tuple-element.37.after_ref), channel_id=1, source_target_pairs={{0,192},{1,193},{2,194},{3,195},{4,196},{5,197},{6,198},{7,199},{8... | collective-permute-start | bytes 786440 | tf_op jit(solution)/shard_map/ppermute | solution.py:31
  22.4 25.8 %collective-permute-start.4 = (bf16[256,512]{1,0:T(8,128)(2,1)}, bf16[256,512]{1,0:T(8,128)(2,1)S(1)}, u32[]{:S(2)}, u32[]{:S(2)}) collective-permute-start(bf16[256,512]{1,0:T(8,128)(2,1)} %get-tuple-element.32), channel_id=1, source_target_pairs={{0,192},{1,193},{2,194},{3,195},{4,196},{5,197},{6,198},{7,199},{8... | collective-permute-start | bytes 786440 | tf_op jit(solution)/shard_map/ppermute | solution.py:31
  44.1 12.0 %collective-permute-start.5 = (bf16[256,512]{1,0:T(8,128)(2,1)}, bf16[256,512]{1,0:T(8,128)(2,1)}, u32[]{:S(2)}, u32[]{:S(2)}) collective-permute-start(bf16[256,512]{1,0:T(8,128)(2,1)} %collective-permute-done.3), channel_id=1, source_target_pairs={{0,64},{1,65},{2,66},{3,67},{4,68},{5,69},{6,70},{7,71},{8,72},{9,... | collective-permute-start | bytes 786440 | tf_op jit(solution)/shard_map/ppermute | solution.py:31
  44.1 13.8 %collective-permute-start.17 = (bf16[256,512]{1,0:T(8,128)(2,1)S(1)}, bf16[256,512]{1,0:T(8,128)(2,1)}, u32[]{:S(2)}, u32[]{:S(2)}) collective-permute-start(bf16[256,512]{1,0:T(8,128)(2,1)S(1)} %get-tuple-element.37.after_ref), channel_id=1, source_target_pairs={{0,64},{1,65},{2,66},{3,67},{4,68},{5,69},{6,70},{7,71},{8,72},{9,... | collective-permute-start | bytes 786440 | tf_op jit(solution)/shard_map/ppermute | solution.py:31
  45.8 15.5 %collective-permute-start.19 = (bf16[256,512]{1,0:T(8,128)(2,1)}, bf16[256,512]{1,0:T(8,128)(2,1)}, u32[]{:S(2)}, u32[]{:S(2)}) collective-permute-start(bf16[256,512]{1,0:T(8,128)(2,1)} %collective-permute-done.18), channel_id=1, source_target_pairs={{0,192},{1,193},{2,194},{3,195},{4,196},{5,197},{6,198},{7,199},{8... | collective-permute-start | bytes 786440 | tf_op jit(solution)/shard_map/ppermute | solution.py:31
  51.0 37.5 %collective-permute-start.1 = (bf16[16,512,128]{2,1,0:T(8,128)(2,1)S(1)}, bf16[16,512,128]{2,1,0:T(8,128)(2,1)}, u32[]{:S(2)}, u32[]{:S(2)}) collective-permute-start(bf16[16,512,128]{2,1,0:T(8,128)(2,1)S(1)} %all-to-all-done.refs_1_), channel_id=1, source_target_pairs={{0,32},{1,33},{2,34},{3,35},{4,36},{5,37},{6,38},{7,39},{8,40},{9,... | collective-permute-start | bytes 6291464 | tf_op jit(solution)/shard_map/ppermute | solution.py:31
  57.1 15.5 %collective-permute-start.6 = (bf16[1024,512]{1,0:T(8,128)(2,1)S(1)}, bf16[1024,512]{1,0:T(8,128)(2,1)}, u32[]{:S(2)}, u32[]{:S(2)}) collective-permute-start(bf16[1024,512]{1,0:T(8,128)(2,1)S(1)} %constant_dynamic-update-slice_fusion.4.refs_3_), channel_id=1, source_target_pairs={{0,8},{1,9},{2,10},{3,11},{4,12},{5,13},{6,14},{7,15},{8,16},{9,17... | collective-permute-start | bytes 3145736 | tf_op jit(solution)/shard_map/ppermute | solution.py:31
  62.9 14.3 %collective-permute-start.21 = (bf16[1024,512]{1,0:T(8,128)(2,1)}, bf16[1024,512]{1,0:T(8,128)(2,1)}, u32[]{:S(2)}, u32[]{:S(2)}) collective-permute-start(bf16[1024,512]{1,0:T(8,128)(2,1)} %constant_dynamic-update-slice_fusion.9.refs_3_), channel_id=1, source_target_pairs={{0,24},{1,25},{2,26},{3,27},{4,28},{5,29},{6,30},{7,31},{8,0},{9,1... | collective-permute-start | bytes 3145736 | tf_op jit(solution)/shard_map/ppermute | solution.py:31
  64.9 23.6 %collective-permute-start.7 = (bf16[1024,512]{1,0:T(8,128)(2,1)S(1)}, bf16[1024,512]{1,0:T(8,128)(2,1)}, u32[]{:S(2)}, u32[]{:S(2)}) collective-permute-start(bf16[1024,512]{1,0:T(8,128)(2,1)S(1)} %constant_dynamic-update-slice_fusion.4.refs_3_), channel_id=1, source_target_pairs={{0,24},{1,25},{2,26},{3,27},{4,28},{5,29},{6,30},{7,31},{8,0},{9,1... | collective-permute-start | bytes 3145736 | tf_op jit(solution)/shard_map/ppermute | solution.py:31
  72.6 19.9 %collective-permute-start.8 = (bf16[1024,512]{1,0:T(8,128)(2,1)}, bf16[1024,512]{1,0:T(8,128)(2,1)}, u32[]{:S(2)}, u32[]{:S(2)}) collective-permute-start(bf16[1024,512]{1,0:T(8,128)(2,1)} %collective-permute-done.6.refs_4_), channel_id=1, source_target_pairs={{0,8},{1,9},{2,10},{3,11},{4,12},{5,13},{6,14},{7,15},{8,16},{9,17... | collective-permute-start | bytes 3145736 | tf_op jit(solution)/shard_map/ppermute | solution.py:31
  72.6 28.3 %collective-permute-start.20 = (bf16[1024,512]{1,0:T(8,128)(2,1)}, bf16[1024,512]{1,0:T(8,128)(2,1)}, u32[]{:S(2)}, u32[]{:S(2)}) collective-permute-start(bf16[1024,512]{1,0:T(8,128)(2,1)} %constant_dynamic-update-slice_fusion.9.refs_3_), channel_id=1, source_target_pairs={{0,8},{1,9},{2,10},{3,11},{4,12},{5,13},{6,14},{7,15},{8,16},{9,17... | collective-permute-start | bytes 3145736 | tf_op jit(solution)/shard_map/ppermute | solution.py:31
  77.3 27.6 %collective-permute-start.22 = (bf16[1024,512]{1,0:T(8,128)(2,1)}, bf16[1024,512]{1,0:T(8,128)(2,1)}, u32[]{:S(2)}, u32[]{:S(2)}) collective-permute-start(bf16[1024,512]{1,0:T(8,128)(2,1)} %collective-permute-done.21.refs_5_), channel_id=1, source_target_pairs={{0,24},{1,25},{2,26},{3,27},{4,28},{5,29},{6,30},{7,31},{8,0},{9,1... | collective-permute-start | bytes 3145736 | tf_op jit(solution)/shard_map/ppermute | solution.py:31
  95.2 16.5 %collective-permute-start.13 = (f32[32,512]{1,0:T(8,128)S(1)}, f32[32,512]{1,0:T(8,128)S(1)}, u32[]{:S(2)}, u32[]{:S(2)}) collective-permute-start(f32[32,512]{1,0:T(8,128)S(1)} %get-tuple-element.21), channel_id=1, source_target_pairs={{0,7},{1,0},{2,1},{3,2},{4,3},{5,4},{6,5},{7,6},{8,15},{9,8},{10,9... | collective-permute-start | bytes 196616 | tf_op jit(solution)/shard_map/ppermute | solution.py:31
  100.8 10.8 %collective-permute-start.9 = (f32[32,512]{1,0:T(8,128)S(1)}, f32[32,512]{1,0:T(8,128)S(1)}, u32[]{:S(2)}, u32[]{:S(2)}) collective-permute-start(f32[32,512]{1,0:T(8,128)S(1)} %get-tuple-element.20), channel_id=1, source_target_pairs={{0,1},{1,2},{2,3},{3,4},{4,5},{5,6},{6,7},{7,0},{8,9},{9,10},{10,1... | collective-permute-start | bytes 196616 | tf_op jit(solution)/shard_map/ppermute | solution.py:31
  111.7 9.6 %collective-permute-start.14 = (f32[64,512]{1,0:T(8,128)S(1)}, f32[64,512]{1,0:T(8,128)S(1)}, u32[]{:S(2)}, u32[]{:S(2)}) collective-permute-start(f32[64,512]{1,0:T(8,128)S(1)} %pad_maximum_fusion.2), channel_id=1, source_target_pairs={{0,7},{1,0},{2,1},{3,2},{4,3},{5,4},{6,5},{7,6},{8,15},{9,8},{10,9... | collective-permute-start | bytes 393224 | tf_op jit(solution)/shard_map/ppermute | solution.py:31
  113.4 13.9 %collective-permute-start.28 = (f32[64,512]{1,0:T(8,128)S(1)}, f32[64,512]{1,0:T(8,128)S(1)}, u32[]{:S(2)}, u32[]{:S(2)}) collective-permute-start(f32[64,512]{1,0:T(8,128)S(1)} %pad_maximum_fusion.4), channel_id=1, source_target_pairs={{0,7},{1,0},{2,1},{3,2},{4,3},{5,4},{6,5},{7,6},{8,15},{9,8},{10,9... | collective-permute-start | bytes 393224 | tf_op jit(solution)/shard_map/ppermute | solution.py:31
  119.0 6.5 %collective-permute-start.11 = (f32[64,512]{1,0:T(8,128)S(1)}, f32[64,512]{1,0:T(8,128)S(1)}, u32[]{:S(2)}, u32[]{:S(2)}) collective-permute-start(f32[64,512]{1,0:T(8,128)S(1)} %dynamic-slice_add_fusion.6), channel_id=1, source_target_pairs={{0,1},{1,2},{2,3},{3,4},{4,5},{5,6},{6,7},{7,0},{8,9},{9,10},{10,1... | collective-permute-start | bytes 393224 | tf_op jit(solution)/shard_map/ppermute | solution.py:31
  121.2 6.1 %collective-permute-start.25 = (f32[64,512]{1,0:T(8,128)S(1)}, f32[64,512]{1,0:T(8,128)S(1)}, u32[]{:S(2)}, u32[]{:S(2)}) collective-permute-start(f32[64,512]{1,0:T(8,128)S(1)} %dynamic-slice_add_fusion.2), channel_id=1, source_target_pairs={{0,1},{1,2},{2,3},{3,4},{4,5},{5,6},{6,7},{7,0},{8,9},{9,10},{10,1... | collective-permute-start | bytes 393224 | tf_op jit(solution)/shard_map/ppermute | solution.py:31
  125.8 8.0 %collective-permute-start.12 = (f32[64,512]{1,0:T(8,128)S(1)}, f32[64,512]{1,0:T(8,128)S(1)}, u32[]{:S(2)}, u32[]{:S(2)}) collective-permute-start(f32[64,512]{1,0:T(8,128)S(1)} %get-tuple-element.14), channel_id=1, source_target_pairs={{0,1},{1,2},{2,3},{3,4},{4,5},{5,6},{6,7},{7,0},{8,9},{9,10},{10,1... | collective-permute-start | bytes 393224 | tf_op jit(solution)/shard_map/ppermute | solution.py:31
  128.7 6.1 %collective-permute-start.26 = (f32[64,512]{1,0:T(8,128)S(1)}, f32[64,512]{1,0:T(8,128)S(1)}, u32[]{:S(2)}, u32[]{:S(2)}) collective-permute-start(f32[64,512]{1,0:T(8,128)S(1)} %get-tuple-element.22), channel_id=1, source_target_pairs={{0,1},{1,2},{2,3},{3,4},{4,5},{5,6},{6,7},{7,0},{8,9},{9,10},{10,1... | collective-permute-start | bytes 393224 | tf_op jit(solution)/shard_map/ppermute | solution.py:31
  139.5 32.8 %all-to-all-start.1 = ((f32[256,1,128]{2,1,0:T(1,128)}), f32[256,1,128]{2,1,0:T(1,128)S(1)}, u32[]{:S(2)}, u32[]{:S(2)}) async-start(f32[256,1,128]{2,1,0:T(1,128)} %broadcast_in_dim.3), calls=%async_computation.1 | async-start | bytes 262144 | tf_op jit(solution)/shard_map/all_to_all | solution.py:179
  159.3 14.6 %collective-permute-start.31 = (f32[32,1024]{1,0:T(8,128)S(1)}, f32[32,1024]{1,0:T(8,128)S(1)}, u32[]{:S(2)}, u32[]{:S(2)}) collective-permute-start(f32[32,1024]{1,0:T(8,128)S(1)} %broadcast_select_fusion), channel_id=1, source_target_pairs={{0,32},{1,33},{2,34},{3,35},{4,36},{5,37},{6,38},{7,39},{8,40},{9,... | collective-permute-start | bytes 393224 | tf_op jit(solution)/shard_map/ppermute | solution.py:31
  (14 other events, 63.2 us)

commit v4 on v3

--- a/solution.py
+++ b/solution.py
@@ -43,43 +43,55 @@
     return send(value, lambda x, c, y, z: (x, c, y + step, z) if c == 0 else (x + step, c, y, z))
 
 
-def z_ring(value, step):
-    return send(value, lambda x, c, y, z: (x, c, y, z + step))
-
-
-def mask_kernel(splits, place_ref, lengths_ref, keys_ref, values_ref, *out_refs):
+def mask_kernel(place_ref, lengths_ref, keys_ref, values_ref, mine_ref, theirs_ref):
     is_keys = place_ref[0] == 0
     limit = lengths_ref[place_ref[1]] - place_ref[2]
+    keys, values = keys_ref[...], values_ref[...]
+    rows = lax.broadcasted_iota(jnp.int32, keys.shape, 0)
+    zero = jnp.zeros_like(keys)
+    keys = jnp.where(rows < limit, keys, zero)
+    values = jnp.where(rows < limit, values, zero)
+    mine_ref[...] = jnp.where(is_keys, keys, values)
+    theirs_ref[...] = jnp.where(is_keys, values, keys)
+
+
+def mask(place, block_lengths, key_grads, value_grads):
+    smem = pl.BlockSpec(memory_space=pltpu.SMEM)
+    vmem = pl.BlockSpec(memory_space=pltpu.VMEM)
+    return pl.pallas_call(
+        mask_kernel,
+        out_shape=[jax.ShapeDtypeStruct(key_grads.shape, key_grads.dtype)] * 2,
+        in_specs=[smem, smem, vmem, vmem],
+        out_specs=[vmem, vmem],
+        cost_estimate=pl.CostEstimate(
+            flops=key_grads.size, bytes_accessed=8 * key_grads.size, transcendentals=0
+        ),
+    )(place, block_lengths, key_grads, value_grads)
+
+
+def lump_kernel(*refs):
+    outs = refs[-len(SPLITS) :]
+    pieces = refs[: -len(SPLITS)]
+    tok_count = pieces[0].shape[0]
     low = 0
-    for i, columns in enumerate(splits):
-        cut = pl.ds(low, columns)
+    for columns, out_ref in zip(SPLITS, outs):
+        for i, piece_ref in enumerate(pieces):
+            out_ref[pl.ds(i * tok_count, tok_count), :] = piece_ref[:, pl.ds(low, columns)]
         low += columns
-        keys, values = keys_ref[:, cut], values_ref[:, cut]
-        rows = lax.broadcasted_iota(jnp.int32, keys.shape, 0)
-        zero = jnp.zeros_like(keys)
-        keys = jnp.where(rows < limit, keys, zero)
-        values = jnp.where(rows < limit, values, zero)
-        out_refs[2 * i][...] = jnp.where(is_keys, keys, values)
-        out_refs[2 * i + 1][...] = jnp.where(is_keys, values, keys)
-
-
-def mask(place, block_lengths, key_grads, value_grads):
-    tok_count = key_grads.shape[0]
-    smem = pl.BlockSpec(memory_space=pltpu.SMEM)
-    vmem = pl.BlockSpec(memory_space=pltpu.VMEM)
-    return pl.pallas_call(
-        functools.partial(mask_kernel, SPLITS),
-        out_shape=[
-            jax.ShapeDtypeStruct((tok_count, columns), key_grads.dtype)
-            for columns in SPLITS
-            for _ in range(2)
-        ],
-        in_specs=[smem, smem, vmem, vmem],
-        out_specs=[vmem] * (2 * len(SPLITS)),
-        cost_estimate=pl.CostEstimate(
-            flops=key_grads.size, bytes_accessed=8 * key_grads.size, transcendentals=0
-        ),
-    )(place, block_lengths, key_grads, value_grads)
+
+
+def lumps(pieces):
+    rows = len(pieces) * pieces[0].shape[0]
+    vmem = pl.BlockSpec(memory_space=pltpu.VMEM)
+    return pl.pallas_call(
+        lump_kernel,
+        out_shape=[jax.ShapeDtypeStruct((rows, n), pieces[0].dtype) for n in SPLITS],
+        in_specs=[vmem] * len(pieces),
+        out_specs=[vmem] * len(SPLITS),
+        cost_estimate=pl.CostEstimate(
+            flops=0, bytes_accessed=4 * rows * sum(SPLITS), transcendentals=0
+        ),
+    )(*pieces)
 
 
 def transpose_kernel(acts_ref, after_ref, out_ref):
@@ -131,7 +143,7 @@
         out_ref[cut, :] = total
 
 
-def multiply(index, acts, other, parts, offsets, start=None, after=()):
+def multiply(index, acts, other, parts, offsets, start=None):
     width, n = acts.shape[1], parts[0].shape[1]
     operands = [acts, other] + ([] if start is None else [start]) + list(parts)
     depth = sum(part.shape[0] for part in parts)
@@ -145,33 +157,13 @@
         kernel,
         out_shape=jax.ShapeDtypeStruct((width, n), jnp.float32),
         in_specs=[pl.BlockSpec(memory_space=pltpu.SMEM)]
-        + [vmem] * len(operands)
-        + [pl.BlockSpec(memory_space=pl.ANY)] * len(after),
+        + [vmem] * len(operands),
         out_specs=vmem,
         compiler_params=pltpu.CompilerParams(vmem_limit_bytes=40 * 1024 * 1024),
         cost_estimate=pl.CostEstimate(
             flops=2 * width * n * depth, bytes_accessed=2 * depth * (n + width), transcendentals=0
         ),
-    )(index, *operands, *after)
-
-
-def reduce_z(partial, z):
-    rows = partial.shape[0] // NZ
-    half = rows // 2
-
-    def block(offset):
-        return lax.dynamic_slice_in_dim(partial, lax.rem(z + offset + NZ, NZ) * rows, rows, axis=0)
-
-    far = block(4)
-    up = z_ring(far[:half], 1)
-    down = z_ring(far[half:], -1)
-    near_up, near_down = block(3), block(-3)
-    up = z_ring(jnp.concatenate((near_up[:half] + up, near_up[half:]), axis=0), 1)
-    down = z_ring(jnp.concatenate((near_down[:half], near_down[half:] + down), axis=0), -1)
-    for offset in (2, 1):
-        up = z_ring(block(offset) + up, 1)
-        down = z_ring(block(-offset) + down, -1)
-    return block(0) + up + down
+    )(index, *operands)
 
 
 def sum_all(value):
@@ -188,13 +180,26 @@
     clip_norm = math.sqrt(2.0 * model_width * head_width)
 
     place = jnp.stack((c, lax.div(position, CH), lax.rem(position, CH))).astype(jnp.int32)
-    masked = mask(place, block_lengths, key_grads, value_grads)
-    grads, rings = [], []
-    for mine, theirs in zip(masked[0::2], masked[1::2]):
-        grads.append(jnp.concatenate((mine, swap_cores(theirs)), axis=0))
-        rings.append((first_ring(grads[-1], 1), first_ring(grads[-1], -1)))
-
-    across = transpose(activations, grads[-1])
+    mine, theirs = mask(place, block_lengths, key_grads, value_grads)
+    received = swap_cores(theirs)
+    mine_before, mine_after = first_ring(mine, 1), first_ring(mine, -1)
+    received_before, received_after = first_ring(received, 1), first_ring(received, -1)
+    mine_opposite = first_ring(mine_before, 1)
+    received_opposite = first_ring(received_after, -1)
+    parts = lumps(
+        (
+            mine,
+            received,
+            mine_before,
+            received_before,
+            mine_after,
+            received_after,
+            mine_opposite,
+            received_opposite,
+        )
+    )
+
+    across = transpose(activations, mine_before)
     acts = lax.all_to_all(across, ("y", "x"), split_axis=0, concat_axis=0, tiled=True)
     other = swap_cores(acts)
 
@@ -208,10 +213,8 @@
     own, minus, plus, across_ring = (tuple(range(4 * i, 4 * i + 4)) for i in range(4))
 
     owned = []
-    for part, (grad, (before, after)) in enumerate(zip(grads, rings)):
+    for part, lump in enumerate(parts):
         step = 1 if part % 2 == 0 else -1
-        opposite = first_ring(before if step == 1 else after, step)
-        lump = jnp.concatenate((grad, before, after, opposite), axis=0)
         lump_before = second_ring(lump, 1)
         lump_after = second_ring(lump, -1)
         lump_opposite = second_ring(lump_before if step == 1 else lump_after, step)
@@ -219,7 +222,7 @@
             index, acts, other, [lump, lump_before, lump_after], [own, minus, plus]
         )
         weight = multiply(index, acts, other, [lump_opposite], [across_ring], weight)
-        owned.append(reduce_z(weight, z))
+        owned.append(lax.psum_scatter(weight, "z", scatter_dimension=0, tiled=True))
 
     total = sum_all(sum(jnp.sum(part * part) for part in owned))
     owned = jnp.concatenate(owned, axis=1)

time: 175 us -> 217 us (1.24)
  waiting for transfers between devices: 67.4 us -> 126 us
  starting transfers between devices: 71 us -> 43.6 us
  between operations: 2.92 us -> 16.2 us
  local copies, waits for them, and re-layouts: 13.9 us -> 4.97 us
  Pallas kernels: 15.6 us -> 19.6 us
    reduce_scatter x0 -> x2, waiting for transfers between devices: none -> 53.5 us  [body(): owned.append(lax.psum_scatter(weight, 'z', scatter_dimension=0, tiled=True))]
    ppermute x32 -> x15, starting transfers between devices: 46.1 us -> 22.6 us  [send(): return lax.ppermute(value, AXES, pairs(move))]
    ppermute x32 -> x15, waiting for transfers between devices: 53.8 us -> 62.2 us  [send(): return lax.ppermute(value, AXES, pairs(move))]
    unnamed x14 -> x20, local copies, waits for them, and re-layouts: 9.69 us -> 4.17 us
    all_to_all x1, starting transfers between devices: 19.7 us -> 15 us  [sum_all(): lax.all_to_all(rows, AXES, split_axis=0, concat_axis=0, tiled=True)[:, 0, 0]]
    concatenate x3 -> x0, local copies, waits for them, and re-layouts: 3.32 us -> none  [the longest x2 2.65 us: body(): lump = jnp.concatenate((grad, before, after, opposite), axis=0)]
    pallas_call x1 -> x2, Pallas kernels: 1.87 us -> 4.8 us  [the longest x1 2.89 us: lumps(): pl.pallas_call(lump_kernel, out_shape=[jax.ShapeDtypeStruct((rows, n), pi...]
    all_to_all x1, waiting for transfers between devices: 2.79 us -> 0.01 us  [body(): lax.all_to_all(across, ('y', 'x'), split_axis=0, concat_axis=0, tiled=True)]
  transfers between devices with their start and end apart: 34 -> 19, of which waited for: 15 -> 11; matrix products, arithmetic and copies ran while one was open for 6% -> 1% of each run, Pallas kernels for 8% -> 8%
where the time goes in v4:
time: 217 us; the launch traced here: 216 us
  waiting for transfers between devices  126 us (58%)
  starting transfers between devices  43.6 us (20%)
  Pallas kernels  19.6 us (9%)
  between operations  16.2 us (7%)
  other arithmetic  5.32 us (2%)
  local copies, waits for them, and re-layouts  4.97 us (2%)
    ppermute x15, waiting for transfers between devices, send(): return lax.ppermute(value, AXES, pairs(move))  62.2 us
    reduce_scatter x2, waiting for transfers between devices, body(): owned.append(lax.psum_scatter(weight, 'z', scatter_dimension=0, tiled=True))  53.5 us
    ppermute x15, starting transfers between devices, send(): return lax.ppermute(value, AXES, pairs(move))  22.6 us
    all_to_all x1, starting transfers between devices, sum_all(): lax.all_to_all(rows, AXES, split_axis=0, concat_axis=0, tiled=True)[:, 0, 0]  15 us
    pallas_call x4, Pallas kernels, multiply(): pl.pallas_call(kernel, out_shape=jax.ShapeDtypeStruct((width, n), jnp.flo...  14.2 us
    all_to_all x1, waiting for transfers between devices, sum_all(): lax.all_to_all(rows, AXES, split_axis=0, concat_axis=0, tiled=True)[:, 0, 0]  10.8 us
    all_to_all x1, starting transfers between devices, body(): lax.all_to_all(across, ('y', 'x'), split_axis=0, concat_axis=0, tiled=True)  5.91 us
  transfers between devices with their start and end apart: 19, of which 11 were waited for; matrix products, arithmetic and copies ran while one was open for 1% of the time, Pallas kernels for 8%

profile of v4, /device:TPU:1, one launch (start us, length us, event | category | flops | bytes accessed | tf_op | source)
XLA Modules:
  0.0 216.1 jit_solution(1449874207643231394)
XLA Ops:
  7.8 1.9 shard_map.59
  9.8 2.1 collective-permute-start
  11.9 5.4 %collective-permute-done.after_ref.refs_2_ = bf16[128,1024]{1,0:T(8,128)(2,1)S(1)} collective-permute-done((bf16[128,1024]{1,0:T(8,128)(2,1)}, bf16[128,1024]{1,0:T(8,128)(2,1)S(1)}, u32[]{:S(2)}, u32[]{:S(2)}) %collective-permute-start) | collective-permute-done | bytes 262176 | tf_op jit(solution)/shard_map/ppermute | solution.py:31
  17.3 1.6 copy-done.1
  20.8 5.9 %all-to-all-start = ((bf16[16,512,128]{2,1,0:T(8,128)(2,1)}), bf16[16,512,128]{2,1,0:T(8,128)(2,1)S(1)}, u32[]{:S(2)}, u32[]{:S(2)}) async-start(bf16[16,512,128]{2,1,0:T(8,128)(2,1)} %copy-done), calls=%async_computation | async-start | bytes 4194304 | tf_op jit(solution)/shard_map/all_to_all | solution.py:203
  26.8 1.9 collective-permute-start.2
  29.9 2.9 %collective-permute-start.5 = (bf16[128,1024]{1,0:T(8,128)(2,1)S(1)}, bf16[128,1024]{1,0:T(8,128)(2,1)S(1)}, u32[]{:S(2)}, u32[]{:S(2)}) collective-permute-start(bf16[128,1024]{1,0:T(8,128)(2,1)S(1)} %collective-permute-done.2.refs_1_), channel_id=1, source_target_pairs={{0,192},{1,193},{2,194},{3,195},{4,196},{5,197},{6,198},{7,199},{8... | collective-permute-start | bytes 786440 | tf_op jit(solution)/shard_map/ppermute | solution.py:31
  34.2 20.8 %collective-permute-done.5.refs_5_ = bf16[128,1024]{1,0:T(8,128)(2,1)S(1)} collective-permute-done((bf16[128,1024]{1,0:T(8,128)(2,1)S(1)}, bf16[128,1024]{1,0:T(8,128)(2,1)S(1)}, u32[]{:S(2)}, u32[]{:S(2)}) %collective-permute-start.5) | collective-permute-done | bytes 262176 | tf_op jit(solution)/shard_map/ppermute | solution.py:31
  56.2 2.4 %collective-permute-start.1 = (bf16[16,512,128]{2,1,0:T(8,128)(2,1)S(1)}, bf16[16,512,128]{2,1,0:T(8,128)(2,1)}, u32[]{:S(2)}, u32[]{:S(2)}) collective-permute-start(bf16[16,512,128]{2,1,0:T(8,128)(2,1)S(1)} %all-to-all-done.refs_1_), channel_id=1, source_target_pairs={{0,32},{1,33},{2,34},{3,35},{4,36},{5,37},{6,38},{7,39},{8,40},{9,... | collective-permute-start | bytes 6291464 | tf_op jit(solution)/shard_map/ppermute | solution.py:31
  60.6 2.9 %shard_map.61 = (bf16[1024,512]{1,0:T(8,128)(2,1)}, bf16[1024,512]{1,0:T(8,128)(2,1)}) custom-call(bf16[128,1024]{1,0:T(8,128)(2,1)} %get-tuple-element.6.refs_0_, bf16[128,1024]{1,0:T(8,128)(2,1)} %copy-done.6, bf16[128,1024]{1,0:T(8,128)(2,1)} %copy-done.4, bf16[128,1024]{1,0:T(8,128)(2,1)} %collective-permute-done.3.refs_3_, bf16[128,1024]{1,0:T(8,128)(2,1)} %copy-done.8, ...), custom_call_target="tpu_custom_call" | custom-call | bytes 4194304 | tf_op jit(solution)/shard_map/pallas_call | solution.py:86
  66.2 12.8 %collective-permute-done.8.refs_4_ = bf16[1024,512]{1,0:T(8,128)(2,1)} collective-permute-done((bf16[1024,512]{1,0:T(8,128)(2,1)}, bf16[1024,512]{1,0:T(8,128)(2,1)}, u32[]{:S(2)}, u32[]{:S(2)}) %collective-permute-start.8) | collective-permute-done | bytes 1048608 | tf_op jit(solution)/shard_map/ppermute | solution.py:31
  79.1 2.9 %collective-permute-start.12 = (bf16[1024,512]{1,0:T(8,128)(2,1)}, bf16[1024,512]{1,0:T(8,128)(2,1)}, u32[]{:S(2)}, u32[]{:S(2)}) collective-permute-start(bf16[1024,512]{1,0:T(8,128)(2,1)} %get-tuple-element.9.refs_3_), channel_id=1, source_target_pairs={{0,24},{1,25},{2,26},{3,27},{4,28},{5,29},{6,30},{7,31},{8,0},{9,1... | collective-permute-start | bytes 3145736 | tf_op jit(solution)/shard_map/ppermute | solution.py:31
  83.3 3.6 %shard_map.62.refs_3_ = f32[512,512]{1,0:T(8,128)S(1)} custom-call(s32[16]{0:T(128)S(1)} %stack.79.refs_0_, bf16[16,512,128]{2,1,0:T(8,128)(2,1)S(1)} %all-to-all-done.refs_1_, bf16[16,512,128]{2,1,0:T(8,128)(2,1)} %collective-permute-done.1.refs_2_, bf16[1024,512]{1,0:T(8,128)(2,1)S(1)} %copy-done.3, bf16[1024,512]{1,0:T(8,128)(2,1)} %collective-permute-done.8.refs_4_, ...), custom_call_target="tpu_custom_call" | custom-call | flops 1610612736 | bytes 6291456 | tf_op jit(solution)/shard_map/pallas_call | solution.py:156
  86.9 7.5 %collective-permute-done.10.refs_4_ = bf16[1024,512]{1,0:T(8,128)(2,1)} collective-permute-done((bf16[1024,512]{1,0:T(8,128)(2,1)}, bf16[1024,512]{1,0:T(8,128)(2,1)}, u32[]{:S(2)}, u32[]{:S(2)}) %collective-permute-start.10) | collective-permute-done | bytes 1048608 | tf_op jit(solution)/shard_map/ppermute | solution.py:31
  94.5 3.5 %shard_map.63 = f32[512,512]{1,0:T(8,128)} custom-call(s32[16]{0:T(128)S(1)} %stack.79.refs_0_, bf16[16,512,128]{2,1,0:T(8,128)(2,1)S(1)} %all-to-all-done.refs_1_, bf16[16,512,128]{2,1,0:T(8,128)(2,1)} %collective-permute-done.1.refs_2_, f32[512,512]{1,0:T(8,128)S(1)} %shard_map.62.refs_3_, bf16[1024,512]{1,0:T(8,128)(2,1)} %collective-permute-done.10.refs_4_), custom_call_target="tpu_custom_call" | custom-call | flops 536870912 | bytes 2097152 | tf_op jit(solution)/shard_map/pallas_call | solution.py:156
  98.2 2.7 %collective-permute-start.13 = (bf16[1024,512]{1,0:T(8,128)(2,1)}, bf16[1024,512]{1,0:T(8,128)(2,1)S(1)}, u32[]{:S(2)}, u32[]{:S(2)}) collective-permute-start(bf16[1024,512]{1,0:T(8,128)(2,1)} %collective-permute-done.12.refs_5_), channel_id=1, source_target_pairs={{0,24},{1,25},{2,26},{3,27},{4,28},{5,29},{6,30},{7,31},{8,0},{9,1... | collective-permute-start | bytes 3145736 | tf_op jit(solution)/shard_map/ppermute | solution.py:31
  100.8 12.5 %collective-permute-done.11.refs_4_ = bf16[1024,512]{1,0:T(8,128)(2,1)S(1)} collective-permute-done((bf16[1024,512]{1,0:T(8,128)(2,1)S(1)}, bf16[1024,512]{1,0:T(8,128)(2,1)S(1)}, u32[]{:S(2)}, u32[]{:S(2)}) %collective-permute-start.11) | collective-permute-done | bytes 1048608 | tf_op jit(solution)/shard_map/ppermute | solution.py:31
  113.3 3.6 %shard_map.64.refs_3_ = f32[512,512]{1,0:T(8,128)S(1)} custom-call(s32[16]{0:T(128)S(1)} %stack.79.refs_0_, bf16[16,512,128]{2,1,0:T(8,128)(2,1)S(1)} %all-to-all-done.refs_1_, bf16[16,512,128]{2,1,0:T(8,128)(2,1)} %collective-permute-done.1.refs_2_, bf16[1024,512]{1,0:T(8,128)(2,1)S(1)} %copy-done.2, bf16[1024,512]{1,0:T(8,128)(2,1)S(1)} %collective-permute-done.11.refs_4_, ...), custom_call_target="tpu_custom_call" | custom-call | flops 1610612736 | bytes 6291456 | tf_op jit(solution)/shard_map/pallas_call | solution.py:156
  117.0 3.3 %shard_map.65 = f32[512,512]{1,0:T(8,128)} custom-call(s32[16]{0:T(128)S(1)} %stack.79.refs_0_, bf16[16,512,128]{2,1,0:T(8,128)(2,1)S(1)} %all-to-all-done.refs_1_, bf16[16,512,128]{2,1,0:T(8,128)(2,1)} %collective-permute-done.1.refs_2_, f32[512,512]{1,0:T(8,128)S(1)} %shard_map.64.refs_3_, bf16[1024,512]{1,0:T(8,128)(2,1)S(1)} %collective-permute-done.13.refs_4_), custom_call_target="tpu_custom_call" | custom-call | flops 536870912 | bytes 2097152 | tf_op jit(solution)/shard_map/pallas_call | solution.py:156
  120.3 15.3 %reduce-scatter.3.cloned.1.call-done = f32[64,512]{1,0:T(8,128)} async-done(((f32[512,512]{1,0:T(8,128)}), f32[64,512]{1,0:T(8,128)}) %reduce-scatter.3.cloned.1.call-update) | async-done | bytes 131088 | tf_op jit(solution)/shard_map/reduce_scatter | solution.py:225
  137.2 38.1 %reduce-scatter.5.cloned.1.call-done = f32[64,512]{1,0:T(8,128)} async-done(((f32[512,512]{1,0:T(8,128)}), f32[64,512]{1,0:T(8,128)}) %reduce-scatter.5.cloned.1.call-update) | async-done | bytes 131088 | tf_op jit(solution)/shard_map/reduce_scatter | solution.py:225
  178.9 15.0 %all-to-all-start.1 = ((f32[256,1,128]{2,1,0:T(1,128)}), f32[256,1,128]{2,1,0:T(1,128)S(1)}, u32[]{:S(2)}, u32[]{:S(2)}) async-start(f32[256,1,128]{2,1,0:T(1,128)} %broadcast_in_dim.3), calls=%async_computation.3 | async-start | bytes 262144 | tf_op jit(solution)/shard_map/all_to_all | solution.py:171
  194.0 2.2 %collective-permute-start.14 = (f32[32,1024]{1,0:T(8,128)S(1)}, f32[32,1024]{1,0:T(8,128)S(1)}, u32[]{:S(2)}, u32[]{:S(2)}) collective-permute-start(f32[32,1024]{1,0:T(8,128)S(1)} %slice_select_fusion), channel_id=1, source_target_pairs={{0,32},{1,33},{2,34},{3,35},{4,36},{5,37},{6,38},{7,39},{8,40},{9,... | collective-permute-start | bytes 393224 | tf_op jit(solution)/shard_map/ppermute | solution.py:31
  196.2 10.8 %all-to-all-done.1 = f32[256,1,128]{2,1,0:T(1,128)S(1)} async-done(((f32[256,1,128]{2,1,0:T(1,128)}), f32[256,1,128]{2,1,0:T(1,128)S(1)}, u32[]{:S(2)}, u32[]{:S(2)}) %all-to-all-start.1) | async-done | bytes 131104 | tf_op jit(solution)/shard_map/all_to_all | solution.py:171
  (51 shorter events, 18.0 us)
Async XLA Ops:
  9.8 7.5 %collective-permute-start = (bf16[128,1024]{1,0:T(8,128)(2,1)}, bf16[128,1024]{1,0:T(8,128)(2,1)S(1)}, u32[]{:S(2)}, u32[]{:S(2)}) collective-permute-start(bf16[128,1024]{1,0:T(8,128)(2,1)} %get-tuple-element.6.refs_0_), channel_id=1, source_target_pairs={{0,64},{1,65},{2,66},{3,67},{4,68},{5,69},{6,70},{7,71},{8,72},{9,... | collective-permute-start | bytes 786440 | tf_op jit(solution)/shard_map/ppermute | solution.py:31
  18.9 15.3 %copy-start.4 = (bf16[128,1024]{1,0:T(8,128)(2,1)}, bf16[128,1024]{1,0:T(8,128)(2,1)S(1)}, u32[]{:S(2)}) copy-start(bf16[128,1024]{1,0:T(8,128)(2,1)S(1)} %collective-permute-done.after_ref.refs_2_) | copy-start | bytes 786436
  20.8 6.0 %copy-start.9 = (bf16[128,1024]{1,0:T(8,128)(2,1)S(1)}, bf16[128,1024]{1,0:T(8,128)(2,1)}, u32[]{:S(2)}) copy-start(bf16[128,1024]{1,0:T(8,128)(2,1)} %get-tuple-element.7) | copy-start | bytes 786436
  20.8 11.9 %copy-start.5 = (bf16[128,1024]{1,0:T(8,128)(2,1)S(1)}, bf16[128,1024]{1,0:T(8,128)(2,1)}, u32[]{:S(2)}) copy-start(bf16[128,1024]{1,0:T(8,128)(2,1)} %get-tuple-element.6.refs_0_) | copy-start | bytes 786436
  20.8 35.4 %all-to-all-start = ((bf16[16,512,128]{2,1,0:T(8,128)(2,1)}), bf16[16,512,128]{2,1,0:T(8,128)(2,1)S(1)}, u32[]{:S(2)}, u32[]{:S(2)}) async-start(bf16[16,512,128]{2,1,0:T(8,128)(2,1)} %copy-done), calls=%async_computation | async-start | bytes 4194304 | tf_op jit(solution)/shard_map/all_to_all | solution.py:203
  26.7 108.9 %reduce-scatter.3.cloned.1.call-start = ((), (), s32[]{:S(2)}) async-start(), calls=%async_computation.4 | async-start | bytes 1179648 | tf_op jit(solution)/shard_map/reduce_scatter | solution.py:225
  26.8 3.1 %collective-permute-start.2 = (bf16[128,1024]{1,0:T(8,128)(2,1)S(1)}, bf16[128,1024]{1,0:T(8,128)(2,1)S(1)}, u32[]{:S(2)}, u32[]{:S(2)}) collective-permute-start(bf16[128,1024]{1,0:T(8,128)(2,1)S(1)} %copy-done.9), channel_id=1, source_target_pairs={{0,32},{1,33},{2,34},{3,35},{4,36},{5,37},{6,38},{7,39},{8,40},{9,... | collective-permute-start | bytes 786440 | tf_op jit(solution)/shard_map/ppermute | solution.py:31
  29.9 30.8 %copy-start.6 = (bf16[128,1024]{1,0:T(8,128)(2,1)}, bf16[128,1024]{1,0:T(8,128)(2,1)S(1)}, u32[]{:S(2)}) copy-start(bf16[128,1024]{1,0:T(8,128)(2,1)S(1)} %collective-permute-done.2.refs_1_) | copy-start | bytes 786436
  29.9 25.1 %collective-permute-start.5 = (bf16[128,1024]{1,0:T(8,128)(2,1)S(1)}, bf16[128,1024]{1,0:T(8,128)(2,1)S(1)}, u32[]{:S(2)}, u32[]{:S(2)}) collective-permute-start(bf16[128,1024]{1,0:T(8,128)(2,1)S(1)} %collective-permute-done.2.refs_1_), channel_id=1, source_target_pairs={{0,192},{1,193},{2,194},{3,195},{4,196},{5,197},{6,198},{7,199},{8... | collective-permute-start | bytes 786440 | tf_op jit(solution)/shard_map/ppermute | solution.py:31
  32.7 25.9 %collective-permute-start.4 = (bf16[128,1024]{1,0:T(8,128)(2,1)S(1)}, bf16[128,1024]{1,0:T(8,128)(2,1)S(1)}, u32[]{:S(2)}, u32[]{:S(2)}) collective-permute-start(bf16[128,1024]{1,0:T(8,128)(2,1)S(1)} %copy-done.5), channel_id=1, source_target_pairs={{0,192},{1,193},{2,194},{3,195},{4,196},{5,197},{6,198},{7,199},{8... | collective-permute-start | bytes 786440 | tf_op jit(solution)/shard_map/ppermute | solution.py:31
  33.3 25.3 %collective-permute-start.3 = (bf16[128,1024]{1,0:T(8,128)(2,1)S(1)}, bf16[128,1024]{1,0:T(8,128)(2,1)}, u32[]{:S(2)}, u32[]{:S(2)}) collective-permute-start(bf16[128,1024]{1,0:T(8,128)(2,1)S(1)} %collective-permute-done.2.refs_1_), channel_id=1, source_target_pairs={{0,64},{1,65},{2,66},{3,67},{4,68},{5,69},{6,70},{7,71},{8,72},{9,... | collective-permute-start | bytes 786440 | tf_op jit(solution)/shard_map/ppermute | solution.py:31
  34.2 25.1 %collective-permute-start.6 = (bf16[128,1024]{1,0:T(8,128)(2,1)S(1)}, bf16[128,1024]{1,0:T(8,128)(2,1)}, u32[]{:S(2)}, u32[]{:S(2)}) collective-permute-start(bf16[128,1024]{1,0:T(8,128)(2,1)S(1)} %collective-permute-done.after_ref.refs_2_), channel_id=1, source_target_pairs={{0,64},{1,65},{2,66},{3,67},{4,68},{5,69},{6,70},{7,71},{8,72},{9,... | collective-permute-start | bytes 786440 | tf_op jit(solution)/shard_map/ppermute | solution.py:31
  55.0 5.6 %collective-permute-start.7 = (bf16[128,1024]{1,0:T(8,128)(2,1)S(1)}, bf16[128,1024]{1,0:T(8,128)(2,1)}, u32[]{:S(2)}, u32[]{:S(2)}) collective-permute-start(bf16[128,1024]{1,0:T(8,128)(2,1)S(1)} %collective-permute-done.5.refs_5_), channel_id=1, source_target_pairs={{0,192},{1,193},{2,194},{3,195},{4,196},{5,197},{6,198},{7,199},{8... | collective-permute-start | bytes 786440 | tf_op jit(solution)/shard_map/ppermute | solution.py:31
  56.2 25.8 %collective-permute-start.1 = (bf16[16,512,128]{2,1,0:T(8,128)(2,1)S(1)}, bf16[16,512,128]{2,1,0:T(8,128)(2,1)}, u32[]{:S(2)}, u32[]{:S(2)}) collective-permute-start(bf16[16,512,128]{2,1,0:T(8,128)(2,1)S(1)} %all-to-all-done.refs_1_), channel_id=1, source_target_pairs={{0,32},{1,33},{2,34},{3,35},{4,36},{5,37},{6,38},{7,39},{8,40},{9,... | collective-permute-start | bytes 6291464 | tf_op jit(solution)/shard_map/ppermute | solution.py:31
  63.5 15.5 %collective-permute-start.8 = (bf16[1024,512]{1,0:T(8,128)(2,1)}, bf16[1024,512]{1,0:T(8,128)(2,1)}, u32[]{:S(2)}, u32[]{:S(2)}) collective-permute-start(bf16[1024,512]{1,0:T(8,128)(2,1)} %get-tuple-element.8.refs_3_), channel_id=1, source_target_pairs={{0,8},{1,9},{2,10},{3,11},{4,12},{5,13},{6,14},{7,15},{8,16},{9,17... | collective-permute-start | bytes 3145736 | tf_op jit(solution)/shard_map/ppermute | solution.py:31
  64.7 17.3 %collective-permute-start.9 = (bf16[1024,512]{1,0:T(8,128)(2,1)}, bf16[1024,512]{1,0:T(8,128)(2,1)S(1)}, u32[]{:S(2)}, u32[]{:S(2)}) collective-permute-start(bf16[1024,512]{1,0:T(8,128)(2,1)} %get-tuple-element.8.refs_3_), channel_id=1, source_target_pairs={{0,24},{1,25},{2,26},{3,27},{4,28},{5,29},{6,30},{7,31},{8,0},{9,1... | collective-permute-start | bytes 3145736 | tf_op jit(solution)/shard_map/ppermute | solution.py:31
  79.0 15.5 %collective-permute-start.10 = (bf16[1024,512]{1,0:T(8,128)(2,1)}, bf16[1024,512]{1,0:T(8,128)(2,1)}, u32[]{:S(2)}, u32[]{:S(2)}) collective-permute-start(bf16[1024,512]{1,0:T(8,128)(2,1)} %collective-permute-done.8.refs_4_), channel_id=1, source_target_pairs={{0,8},{1,9},{2,10},{3,11},{4,12},{5,13},{6,14},{7,15},{8,16},{9,17... | collective-permute-start | bytes 3145736 | tf_op jit(solution)/shard_map/ppermute | solution.py:31
  79.1 19.1 %collective-permute-start.12 = (bf16[1024,512]{1,0:T(8,128)(2,1)}, bf16[1024,512]{1,0:T(8,128)(2,1)}, u32[]{:S(2)}, u32[]{:S(2)}) collective-permute-start(bf16[1024,512]{1,0:T(8,128)(2,1)} %get-tuple-element.9.refs_3_), channel_id=1, source_target_pairs={{0,24},{1,25},{2,26},{3,27},{4,28},{5,29},{6,30},{7,31},{8,0},{9,1... | collective-permute-start | bytes 3145736 | tf_op jit(solution)/shard_map/ppermute | solution.py:31
  86.9 11.2 %copy-start.2 = (bf16[1024,512]{1,0:T(8,128)(2,1)S(1)}, bf16[1024,512]{1,0:T(8,128)(2,1)}, u32[]{:S(2)}) copy-start(bf16[1024,512]{1,0:T(8,128)(2,1)} %get-tuple-element.9.refs_3_) | copy-start | bytes 3145732
  98.0 77.3 %reduce-scatter.5.cloned.1.call-start = ((), (), s32[]{:S(2)}) async-start(), calls=%async_computation.5 | async-start | bytes 1179648 | tf_op jit(solution)/shard_map/reduce_scatter | solution.py:225
  98.1 15.2 %collective-permute-start.11 = (bf16[1024,512]{1,0:T(8,128)(2,1)S(1)}, bf16[1024,512]{1,0:T(8,128)(2,1)S(1)}, u32[]{:S(2)}, u32[]{:S(2)}) collective-permute-start(bf16[1024,512]{1,0:T(8,128)(2,1)S(1)} %copy-done.2), channel_id=1, source_target_pairs={{0,8},{1,9},{2,10},{3,11},{4,12},{5,13},{6,14},{7,15},{8,16},{9,17... | collective-permute-start | bytes 3145736 | tf_op jit(solution)/shard_map/ppermute | solution.py:31
  98.2 18.8 %collective-permute-start.13 = (bf16[1024,512]{1,0:T(8,128)(2,1)}, bf16[1024,512]{1,0:T(8,128)(2,1)S(1)}, u32[]{:S(2)}, u32[]{:S(2)}) collective-permute-start(bf16[1024,512]{1,0:T(8,128)(2,1)} %collective-permute-done.12.refs_5_), channel_id=1, source_target_pairs={{0,24},{1,25},{2,26},{3,27},{4,28},{5,29},{6,30},{7,31},{8,0},{9,1... | collective-permute-start | bytes 3145736 | tf_op jit(solution)/shard_map/ppermute | solution.py:31
  178.9 28.1 %all-to-all-start.1 = ((f32[256,1,128]{2,1,0:T(1,128)}), f32[256,1,128]{2,1,0:T(1,128)S(1)}, u32[]{:S(2)}, u32[]{:S(2)}) async-start(f32[256,1,128]{2,1,0:T(1,128)} %broadcast_in_dim.3), calls=%async_computation.3 | async-start | bytes 262144 | tf_op jit(solution)/shard_map/all_to_all | solution.py:171
  194.0 14.6 %collective-permute-start.14 = (f32[32,1024]{1,0:T(8,128)S(1)}, f32[32,1024]{1,0:T(8,128)S(1)}, u32[]{:S(2)}, u32[]{:S(2)}) collective-permute-start(f32[32,1024]{1,0:T(8,128)S(1)} %slice_select_fusion), channel_id=1, source_target_pairs={{0,32},{1,33},{2,34},{3,35},{4,36},{5,37},{6,38},{7,39},{8,40},{9,... | collective-permute-start | bytes 393224 | tf_op jit(solution)/shard_map/ppermute | solution.py:31
  (5 other events, 11.8 us)
Sparse Core Ops, SparseCore 0:
  98.2 37.4 reduce-scatter.2
  138.2 37.1 reduce-scatter.4

commit v5 on v3

v5 whole, which is shorter than its diff:
```python
import functools
import itertools
import math

import jax
import jax.numpy as jnp
from jax import lax
from jax.experimental import pallas as pl
from jax.experimental.pallas import tpu as pltpu
from jax.sharding import Mesh, PartitionSpec as P

CH = 512
AXES = ("x", "c", "y", "z")
NX, NC, NY, NZ = 4, 2, 4, 8
DEVICES = NX * NC * NY * NZ
OFFSETS = (0, -1, 1, 2)
COLUMNS = 256


def pairs(move):
    out = []
    for x, c, y, z in itertools.product(range(NX), range(NC), range(NY), range(NZ)):
        tx, tc, ty, tz = move(x, c, y, z)
        source = ((x * NC + c) * NY + y) * NZ + z
        target = (((tx % NX) * NC + tc % NC) * NY + ty % NY) * NZ + tz % NZ
        out.append((source, target))
    return out


def send(value, move):
    return lax.ppermute(value, AXES, pairs(move))


def swap_cores(value):
    return send(value, lambda x, c, y, z: (x, 1 - c, y, z))


def first_ring(value, step):
    return send(value, lambda x, c, y, z: (x + step, c, y, z) if c == 0 else (x, c, y + step, z))


def second_ring(value, step):
    return send(value, lambda x, c, y, z: (x, c, y + step, z) if c == 0 else (x + step, c, y, z))


def z_ring(value, step):
    return send(value, lambda x, c, y, z: (x, c, y, z + step))


VMEM = pl.BlockSpec(memory_space=pltpu.VMEM)
SMEM = pl.BlockSpec(memory_space=pltpu.SMEM)
ANY = pl.BlockSpec(memory_space=pl.ANY)


def mask_kernel(place_ref, lengths_ref, keys_ref, values_ref, mine_ref, theirs_ref):
    is_keys = place_ref[0] == 0
    limit = lengths_ref[place_ref[1]] - place_ref[2]
    keys, values = keys_ref[...], values_ref[...]
    rows = lax.broadcasted_iota(jnp.int32, keys.shape, 0)
    zero = jnp.zeros_like(keys)
    keys = jnp.where(rows < limit, keys, zero)
    values = jnp.where(rows < limit, values, zero)
    mine_ref[...] = jnp.where(is_keys, keys, values)
    theirs_ref[...] = jnp.where(is_keys, values, keys)


def mask(place, block_lengths, key_grads, value_grads):
    return pl.pallas_call(
        mask_kernel,
        out_shape=[jax.ShapeDtypeStruct(key_grads.shape, key_grads.dtype)] * 2,
        in_specs=[SMEM, SMEM, VMEM, VMEM],
        out_specs=[VMEM, VMEM],
        cost_estimate=pl.CostEstimate(
            flops=key_grads.size, bytes_accessed=8 * key_grads.size, transcendentals=0
        ),
    )(place, block_lengths, key_grads, value_grads)


def stack(pieces):
    tok_count, width = pieces[0].shape
    half = len(pieces) // 2

    def kernel(*refs):
        for i, piece_ref in enumerate(refs[:-2]):
            refs[-2 + i // half][pl.ds(i % half * tok_count, tok_count), :] = piece_ref[...]

    return pl.pallas_call(
        kernel,
        out_shape=[jax.ShapeDtypeStruct((half * tok_count, width), pieces[0].dtype)] * 2,
        in_specs=[VMEM] * len(pieces),
        out_specs=[VMEM] * 2,
        cost_estimate=pl.CostEstimate(
            flops=0, bytes_accessed=8 * half * tok_count * width, transcendentals=0
        ),
    )(*pieces)


def transpose_kernel(acts_ref, out_ref):
    owner_rows = out_ref.shape[1] // NZ
    for at in range(0, acts_ref.shape[1], 128):
        turned = acts_ref[:, at : at + 128].T
        for low in range(0, 128, owner_rows):
            piece = (at + low) // owner_rows
            y, z, x = piece // (NZ * NX), piece // NX % NZ, piece % NX
            out_ref[y * NX + x, z * owner_rows : (z + 1) * owner_rows, :] = turned[
                low : low + owner_rows
            ]


def transpose(acts):
    tok_count, model_width = acts.shape
    return pl.pallas_call(
        transpose_kernel,
        out_shape=jax.ShapeDtypeStruct(
            (NX * NY, model_width // (NX * NY), tok_count), acts.dtype
        ),
        in_specs=[VMEM],
        out_specs=VMEM,
        compiler_params=pltpu.CompilerParams(vmem_limit_bytes=24 * 1024 * 1024),
        cost_estimate=pl.CostEstimate(
            flops=acts.size, bytes_accessed=4 * acts.size, transcendentals=0
        ),
    )(acts)


def choose(index, acts, other):
    blocks, width, tok_count = acts.shape

    def kernel(index_ref, acts_ref, other_ref, out_ref):
        for at in range(blocks):
            low = at % 2 * 2 * tok_count
            block = index_ref[at]
            out_ref[at // 2, :, low : low + tok_count] = acts_ref[block]
            out_ref[at // 2, :, low + tok_count : low + 2 * tok_count] = other_ref[block]

    return pl.pallas_call(
        kernel,
        out_shape=jax.ShapeDtypeStruct((blocks // 2, width, 4 * tok_count), acts.dtype),
        in_specs=[SMEM, VMEM, VMEM],
        out_specs=VMEM,
        compiler_params=pltpu.CompilerParams(vmem_limit_bytes=24 * 1024 * 1024),
        cost_estimate=pl.CostEstimate(
            flops=0, bytes_accessed=8 * acts.size, transcendentals=0
        ),
    )(index, acts, other)


def multiply(chosen, parts, first, start=None):
    _, width, depth = chosen.shape
    n = parts[0].shape[1]
    count = len(parts)

    def kernel(chosen_ref, *refs):
        total = None if start is None else refs[count][...]
        for part in range(count):
            product = jnp.dot(
                chosen_ref[part], refs[part][...], preferred_element_type=jnp.float32
            )
            total = product if total is None else total + product
        refs[-1][...] = total

    columns = pl.BlockSpec((width, COLUMNS), lambda i: (0, i))
    return pl.pallas_call(
        kernel,
        out_shape=jax.ShapeDtypeStruct((width, n), jnp.float32),
        grid=(n // COLUMNS,),
        in_specs=[pl.BlockSpec((count, width, depth), lambda i: (first // count, 0, 0))]
        + [pl.BlockSpec((depth, COLUMNS), lambda i: (0, i))] * count
        + ([] if start is None else [columns]),
        out_specs=columns,
        compiler_params=pltpu.CompilerParams(vmem_limit_bytes=32 * 1024 * 1024),
        cost_estimate=pl.CostEstimate(
            flops=2 * width * n * depth * count,
            bytes_accessed=2 * depth * count * (n + width),
            transcendentals=0,
        ),
    )(chosen, *parts, *(() if start is None else (start,)))


def reduce_z(partial, z):
    rows = partial.shape[0] // NZ
    half = rows // 2

    def block(offset):
        return lax.dynamic_slice_in_dim(partial, lax.rem(z + offset + NZ, NZ) * rows, rows, axis=0)

    far = block(4)
    up = z_ring(far[:half], 1)
    down = z_ring(far[half:], -1)
    near_up, near_down = block(3), block(-3)
    up = z_ring(jnp.concatenate((near_up[:half] + up, near_up[half:]), axis=0), 1)
    down = z_ring(jnp.concatenate((near_down[:half], near_down[half:] + down), axis=0), -1)
    for offset in (2, 1):
        up = z_ring(block(offset) + up, 1)
        down = z_ring(block(-offset) + down, -1)
    return block(0) + up + down


def sum_all(value):
    rows = jnp.broadcast_to(value, (DEVICES, 1, 128))
    return jnp.sum(lax.all_to_all(rows, AXES, split_axis=0, concat_axis=0, tiled=True)[:, 0, 0])


def body(activations, key_grads, value_grads, block_lengths):
    tok_count, model_width = activations.shape
    head_width = key_grads.shape[1]
    x, c, y, z = (lax.axis_index(axis) for axis in AXES)
    is_keys = c == 0
    position = (((x * NC + c) * NY + y) * NZ + z) * tok_count
    clip_norm = math.sqrt(2.0 * model_width * head_width)

    place = jnp.stack((c, lax.div(position, CH), lax.rem(position, CH))).astype(jnp.int32)
    mine, theirs = mask(place, block_lengths, key_grads, value_grads)
    received = swap_cores(theirs)
    mine_before, mine_after = first_ring(mine, 1), first_ring(mine, -1)
    received_before, received_after = first_ring(received, 1), first_ring(received, -1)
    pieces = (mine, received, mine_before, received_before, mine_after, received_after)
    pieces += (first_ring(mine_before, 1), first_ring(received_after, -1))

    across, *_ = lax.optimization_barrier((transpose(activations), *pieces))
    acts = lax.all_to_all(across, ("y", "x"), split_axis=0, concat_axis=0, tiled=True)

    first, second = jnp.where(is_keys, x, y), jnp.where(is_keys, y, x)
    index = []
    for offset2 in OFFSETS:
        for offset1 in OFFSETS:
            at1, at2 = lax.rem(first + offset1 + 4, 4), lax.rem(second + offset2 + 4, 4)
            index.append(jnp.where(is_keys, at2 * NX + at1, at1 * NX + at2))
    index = jnp.stack(index).astype(jnp.int32)

    upper, lower = stack(pieces)
    upper_before, upper_after = second_ring(upper, 1), second_ring(upper, -1)
    lower_before, lower_after = second_ring(lower, 1), second_ring(lower, -1)
    acts, upper_before, upper_after, lower_before, lower_after = lax.optimization_barrier(
        (acts, upper_before, upper_after, lower_before, lower_after)
    )
    chosen = choose(index, acts, swap_cores(acts))
    opposite = [second_ring(upper_before, 1), second_ring(lower_after, -1)]
    direct = [upper, lower, upper_before, lower_before, upper_after, lower_after]
    weight = multiply(chosen, direct, 0)
    weight = multiply(chosen, opposite, 6, weight)
    owned = reduce_z(weight, z)

    total = sum_all(jnp.sum(owned * owned))
    half = owned.shape[0] // 2
    kept = jnp.where(is_keys, owned[:half], owned[half:])
    swapped = swap_cores(jnp.where(is_keys, owned[half:], owned[:half]))
    factor = jnp.minimum(1.0, clip_norm / jnp.sqrt(total))
    key_clipped = (jnp.where(is_keys, kept, swapped) * factor).astype(jnp.bfloat16)
    value_clipped = (jnp.where(is_keys, swapped, kept) * factor).astype(jnp.bfloat16)
    return key_clipped, value_clipped


def solution(mesh):
    fine = Mesh(mesh.devices.reshape(NX, NC, NY, NZ), AXES)
    tokens = P(AXES, None)
    owners = P(("y", "z", "x", "c"), None)
    return jax.shard_map(
        body,
        mesh=fine,
        in_specs=(tokens, tokens, tokens, P()),
        out_specs=(owners, owners),
        check_vma=False,
    )
```

time: 175 us -> 168 us (0.960)
  waiting for transfers between devices: 67.4 us -> 84.3 us
  starting transfers between devices: 71 us -> 55.3 us
  local copies, waits for them, and re-layouts: 13.9 us -> 5.79 us
  Pallas kernels: 15.6 us -> 17.6 us
    ppermute x32 -> x23, waiting for transfers between devices: 53.8 us -> 73.6 us  [send(): return lax.ppermute(value, AXES, pairs(move))]
    ppermute x32 -> x23, starting transfers between devices: 46.1 us -> 30.8 us  [send(): return lax.ppermute(value, AXES, pairs(move))]
    unnamed x14 -> x30, local copies, waits for them, and re-layouts: 9.69 us -> 4.32 us
    pallas_call x1 -> x3, Pallas kernels: 1.87 us -> 7.16 us  [the longest x1 2.9 us: stack(): pl.pallas_call(kernel, out_shape=[jax.ShapeDtypeStruct((half * tok_count,...]
    pallas_call x4 -> x2, Pallas kernels: 13.2 us -> 8.53 us  [multiply(): pl.pallas_call(kernel, out_shape=jax.ShapeDtypeStruct((width, n), jnp.flo...]
    concatenate x3 -> x0, local copies, waits for them, and re-layouts: 3.32 us -> none  [the longest x2 2.65 us: body(): lump = jnp.concatenate((grad, before, after, opposite), axis=0)]
    all_to_all x1, waiting for transfers between devices: 2.79 us -> 0.01 us  [body(): lax.all_to_all(across, ('y', 'x'), split_axis=0, concat_axis=0, tiled=True)]
  transfers between devices with their start and end apart: 34 -> 25, of which waited for: 15 -> 13; matrix products, arithmetic and copies ran while one was open for 6% -> 1% of each run, Pallas kernels for 8% -> 7%
where the time goes in v5:
time: 168 us
  waiting for transfers between devices  84.3 us (50%)
  starting transfers between devices  55.3 us (33%)
  Pallas kernels  17.6 us (10%)
  local copies, waits for them, and re-layouts  5.79 us (3%)
  other arithmetic  3.11 us (2%)
    ppermute x23, waiting for transfers between devices, send(): return lax.ppermute(value, AXES, pairs(move))  73.6 us
    ppermute x23, starting transfers between devices, send(): return lax.ppermute(value, AXES, pairs(move))  30.8 us
    all_to_all x1, starting transfers between devices, sum_all(): lax.all_to_all(rows, AXES, split_axis=0, concat_axis=0, tiled=True)[:, 0, 0]  19.4 us
    all_to_all x1, waiting for transfers between devices, sum_all(): lax.all_to_all(rows, AXES, split_axis=0, concat_axis=0, tiled=True)[:, 0, 0]  10.8 us
    pallas_call x2, Pallas kernels, multiply(): pl.pallas_call(kernel, out_shape=jax.ShapeDtypeStruct((width, n), jnp.flo...  8.53 us
    all_to_all x1, starting transfers between devices, body(): lax.all_to_all(across, ('y', 'x'), split_axis=0, concat_axis=0, tiled=True)  5.14 us
    unnamed x30, local copies, waits for them, and re-layouts  4.32 us
  transfers between devices with their start and end apart: 25, of which 13 were waited for; matrix products, arithmetic and copies ran while one was open for 1% of the time, Pallas kernels for 7%

profile of v5, /device:TPU:1, one launch (start us, length us, event | category | flops | bytes accessed | tf_op | source)
XLA Modules:
  0.0 167.8 jit_solution(13153723927092244732)
XLA Ops:
  3.2 3.2 %collective-permute-start = (bf16[128,1024]{1,0:T(8,128)(2,1)}, bf16[128,1024]{1,0:T(8,128)(2,1)S(1)}, u32[]{:S(2)}, u32[]{:S(2)}) collective-permute-start(bf16[128,1024]{1,0:T(8,128)(2,1)} %get-tuple-element.13), channel_id=1, source_target_pairs={{0,32},{1,33},{2,34},{3,35},{4,36},{5,37},{6,38},{7,39},{8,40},{9,... | collective-permute-start | bytes 786440 | tf_op jit(solution)/shard_map/ppermute | solution.py:31
  10.6 2.8 %collective-permute-done.1.refs_2_ = bf16[128,1024]{1,0:T(8,128)(2,1)S(1)} collective-permute-done((bf16[128,1024]{1,0:T(8,128)(2,1)}, bf16[128,1024]{1,0:T(8,128)(2,1)S(1)}, u32[]{:S(2)}, u32[]{:S(2)}) %collective-permute-start.1) | collective-permute-done | bytes 262176 | tf_op jit(solution)/shard_map/ppermute | solution.py:31
  13.4 2.7 %collective-permute-start.6 = (bf16[128,1024]{1,0:T(8,128)(2,1)S(1)}, bf16[128,1024]{1,0:T(8,128)(2,1)}, u32[]{:S(2)}, u32[]{:S(2)}) collective-permute-start(bf16[128,1024]{1,0:T(8,128)(2,1)S(1)} %collective-permute-done.4.refs_5_), channel_id=1, source_target_pairs={{0,192},{1,193},{2,194},{3,195},{4,196},{5,197},{6,198},{7,199},{8... | collective-permute-start | bytes 786440 | tf_op jit(solution)/shard_map/ppermute | solution.py:31
  17.6 2.0 %shard_map.59 = bf16[16,512,128]{2,1,0:T(8,128)(2,1)} custom-call(bf16[128,8192]{1,0:T(8,128)(2,1)S(1)} %copy-done), custom_call_target="tpu_custom_call" | custom-call | flops 1048576 | bytes 4194304 | tf_op jit(solution)/shard_map/pallas_call | solution.py:112
  20.8 5.1 %all-to-all-start = ((bf16[16,512,128]{2,1,0:T(8,128)(2,1)}), bf16[16,512,128]{2,1,0:T(8,128)(2,1)S(1)}, u32[]{:S(2)}, u32[]{:S(2)}) async-start(bf16[16,512,128]{2,1,0:T(8,128)(2,1)} %shard_map.59), calls=%async_computation | async-start | bytes 4194304 | tf_op jit(solution)/shard_map/all_to_all | solution.py:221
  25.9 2.9 %shard_map.61 = (bf16[512,1024]{1,0:T(8,128)(2,1)}, bf16[512,1024]{1,0:T(8,128)(2,1)}) custom-call(bf16[128,1024]{1,0:T(8,128)(2,1)} %get-tuple-element.12.refs_0_, bf16[128,1024]{1,0:T(8,128)(2,1)} %copy-done.9, bf16[128,1024]{1,0:T(8,128)(2,1)} %copy-done.10, bf16[128,1024]{1,0:T(8,128)(2,1)} %copy-done.13, bf16[128,1024]{1,0:T(8,128)(2,1)} %copy-done.12, ...), custom_call_target="tpu_custom_call" | custom-call | bytes 4194304 | tf_op jit(solution)/shard_map/pallas_call | solution.py:87
  28.8 2.6 %collective-permute-start.10 = (bf16[512,1024]{1,0:T(8,128)(2,1)}, bf16[512,1024]{1,0:T(8,128)(2,1)S(1)}, u32[]{:S(2)}, u32[]{:S(2)}) collective-permute-start(bf16[512,1024]{1,0:T(8,128)(2,1)} %get-tuple-element.16.refs_1_), channel_id=1, source_target_pairs={{0,24},{1,25},{2,26},{3,27},{4,28},{5,29},{6,30},{7,31},{8,0},{9,1... | collective-permute-start | bytes 3145736 | tf_op jit(solution)/shard_map/ppermute | solution.py:31
  31.4 2.7 %collective-permute-start.8 = (bf16[512,1024]{1,0:T(8,128)(2,1)}, bf16[512,1024]{1,0:T(8,128)(2,1)S(1)}, u32[]{:S(2)}, u32[]{:S(2)}) collective-permute-start(bf16[512,1024]{1,0:T(8,128)(2,1)} %get-tuple-element.15.refs_0_), channel_id=1, source_target_pairs={{0,24},{1,25},{2,26},{3,27},{4,28},{5,29},{6,30},{7,31},{8,0},{9,1... | collective-permute-start | bytes 3145736 | tf_op jit(solution)/shard_map/ppermute | solution.py:31
  34.1 29.9 %collective-permute-done.10.refs_5_ = bf16[512,1024]{1,0:T(8,128)(2,1)S(1)} collective-permute-done((bf16[512,1024]{1,0:T(8,128)(2,1)}, bf16[512,1024]{1,0:T(8,128)(2,1)S(1)}, u32[]{:S(2)}, u32[]{:S(2)}) %collective-permute-start.10) | collective-permute-done | bytes 1048608 | tf_op jit(solution)/shard_map/ppermute | solution.py:31
  64.0 11.2 %collective-permute-done.8.refs_4_ = bf16[512,1024]{1,0:T(8,128)(2,1)S(1)} collective-permute-done((bf16[512,1024]{1,0:T(8,128)(2,1)}, bf16[512,1024]{1,0:T(8,128)(2,1)S(1)}, u32[]{:S(2)}, u32[]{:S(2)}) %collective-permute-start.8) | collective-permute-done | bytes 1048608 | tf_op jit(solution)/shard_map/ppermute | solution.py:31
  81.5 2.4 %shard_map.62.chosen_ref = bf16[8,512,512]{2,1,0:T(8,128)(2,1)S(1)} custom-call(s32[16]{0:T(128)S(1)} %stack.79.index_ref, bf16[16,512,128]{2,1,0:T(8,128)(2,1)S(1)} %all-to-all-done.acts_ref, bf16[16,512,128]{2,1,0:T(8,128)(2,1)} %collective-permute-done.11.other_ref), custom_call_target="tpu_custom_call" | custom-call | bytes 8388608 | tf_op jit(solution)/shard_map/pallas_call | solution.py:136
  83.9 4.9 %shard_map.63.refs_2_ = f32[512,1024]{1,0:T(8,128)S(1)} custom-call(bf16[8,512,512]{2,1,0:T(8,128)(2,1)S(1)} %shard_map.62.chosen_ref, bf16[512,1024]{1,0:T(8,128)(2,1)S(1)} %copy-done.1, bf16[512,1024]{1,0:T(8,128)(2,1)S(1)} %copy-done.2, bf16[512,1024]{1,0:T(8,128)(2,1)S(1)} %copy-done.4, bf16[512,1024]{1,0:T(8,128)(2,1)S(1)} %copy-done.8, ...), custom_call_target="tpu_custom_call" | custom-call | flops 3221225472 | bytes 9437184 | tf_op jit(solution)/shard_map/pallas_call | solution.py:163
  88.9 3.8 %collective-permute-done.12.refs_0_ = bf16[512,1024]{1,0:T(8,128)(2,1)} collective-permute-done((bf16[512,1024]{1,0:T(8,128)(2,1)}, bf16[512,1024]{1,0:T(8,128)(2,1)}, u32[]{:S(2)}, u32[]{:S(2)}) %collective-permute-start.12) | collective-permute-done | bytes 1048608 | tf_op jit(solution)/shard_map/ppermute | solution.py:31
  92.7 3.6 %shard_map.64 = f32[512,1024]{1,0:T(8,128)S(1)} custom-call(bf16[8,512,512]{2,1,0:T(8,128)(2,1)S(1)} %shard_map.62.chosen_ref, bf16[512,1024]{1,0:T(8,128)(2,1)} %collective-permute-done.12.refs_0_, bf16[512,1024]{1,0:T(8,128)(2,1)} %collective-permute-done.13.refs_1_, f32[512,1024]{1,0:T(8,128)S(1)} %shard_map.63.refs_2_), custom_call_target="tpu_custom_call" | custom-call | flops 1073741824 | bytes 3145728 | tf_op jit(solution)/shard_map/pallas_call | solution.py:163
  98.0 4.0 %collective-permute-start.18 = (f32[32,1024]{1,0:T(8,128)S(1)}, f32[32,1024]{1,0:T(8,128)S(1)}, u32[]{:S(2)}, u32[]{:S(2)}) collective-permute-start(f32[32,1024]{1,0:T(8,128)S(1)} %get-tuple-element.31), channel_id=1, source_target_pairs={{0,7},{1,0},{2,1},{3,2},{4,3},{5,4},{6,5},{7,6},{8,15},{9,8},{10,9... | collective-permute-start | bytes 393224 | tf_op jit(solution)/shard_map/ppermute | solution.py:31
  102.0 2.3 %collective-permute-done.14 = f32[32,1024]{1,0:T(8,128)S(1)} collective-permute-done((f32[32,1024]{1,0:T(8,128)S(1)}, f32[32,1024]{1,0:T(8,128)S(1)}, u32[]{:S(2)}, u32[]{:S(2)}) %collective-permute-start.14) | collective-permute-done | bytes 131104 | tf_op jit(solution)/shard_map/ppermute | solution.py:31
  104.5 2.8 %collective-permute-start.19 = (f32[64,1024]{1,0:T(8,128)S(1)}, f32[64,1024]{1,0:T(8,128)S(1)}, u32[]{:S(2)}, u32[]{:S(2)}) collective-permute-start(f32[64,1024]{1,0:T(8,128)S(1)} %pad_maximum_fusion.1), channel_id=1, source_target_pairs={{0,7},{1,0},{2,1},{3,2},{4,3},{5,4},{6,5},{7,6},{8,15},{9,8},{10,9... | collective-permute-start | bytes 786440 | tf_op jit(solution)/shard_map/ppermute | solution.py:31
  107.4 4.0 %collective-permute-done.15 = f32[64,1024]{1,0:T(8,128)S(1)} collective-permute-done((f32[64,1024]{1,0:T(8,128)S(1)}, f32[64,1024]{1,0:T(8,128)S(1)}, u32[]{:S(2)}, u32[]{:S(2)}) %collective-permute-start.15) | collective-permute-done | bytes 262176 | tf_op jit(solution)/shard_map/ppermute | solution.py:31
  111.5 6.4 %collective-permute-done.16 = f32[64,1024]{1,0:T(8,128)S(1)} collective-permute-done((f32[64,1024]{1,0:T(8,128)S(1)}, f32[64,1024]{1,0:T(8,128)S(1)}, u32[]{:S(2)}, u32[]{:S(2)}) %collective-permute-start.16) | collective-permute-done | bytes 262176 | tf_op jit(solution)/shard_map/ppermute | solution.py:31
  119.5 3.8 %collective-permute-done.20 = f32[64,1024]{1,0:T(8,128)S(1)} collective-permute-done((f32[64,1024]{1,0:T(8,128)S(1)}, f32[64,1024]{1,0:T(8,128)S(1)}, u32[]{:S(2)}, u32[]{:S(2)}) %collective-permute-start.20) | collective-permute-done | bytes 262176 | tf_op jit(solution)/shard_map/ppermute | solution.py:31
  124.9 6.2 %collective-permute-done.21 = f32[64,1024]{1,0:T(8,128)S(1)} collective-permute-done((f32[64,1024]{1,0:T(8,128)S(1)}, f32[64,1024]{1,0:T(8,128)S(1)}, u32[]{:S(2)}, u32[]{:S(2)}) %collective-permute-start.21) | collective-permute-done | bytes 262176 | tf_op jit(solution)/shard_map/ppermute | solution.py:31
  133.2 19.4 %all-to-all-start.1 = ((f32[256,1,128]{2,1,0:T(1,128)}), f32[256,1,128]{2,1,0:T(1,128)S(1)}, u32[]{:S(2)}, u32[]{:S(2)}) async-start(f32[256,1,128]{2,1,0:T(1,128)} %broadcast_in_dim.3), calls=%async_computation.1 | async-start | bytes 262144 | tf_op jit(solution)/shard_map/all_to_all | solution.py:201
  152.6 2.2 %collective-permute-start.22 = (f32[32,1024]{1,0:T(8,128)S(1)}, f32[32,1024]{1,0:T(8,128)S(1)}, u32[]{:S(2)}, u32[]{:S(2)}) collective-permute-start(f32[32,1024]{1,0:T(8,128)S(1)} %slice_select_fusion), channel_id=1, source_target_pairs={{0,32},{1,33},{2,34},{3,35},{4,36},{5,37},{6,38},{7,39},{8,40},{9,... | collective-permute-start | bytes 393224 | tf_op jit(solution)/shard_map/ppermute | solution.py:31
  154.8 10.8 %all-to-all-done.1 = f32[256,1,128]{2,1,0:T(1,128)S(1)} async-done(((f32[256,1,128]{2,1,0:T(1,128)}), f32[256,1,128]{2,1,0:T(1,128)S(1)}, u32[]{:S(2)}, u32[]{:S(2)}) %all-to-all-start.1) | async-done | bytes 131104 | tf_op jit(solution)/shard_map/all_to_all | solution.py:201
  (76 shorter events, 24.6 us)
Async XLA Ops:
  3.2 4.6 %collective-permute-start = (bf16[128,1024]{1,0:T(8,128)(2,1)}, bf16[128,1024]{1,0:T(8,128)(2,1)S(1)}, u32[]{:S(2)}, u32[]{:S(2)}) collective-permute-start(bf16[128,1024]{1,0:T(8,128)(2,1)} %get-tuple-element.13), channel_id=1, source_target_pairs={{0,32},{1,33},{2,34},{3,35},{4,36},{5,37},{6,38},{7,39},{8,40},{9,... | collective-permute-start | bytes 786440 | tf_op jit(solution)/shard_map/ppermute | solution.py:31
  6.4 6.9 %collective-permute-start.1 = (bf16[128,1024]{1,0:T(8,128)(2,1)}, bf16[128,1024]{1,0:T(8,128)(2,1)S(1)}, u32[]{:S(2)}, u32[]{:S(2)}) collective-permute-start(bf16[128,1024]{1,0:T(8,128)(2,1)} %get-tuple-element.12.refs_0_), channel_id=1, source_target_pairs={{0,64},{1,65},{2,66},{3,67},{4,68},{5,69},{6,70},{7,71},{8,72},{9,... | collective-permute-start | bytes 786440 | tf_op jit(solution)/shard_map/ppermute | solution.py:31
  7.8 5.6 %collective-permute-start.4 = (bf16[128,1024]{1,0:T(8,128)(2,1)S(1)}, bf16[128,1024]{1,0:T(8,128)(2,1)S(1)}, u32[]{:S(2)}, u32[]{:S(2)}) collective-permute-start(bf16[128,1024]{1,0:T(8,128)(2,1)S(1)} %collective-permute-done.refs_1_), channel_id=1, source_target_pairs={{0,192},{1,193},{2,194},{3,195},{4,196},{5,197},{6,198},{7,199},{8... | collective-permute-start | bytes 786440 | tf_op jit(solution)/shard_map/ppermute | solution.py:31
  9.1 10.5 %collective-permute-start.3 = (bf16[128,1024]{1,0:T(8,128)(2,1)}, bf16[128,1024]{1,0:T(8,128)(2,1)S(1)}, u32[]{:S(2)}, u32[]{:S(2)}) collective-permute-start(bf16[128,1024]{1,0:T(8,128)(2,1)} %get-tuple-element.12.refs_0_), channel_id=1, source_target_pairs={{0,192},{1,193},{2,194},{3,195},{4,196},{5,197},{6,198},{7,199},{8... | collective-permute-start | bytes 786440 | tf_op jit(solution)/shard_map/ppermute | solution.py:31
  9.2 10.4 %collective-permute-start.2 = (bf16[128,1024]{1,0:T(8,128)(2,1)S(1)}, bf16[128,1024]{1,0:T(8,128)(2,1)S(1)}, u32[]{:S(2)}, u32[]{:S(2)}) collective-permute-start(bf16[128,1024]{1,0:T(8,128)(2,1)S(1)} %collective-permute-done.refs_1_), channel_id=1, source_target_pairs={{0,64},{1,65},{2,66},{3,67},{4,68},{5,69},{6,70},{7,71},{8,72},{9,... | collective-permute-start | bytes 786440 | tf_op jit(solution)/shard_map/ppermute | solution.py:31
  13.3 6.7 %collective-permute-start.5 = (bf16[128,1024]{1,0:T(8,128)(2,1)S(1)}, bf16[128,1024]{1,0:T(8,128)(2,1)S(1)}, u32[]{:S(2)}, u32[]{:S(2)}) collective-permute-start(bf16[128,1024]{1,0:T(8,128)(2,1)S(1)} %collective-permute-done.1.refs_2_), channel_id=1, source_target_pairs={{0,64},{1,65},{2,66},{3,67},{4,68},{5,69},{6,70},{7,71},{8,72},{9,... | collective-permute-start | bytes 786440 | tf_op jit(solution)/shard_map/ppermute | solution.py:31
  13.4 7.4 %collective-permute-start.6 = (bf16[128,1024]{1,0:T(8,128)(2,1)S(1)}, bf16[128,1024]{1,0:T(8,128)(2,1)}, u32[]{:S(2)}, u32[]{:S(2)}) collective-permute-start(bf16[128,1024]{1,0:T(8,128)(2,1)S(1)} %collective-permute-done.4.refs_5_), channel_id=1, source_target_pairs={{0,192},{1,193},{2,194},{3,195},{4,196},{5,197},{6,198},{7,199},{8... | collective-permute-start | bytes 786440 | tf_op jit(solution)/shard_map/ppermute | solution.py:31
  20.8 56.4 %all-to-all-start = ((bf16[16,512,128]{2,1,0:T(8,128)(2,1)}), bf16[16,512,128]{2,1,0:T(8,128)(2,1)S(1)}, u32[]{:S(2)}, u32[]{:S(2)}) async-start(bf16[16,512,128]{2,1,0:T(8,128)(2,1)} %shard_map.59), calls=%async_computation | async-start | bytes 4194304 | tf_op jit(solution)/shard_map/all_to_all | solution.py:221
  28.8 35.2 %collective-permute-start.10 = (bf16[512,1024]{1,0:T(8,128)(2,1)}, bf16[512,1024]{1,0:T(8,128)(2,1)S(1)}, u32[]{:S(2)}, u32[]{:S(2)}) collective-permute-start(bf16[512,1024]{1,0:T(8,128)(2,1)} %get-tuple-element.16.refs_1_), channel_id=1, source_target_pairs={{0,24},{1,25},{2,26},{3,27},{4,28},{5,29},{6,30},{7,31},{8,0},{9,1... | collective-permute-start | bytes 3145736 | tf_op jit(solution)/shard_map/ppermute | solution.py:31
  31.4 32.6 %collective-permute-start.7 = (bf16[512,1024]{1,0:T(8,128)(2,1)}, bf16[512,1024]{1,0:T(8,128)(2,1)S(1)}, u32[]{:S(2)}, u32[]{:S(2)}) collective-permute-start(bf16[512,1024]{1,0:T(8,128)(2,1)} %get-tuple-element.15.refs_0_), channel_id=1, source_target_pairs={{0,8},{1,9},{2,10},{3,11},{4,12},{5,13},{6,14},{7,15},{8,16},{9,17... | collective-permute-start | bytes 3145736 | tf_op jit(solution)/shard_map/ppermute | solution.py:31
  31.4 43.8 %collective-permute-start.8 = (bf16[512,1024]{1,0:T(8,128)(2,1)}, bf16[512,1024]{1,0:T(8,128)(2,1)S(1)}, u32[]{:S(2)}, u32[]{:S(2)}) collective-permute-start(bf16[512,1024]{1,0:T(8,128)(2,1)} %get-tuple-element.15.refs_0_), channel_id=1, source_target_pairs={{0,24},{1,25},{2,26},{3,27},{4,28},{5,29},{6,30},{7,31},{8,0},{9,1... | collective-permute-start | bytes 3145736 | tf_op jit(solution)/shard_map/ppermute | solution.py:31
  34.1 42.1 %collective-permute-start.9 = (bf16[512,1024]{1,0:T(8,128)(2,1)}, bf16[512,1024]{1,0:T(8,128)(2,1)S(1)}, u32[]{:S(2)}, u32[]{:S(2)}) collective-permute-start(bf16[512,1024]{1,0:T(8,128)(2,1)} %get-tuple-element.16.refs_1_), channel_id=1, source_target_pairs={{0,8},{1,9},{2,10},{3,11},{4,12},{5,13},{6,14},{7,15},{8,16},{9,17... | collective-permute-start | bytes 3145736 | tf_op jit(solution)/shard_map/ppermute | solution.py:31
  77.2 15.5 %collective-permute-start.12 = (bf16[512,1024]{1,0:T(8,128)(2,1)}, bf16[512,1024]{1,0:T(8,128)(2,1)}, u32[]{:S(2)}, u32[]{:S(2)}) collective-permute-start(bf16[512,1024]{1,0:T(8,128)(2,1)} %copy-done.3), channel_id=1, source_target_pairs={{0,8},{1,9},{2,10},{3,11},{4,12},{5,13},{6,14},{7,15},{8,16},{9,17... | collective-permute-start | bytes 3145736 | tf_op jit(solution)/shard_map/ppermute | solution.py:31
  78.6 14.1 %collective-permute-start.13 = (bf16[512,1024]{1,0:T(8,128)(2,1)S(1)}, bf16[512,1024]{1,0:T(8,128)(2,1)}, u32[]{:S(2)}, u32[]{:S(2)}) collective-permute-start(bf16[512,1024]{1,0:T(8,128)(2,1)S(1)} %collective-permute-done.10.refs_5_), channel_id=1, source_target_pairs={{0,24},{1,25},{2,26},{3,27},{4,28},{5,29},{6,30},{7,31},{8,0},{9,1... | collective-permute-start | bytes 3145736 | tf_op jit(solution)/shard_map/ppermute | solution.py:31
  96.3 8.0 %collective-permute-start.14 = (f32[32,1024]{1,0:T(8,128)S(1)}, f32[32,1024]{1,0:T(8,128)S(1)}, u32[]{:S(2)}, u32[]{:S(2)}) collective-permute-start(f32[32,1024]{1,0:T(8,128)S(1)} %get-tuple-element.30), channel_id=1, source_target_pairs={{0,1},{1,2},{2,3},{3,4},{4,5},{5,6},{6,7},{7,0},{8,9},{9,10},{10,1... | collective-permute-start | bytes 393224 | tf_op jit(solution)/shard_map/ppermute | solution.py:31
  98.0 6.3 %collective-permute-start.18 = (f32[32,1024]{1,0:T(8,128)S(1)}, f32[32,1024]{1,0:T(8,128)S(1)}, u32[]{:S(2)}, u32[]{:S(2)}) collective-permute-start(f32[32,1024]{1,0:T(8,128)S(1)} %get-tuple-element.31), channel_id=1, source_target_pairs={{0,7},{1,0},{2,1},{3,2},{4,3},{5,4},{6,5},{7,6},{8,15},{9,8},{10,9... | collective-permute-start | bytes 393224 | tf_op jit(solution)/shard_map/ppermute | solution.py:31
  104.4 6.9 %collective-permute-start.15 = (f32[64,1024]{1,0:T(8,128)S(1)}, f32[64,1024]{1,0:T(8,128)S(1)}, u32[]{:S(2)}, u32[]{:S(2)}) collective-permute-start(f32[64,1024]{1,0:T(8,128)S(1)} %pad_maximum_fusion), channel_id=1, source_target_pairs={{0,1},{1,2},{2,3},{3,4},{4,5},{5,6},{6,7},{7,0},{8,9},{9,10},{10,1... | collective-permute-start | bytes 786440 | tf_op jit(solution)/shard_map/ppermute | solution.py:31
  104.5 7.0 %collective-permute-start.19 = (f32[64,1024]{1,0:T(8,128)S(1)}, f32[64,1024]{1,0:T(8,128)S(1)}, u32[]{:S(2)}, u32[]{:S(2)}) collective-permute-start(f32[64,1024]{1,0:T(8,128)S(1)} %pad_maximum_fusion.1), channel_id=1, source_target_pairs={{0,7},{1,0},{2,1},{3,2},{4,3},{5,4},{6,5},{7,6},{8,15},{9,8},{10,9... | collective-permute-start | bytes 786440 | tf_op jit(solution)/shard_map/ppermute | solution.py:31
  111.4 6.5 %collective-permute-start.16 = (f32[64,1024]{1,0:T(8,128)S(1)}, f32[64,1024]{1,0:T(8,128)S(1)}, u32[]{:S(2)}, u32[]{:S(2)}) collective-permute-start(f32[64,1024]{1,0:T(8,128)S(1)} %dynamic-slice_add_fusion.2), channel_id=1, source_target_pairs={{0,1},{1,2},{2,3},{3,4},{4,5},{5,6},{6,7},{7,0},{8,9},{9,10},{10,1... | collective-permute-start | bytes 786440 | tf_op jit(solution)/shard_map/ppermute | solution.py:31
  118.0 5.3 %collective-permute-start.20 = (f32[64,1024]{1,0:T(8,128)S(1)}, f32[64,1024]{1,0:T(8,128)S(1)}, u32[]{:S(2)}, u32[]{:S(2)}) collective-permute-start(f32[64,1024]{1,0:T(8,128)S(1)} %get-tuple-element.25), channel_id=1, source_target_pairs={{0,7},{1,0},{2,1},{3,2},{4,3},{5,4},{6,5},{7,6},{8,15},{9,8},{10,9... | collective-permute-start | bytes 786440 | tf_op jit(solution)/shard_map/ppermute | solution.py:31
  118.4 6.5 %collective-permute-start.17 = (f32[64,1024]{1,0:T(8,128)S(1)}, f32[64,1024]{1,0:T(8,128)S(1)}, u32[]{:S(2)}, u32[]{:S(2)}) collective-permute-start(f32[64,1024]{1,0:T(8,128)S(1)} %get-tuple-element.24), channel_id=1, source_target_pairs={{0,1},{1,2},{2,3},{3,4},{4,5},{5,6},{6,7},{7,0},{8,9},{9,10},{10,1... | collective-permute-start | bytes 786440 | tf_op jit(solution)/shard_map/ppermute | solution.py:31
  123.3 7.8 %collective-permute-start.21 = (f32[64,1024]{1,0:T(8,128)S(1)}, f32[64,1024]{1,0:T(8,128)S(1)}, u32[]{:S(2)}, u32[]{:S(2)}) collective-permute-start(f32[64,1024]{1,0:T(8,128)S(1)} %dynamic-slice_add_fusion.1), channel_id=1, source_target_pairs={{0,7},{1,0},{2,1},{3,2},{4,3},{5,4},{6,5},{7,6},{8,15},{9,8},{10,9... | collective-permute-start | bytes 786440 | tf_op jit(solution)/shard_map/ppermute | solution.py:31
  133.2 32.4 %all-to-all-start.1 = ((f32[256,1,128]{2,1,0:T(1,128)}), f32[256,1,128]{2,1,0:T(1,128)S(1)}, u32[]{:S(2)}, u32[]{:S(2)}) async-start(f32[256,1,128]{2,1,0:T(1,128)} %broadcast_in_dim.3), calls=%async_computation.1 | async-start | bytes 262144 | tf_op jit(solution)/shard_map/all_to_all | solution.py:201
  152.6 14.6 %collective-permute-start.22 = (f32[32,1024]{1,0:T(8,128)S(1)}, f32[32,1024]{1,0:T(8,128)S(1)}, u32[]{:S(2)}, u32[]{:S(2)}) collective-permute-start(f32[32,1024]{1,0:T(8,128)S(1)} %slice_select_fusion), channel_id=1, source_target_pairs={{0,32},{1,33},{2,34},{3,35},{4,36},{5,37},{6,38},{7,39},{8,40},{9,... | collective-permute-start | bytes 393224 | tf_op jit(solution)/shard_map/ppermute | solution.py:31
  (16 other events, 66.0 us)

commit v6 on v5

--- a/solution.py
+++ b/solution.py
@@ -177,28 +177,27 @@
     )(chosen, *parts, *(() if start is None else (start,)))
 
 
-def reduce_z(partial, z):
+def z_block(partial, z, offset):
     rows = partial.shape[0] // NZ
-    half = rows // 2
-
-    def block(offset):
-        return lax.dynamic_slice_in_dim(partial, lax.rem(z + offset + NZ, NZ) * rows, rows, axis=0)
-
-    far = block(4)
-    up = z_ring(far[:half], 1)
-    down = z_ring(far[half:], -1)
-    near_up, near_down = block(3), block(-3)
-    up = z_ring(jnp.concatenate((near_up[:half] + up, near_up[half:]), axis=0), 1)
-    down = z_ring(jnp.concatenate((near_down[:half], near_down[half:] + down), axis=0), -1)
-    for offset in (2, 1):
-        up = z_ring(block(offset) + up, 1)
-        down = z_ring(block(-offset) + down, -1)
-    return block(0) + up + down
-
-
-def sum_all(value):
-    rows = jnp.broadcast_to(value, (DEVICES, 1, 128))
-    return jnp.sum(lax.all_to_all(rows, AXES, split_axis=0, concat_axis=0, tiled=True)[:, 0, 0])
+    return lax.dynamic_slice_in_dim(partial, lax.rem(z + offset + NZ, NZ) * rows, rows, axis=0)
+
+
+def z_step(partial, z, offset, moving=None):
+    up, down = z_block(partial, z, offset), z_block(partial, z, -offset)
+    half = up.shape[0] // 2
+    if offset == 4:
+        up, down = up[:half], down[half:]
+    elif offset == 3:
+        up = jnp.concatenate((up[:half] + moving[0], up[half:]), axis=0)
+        down = jnp.concatenate((down[:half], down[half:] + moving[1]), axis=0)
+    else:
+        up, down = up + moving[0], down + moving[1]
+    return z_ring(up, 1), z_ring(down, -1)
+
+
+def sum_all(squares):
+    rows = jnp.broadcast_to(squares[None], (DEVICES, 1, 128))
+    return jnp.sum(lax.all_to_all(rows, AXES, split_axis=0, concat_axis=0, tiled=True))
 
 
 def body(activations, key_grads, value_grads, block_lengths):
@@ -239,9 +238,16 @@
     direct = [upper, lower, upper_before, lower_before, upper_after, lower_after]
     weight = multiply(chosen, direct, 0)
     weight = multiply(chosen, opposite, 6, weight)
-    owned = reduce_z(weight, z)
-
-    total = sum_all(jnp.sum(owned * owned))
+    streams = jnp.split(weight, 2, axis=1)
+    moving = [None] * len(streams)
+    for offset in (4, 3, 2, 1):
+        moving = [z_step(part, z, offset, old) for part, old in zip(streams, moving)]
+    owned = jnp.concatenate(
+        [z_block(part, z, 0) + up + down for part, (up, down) in zip(streams, moving)], axis=1
+    )
+
+    squares = jnp.sum((owned * owned).reshape(-1, 128), axis=0)
+    total = sum_all(squares[None])
     half = owned.shape[0] // 2
     kept = jnp.where(is_keys, owned[:half], owned[half:])
     swapped = swap_cores(jnp.where(is_keys, owned[half:], owned[:half]))

time: 168 us -> 163 us (0.970)
  waiting for transfers between devices: 84.3 us -> 74 us
  starting transfers between devices: 55.3 us -> 61.4 us
    ppermute x23 -> x31, waiting for transfers between devices: 73.6 us -> 63.3 us  [send(): return lax.ppermute(value, AXES, pairs(move))]
    ppermute x23 -> x31, starting transfers between devices: 30.8 us -> 39.3 us  [send(): return lax.ppermute(value, AXES, pairs(move))]
    all_to_all x1, starting transfers between devices: 19.4 us -> 16.9 us  [sum_all(): lax.all_to_all(rows, AXES, split_axis=0, concat_axis=0, tiled=True)]
  transfers between devices with their start and end apart: 25 -> 33, of which waited for: 13 -> 15; matrix products, arithmetic and copies ran while one was open for 1% -> 1% of each run, Pallas kernels for 7% -> 7%
where the time goes in v6:
time: 163 us
  waiting for transfers between devices  74 us (45%)
  starting transfers between devices  61.4 us (38%)
  Pallas kernels  17.6 us (11%)
  local copies, waits for them, and re-layouts  5.38 us (3%)
  other arithmetic  2.42 us (1%)
  between operations  1.72 us (1%)
    ppermute x31, waiting for transfers between devices, send(): return lax.ppermute(value, AXES, pairs(move))  63.3 us
    ppermute x31, starting transfers between devices, send(): return lax.ppermute(value, AXES, pairs(move))  39.3 us
    all_to_all x1, starting transfers between devices, sum_all(): lax.all_to_all(rows, AXES, split_axis=0, concat_axis=0, tiled=True)  16.9 us
    all_to_all x1, waiting for transfers between devices, sum_all(): lax.all_to_all(rows, AXES, split_axis=0, concat_axis=0, tiled=True)  10.8 us
    pallas_call x2, Pallas kernels, multiply(): pl.pallas_call(kernel, out_shape=jax.ShapeDtypeStruct((width, n), jnp.flo...  8.53 us
    all_to_all x1, starting transfers between devices, body(): lax.all_to_all(across, ('y', 'x'), split_axis=0, concat_axis=0, tiled=True)  5.13 us
    unnamed x30, local copies, waits for them, and re-layouts  4.3 us
  transfers between devices with their start and end apart: 33, of which 15 were waited for; matrix products, arithmetic and copies ran while one was open for 1% of the time, Pallas kernels for 7%

profile of v6, /device:TPU:1, one launch (start us, length us, event | category | flops | bytes accessed | tf_op | source)
XLA Modules:
  0.0 162.5 jit_solution(10290460152357937206)
XLA Ops:
  3.2 3.2 %collective-permute-start = (bf16[128,1024]{1,0:T(8,128)(2,1)}, bf16[128,1024]{1,0:T(8,128)(2,1)S(1)}, u32[]{:S(2)}, u32[]{:S(2)}) collective-permute-start(bf16[128,1024]{1,0:T(8,128)(2,1)} %get-tuple-element.13), channel_id=1, source_target_pairs={{0,32},{1,33},{2,34},{3,35},{4,36},{5,37},{6,38},{7,39},{8,40},{9,... | collective-permute-start | bytes 786440 | tf_op jit(solution)/shard_map/ppermute | solution.py:31
  10.6 2.8 %collective-permute-done.1.refs_2_ = bf16[128,1024]{1,0:T(8,128)(2,1)S(1)} collective-permute-done((bf16[128,1024]{1,0:T(8,128)(2,1)}, bf16[128,1024]{1,0:T(8,128)(2,1)S(1)}, u32[]{:S(2)}, u32[]{:S(2)}) %collective-permute-start.1) | collective-permute-done | bytes 262176 | tf_op jit(solution)/shard_map/ppermute | solution.py:31
  13.4 2.7 %collective-permute-start.6 = (bf16[128,1024]{1,0:T(8,128)(2,1)S(1)}, bf16[128,1024]{1,0:T(8,128)(2,1)}, u32[]{:S(2)}, u32[]{:S(2)}) collective-permute-start(bf16[128,1024]{1,0:T(8,128)(2,1)S(1)} %collective-permute-done.4.refs_5_), channel_id=1, source_target_pairs={{0,192},{1,193},{2,194},{3,195},{4,196},{5,197},{6,198},{7,199},{8... | collective-permute-start | bytes 786440 | tf_op jit(solution)/shard_map/ppermute | solution.py:31
  17.6 1.9 %shard_map.59 = bf16[16,512,128]{2,1,0:T(8,128)(2,1)} custom-call(bf16[128,8192]{1,0:T(8,128)(2,1)S(1)} %copy-done), custom_call_target="tpu_custom_call" | custom-call | flops 1048576 | bytes 4194304 | tf_op jit(solution)/shard_map/pallas_call | solution.py:112
  20.8 5.1 %all-to-all-start = ((bf16[16,512,128]{2,1,0:T(8,128)(2,1)}), bf16[16,512,128]{2,1,0:T(8,128)(2,1)S(1)}, u32[]{:S(2)}, u32[]{:S(2)}) async-start(bf16[16,512,128]{2,1,0:T(8,128)(2,1)} %shard_map.59), calls=%async_computation | async-start | bytes 4194304 | tf_op jit(solution)/shard_map/all_to_all | solution.py:220
  25.9 2.9 %shard_map.61 = (bf16[512,1024]{1,0:T(8,128)(2,1)}, bf16[512,1024]{1,0:T(8,128)(2,1)}) custom-call(bf16[128,1024]{1,0:T(8,128)(2,1)} %get-tuple-element.12.refs_0_, bf16[128,1024]{1,0:T(8,128)(2,1)} %copy-done.9, bf16[128,1024]{1,0:T(8,128)(2,1)} %copy-done.10, bf16[128,1024]{1,0:T(8,128)(2,1)} %copy-done.13, bf16[128,1024]{1,0:T(8,128)(2,1)} %copy-done.12, ...), custom_call_target="tpu_custom_call" | custom-call | bytes 4194304 | tf_op jit(solution)/shard_map/pallas_call | solution.py:87
  28.9 2.6 %collective-permute-start.10 = (bf16[512,1024]{1,0:T(8,128)(2,1)}, bf16[512,1024]{1,0:T(8,128)(2,1)S(1)}, u32[]{:S(2)}, u32[]{:S(2)}) collective-permute-start(bf16[512,1024]{1,0:T(8,128)(2,1)} %get-tuple-element.16.refs_1_), channel_id=1, source_target_pairs={{0,24},{1,25},{2,26},{3,27},{4,28},{5,29},{6,30},{7,31},{8,0},{9,1... | collective-permute-start | bytes 3145736 | tf_op jit(solution)/shard_map/ppermute | solution.py:31
  31.4 2.7 %collective-permute-start.8 = (bf16[512,1024]{1,0:T(8,128)(2,1)}, bf16[512,1024]{1,0:T(8,128)(2,1)S(1)}, u32[]{:S(2)}, u32[]{:S(2)}) collective-permute-start(bf16[512,1024]{1,0:T(8,128)(2,1)} %get-tuple-element.15.refs_0_), channel_id=1, source_target_pairs={{0,24},{1,25},{2,26},{3,27},{4,28},{5,29},{6,30},{7,31},{8,0},{9,1... | collective-permute-start | bytes 3145736 | tf_op jit(solution)/shard_map/ppermute | solution.py:31
  34.1 29.9 %collective-permute-done.10.refs_5_ = bf16[512,1024]{1,0:T(8,128)(2,1)S(1)} collective-permute-done((bf16[512,1024]{1,0:T(8,128)(2,1)}, bf16[512,1024]{1,0:T(8,128)(2,1)S(1)}, u32[]{:S(2)}, u32[]{:S(2)}) %collective-permute-start.10) | collective-permute-done | bytes 1048608 | tf_op jit(solution)/shard_map/ppermute | solution.py:31
  64.0 11.2 %collective-permute-done.8.refs_4_ = bf16[512,1024]{1,0:T(8,128)(2,1)S(1)} collective-permute-done((bf16[512,1024]{1,0:T(8,128)(2,1)}, bf16[512,1024]{1,0:T(8,128)(2,1)S(1)}, u32[]{:S(2)}, u32[]{:S(2)}) %collective-permute-start.8) | collective-permute-done | bytes 1048608 | tf_op jit(solution)/shard_map/ppermute | solution.py:31
  81.5 2.4 %shard_map.62.chosen_ref = bf16[8,512,512]{2,1,0:T(8,128)(2,1)S(1)} custom-call(s32[16]{0:T(128)S(1)} %stack.79.index_ref, bf16[16,512,128]{2,1,0:T(8,128)(2,1)S(1)} %all-to-all-done.acts_ref, bf16[16,512,128]{2,1,0:T(8,128)(2,1)} %collective-permute-done.11.other_ref), custom_call_target="tpu_custom_call" | custom-call | bytes 8388608 | tf_op jit(solution)/shard_map/pallas_call | solution.py:136
  83.9 4.9 %shard_map.63.refs_2_ = f32[512,1024]{1,0:T(8,128)S(1)} custom-call(bf16[8,512,512]{2,1,0:T(8,128)(2,1)S(1)} %shard_map.62.chosen_ref, bf16[512,1024]{1,0:T(8,128)(2,1)S(1)} %copy-done.1, bf16[512,1024]{1,0:T(8,128)(2,1)S(1)} %copy-done.2, bf16[512,1024]{1,0:T(8,128)(2,1)S(1)} %copy-done.4, bf16[512,1024]{1,0:T(8,128)(2,1)S(1)} %copy-done.8, ...), custom_call_target="tpu_custom_call" | custom-call | flops 3221225472 | bytes 9437184 | tf_op jit(solution)/shard_map/pallas_call | solution.py:163
  88.9 3.8 %collective-permute-done.12.refs_0_ = bf16[512,1024]{1,0:T(8,128)(2,1)} collective-permute-done((bf16[512,1024]{1,0:T(8,128)(2,1)}, bf16[512,1024]{1,0:T(8,128)(2,1)}, u32[]{:S(2)}, u32[]{:S(2)}) %collective-permute-start.12) | collective-permute-done | bytes 1048608 | tf_op jit(solution)/shard_map/ppermute | solution.py:31
  92.7 3.6 %shard_map.64 = f32[512,1024]{1,0:T(8,128)S(1)} custom-call(bf16[8,512,512]{2,1,0:T(8,128)(2,1)S(1)} %shard_map.62.chosen_ref, bf16[512,1024]{1,0:T(8,128)(2,1)} %collective-permute-done.12.refs_0_, bf16[512,1024]{1,0:T(8,128)(2,1)} %collective-permute-done.13.refs_1_, f32[512,1024]{1,0:T(8,128)S(1)} %shard_map.63.refs_2_), custom_call_target="tpu_custom_call" | custom-call | flops 1073741824 | bytes 3145728 | tf_op jit(solution)/shard_map/pallas_call | solution.py:163
  99.8 4.0 %collective-permute-done.14 = f32[32,512]{1,0:T(8,128)S(1)} collective-permute-done((f32[32,512]{1,0:T(8,128)S(1)}, f32[32,512]{1,0:T(8,128)S(1)}, u32[]{:S(2)}, u32[]{:S(2)}) %collective-permute-start.14) | collective-permute-done | bytes 65568 | tf_op jit(solution)/shard_map/ppermute | solution.py:31
  105.5 2.7 %collective-permute-start.26 = (f32[32,512]{1,0:T(8,128)S(1)}, f32[32,512]{1,0:T(8,128)S(1)}, u32[]{:S(2)}, u32[]{:S(2)}) collective-permute-start(f32[32,512]{1,0:T(8,128)S(1)} %get-tuple-element.34), channel_id=1, source_target_pairs={{0,7},{1,0},{2,1},{3,2},{4,3},{5,4},{6,5},{7,6},{8,15},{9,8},{10,9... | collective-permute-start | bytes 196616 | tf_op jit(solution)/shard_map/ppermute | solution.py:31
  108.4 2.7 %collective-permute-start.19 = (f32[64,512]{1,0:T(8,128)S(1)}, f32[64,512]{1,0:T(8,128)S(1)}, u32[]{:S(2)}, u32[]{:S(2)}) collective-permute-start(f32[64,512]{1,0:T(8,128)S(1)} %pad_maximum_fusion.2), channel_id=1, source_target_pairs={{0,7},{1,0},{2,1},{3,2},{4,3},{5,4},{6,5},{7,6},{8,15},{9,8},{10,9... | collective-permute-start | bytes 393224 | tf_op jit(solution)/shard_map/ppermute | solution.py:31
  111.1 2.4 %collective-permute-start.27 = (f32[64,512]{1,0:T(8,128)S(1)}, f32[64,512]{1,0:T(8,128)S(1)}, u32[]{:S(2)}, u32[]{:S(2)}) collective-permute-start(f32[64,512]{1,0:T(8,128)S(1)} %pad_maximum_fusion.4), channel_id=1, source_target_pairs={{0,7},{1,0},{2,1},{3,2},{4,3},{5,4},{6,5},{7,6},{8,15},{9,8},{10,9... | collective-permute-start | bytes 393224 | tf_op jit(solution)/shard_map/ppermute | solution.py:31
  114.9 3.8 %collective-permute-done.16 = f32[64,512]{1,0:T(8,128)S(1)} collective-permute-done((f32[64,512]{1,0:T(8,128)S(1)}, f32[64,512]{1,0:T(8,128)S(1)}, u32[]{:S(2)}, u32[]{:S(2)}) %collective-permute-start.16) | collective-permute-done | bytes 131104 | tf_op jit(solution)/shard_map/ppermute | solution.py:31
  124.8 2.3 %collective-permute-start.29 = (f32[64,512]{1,0:T(8,128)S(1)}, f32[64,512]{1,0:T(8,128)S(1)}, u32[]{:S(2)}, u32[]{:S(2)}) collective-permute-start(f32[64,512]{1,0:T(8,128)S(1)} %dynamic-slice_add_fusion.1), channel_id=1, source_target_pairs={{0,7},{1,0},{2,1},{3,2},{4,3},{5,4},{6,5},{7,6},{8,15},{9,8},{10,9... | collective-permute-start | bytes 393224 | tf_op jit(solution)/shard_map/ppermute | solution.py:31
  127.6 2.0 %collective-permute-done.29 = f32[64,512]{1,0:T(8,128)S(1)} collective-permute-done((f32[64,512]{1,0:T(8,128)S(1)}, f32[64,512]{1,0:T(8,128)S(1)}, u32[]{:S(2)}, u32[]{:S(2)}) %collective-permute-start.29) | collective-permute-done | bytes 131104 | tf_op jit(solution)/shard_map/ppermute | solution.py:31
  130.5 16.9 %all-to-all-start.1 = ((f32[256,1,128]{2,1,0:T(1,128)}), f32[256,1,128]{2,1,0:T(1,128)S(1)}, u32[]{:S(2)}, u32[]{:S(2)}) async-start(f32[256,1,128]{2,1,0:T(1,128)} %broadcast_in_dim.2), calls=%async_computation.1 | async-start | bytes 262144 | tf_op jit(solution)/shard_map/all_to_all | solution.py:200
  147.5 2.2 %collective-permute-start.30 = (f32[32,1024]{1,0:T(8,128)S(1)}, f32[32,1024]{1,0:T(8,128)S(1)}, u32[]{:S(2)}, u32[]{:S(2)}) collective-permute-start(f32[32,1024]{1,0:T(8,128)S(1)} %broadcast_select_fusion), channel_id=1, source_target_pairs={{0,32},{1,33},{2,34},{3,35},{4,36},{5,37},{6,38},{7,39},{8,40},{9,... | collective-permute-start | bytes 393224 | tf_op jit(solution)/shard_map/ppermute | solution.py:31
  149.7 10.8 %all-to-all-done.1 = f32[256,1,128]{2,1,0:T(1,128)S(1)} async-done(((f32[256,1,128]{2,1,0:T(1,128)}), f32[256,1,128]{2,1,0:T(1,128)S(1)}, u32[]{:S(2)}, u32[]{:S(2)}) %all-to-all-start.1) | async-done | bytes 131104 | tf_op jit(solution)/shard_map/all_to_all | solution.py:200
  (106 shorter events, 31.2 us)
Async XLA Ops:
  6.4 6.9 %collective-permute-start.1 = (bf16[128,1024]{1,0:T(8,128)(2,1)}, bf16[128,1024]{1,0:T(8,128)(2,1)S(1)}, u32[]{:S(2)}, u32[]{:S(2)}) collective-permute-start(bf16[128,1024]{1,0:T(8,128)(2,1)} %get-tuple-element.12.refs_0_), channel_id=1, source_target_pairs={{0,64},{1,65},{2,66},{3,67},{4,68},{5,69},{6,70},{7,71},{8,72},{9,... | collective-permute-start | bytes 786440 | tf_op jit(solution)/shard_map/ppermute | solution.py:31
  7.8 5.6 %collective-permute-start.4 = (bf16[128,1024]{1,0:T(8,128)(2,1)S(1)}, bf16[128,1024]{1,0:T(8,128)(2,1)S(1)}, u32[]{:S(2)}, u32[]{:S(2)}) collective-permute-start(bf16[128,1024]{1,0:T(8,128)(2,1)S(1)} %collective-permute-done.refs_1_), channel_id=1, source_target_pairs={{0,192},{1,193},{2,194},{3,195},{4,196},{5,197},{6,198},{7,199},{8... | collective-permute-start | bytes 786440 | tf_op jit(solution)/shard_map/ppermute | solution.py:31
  9.1 10.5 %collective-permute-start.3 = (bf16[128,1024]{1,0:T(8,128)(2,1)}, bf16[128,1024]{1,0:T(8,128)(2,1)S(1)}, u32[]{:S(2)}, u32[]{:S(2)}) collective-permute-start(bf16[128,1024]{1,0:T(8,128)(2,1)} %get-tuple-element.12.refs_0_), channel_id=1, source_target_pairs={{0,192},{1,193},{2,194},{3,195},{4,196},{5,197},{6,198},{7,199},{8... | collective-permute-start | bytes 786440 | tf_op jit(solution)/shard_map/ppermute | solution.py:31
  9.2 10.3 %collective-permute-start.2 = (bf16[128,1024]{1,0:T(8,128)(2,1)S(1)}, bf16[128,1024]{1,0:T(8,128)(2,1)S(1)}, u32[]{:S(2)}, u32[]{:S(2)}) collective-permute-start(bf16[128,1024]{1,0:T(8,128)(2,1)S(1)} %collective-permute-done.refs_1_), channel_id=1, source_target_pairs={{0,64},{1,65},{2,66},{3,67},{4,68},{5,69},{6,70},{7,71},{8,72},{9,... | collective-permute-start | bytes 786440 | tf_op jit(solution)/shard_map/ppermute | solution.py:31
  13.4 6.7 %collective-permute-start.5 = (bf16[128,1024]{1,0:T(8,128)(2,1)S(1)}, bf16[128,1024]{1,0:T(8,128)(2,1)S(1)}, u32[]{:S(2)}, u32[]{:S(2)}) collective-permute-start(bf16[128,1024]{1,0:T(8,128)(2,1)S(1)} %collective-permute-done.1.refs_2_), channel_id=1, source_target_pairs={{0,64},{1,65},{2,66},{3,67},{4,68},{5,69},{6,70},{7,71},{8,72},{9,... | collective-permute-start | bytes 786440 | tf_op jit(solution)/shard_map/ppermute | solution.py:31
  13.4 7.4 %collective-permute-start.6 = (bf16[128,1024]{1,0:T(8,128)(2,1)S(1)}, bf16[128,1024]{1,0:T(8,128)(2,1)}, u32[]{:S(2)}, u32[]{:S(2)}) collective-permute-start(bf16[128,1024]{1,0:T(8,128)(2,1)S(1)} %collective-permute-done.4.refs_5_), channel_id=1, source_target_pairs={{0,192},{1,193},{2,194},{3,195},{4,196},{5,197},{6,198},{7,199},{8... | collective-permute-start | bytes 786440 | tf_op jit(solution)/shard_map/ppermute | solution.py:31
  20.8 56.4 %all-to-all-start = ((bf16[16,512,128]{2,1,0:T(8,128)(2,1)}), bf16[16,512,128]{2,1,0:T(8,128)(2,1)S(1)}, u32[]{:S(2)}, u32[]{:S(2)}) async-start(bf16[16,512,128]{2,1,0:T(8,128)(2,1)} %shard_map.59), calls=%async_computation | async-start | bytes 4194304 | tf_op jit(solution)/shard_map/all_to_all | solution.py:220
  28.9 35.1 %collective-permute-start.10 = (bf16[512,1024]{1,0:T(8,128)(2,1)}, bf16[512,1024]{1,0:T(8,128)(2,1)S(1)}, u32[]{:S(2)}, u32[]{:S(2)}) collective-permute-start(bf16[512,1024]{1,0:T(8,128)(2,1)} %get-tuple-element.16.refs_1_), channel_id=1, source_target_pairs={{0,24},{1,25},{2,26},{3,27},{4,28},{5,29},{6,30},{7,31},{8,0},{9,1... | collective-permute-start | bytes 3145736 | tf_op jit(solution)/shard_map/ppermute | solution.py:31
  31.4 32.6 %collective-permute-start.7 = (bf16[512,1024]{1,0:T(8,128)(2,1)}, bf16[512,1024]{1,0:T(8,128)(2,1)S(1)}, u32[]{:S(2)}, u32[]{:S(2)}) collective-permute-start(bf16[512,1024]{1,0:T(8,128)(2,1)} %get-tuple-element.15.refs_0_), channel_id=1, source_target_pairs={{0,8},{1,9},{2,10},{3,11},{4,12},{5,13},{6,14},{7,15},{8,16},{9,17... | collective-permute-start | bytes 3145736 | tf_op jit(solution)/shard_map/ppermute | solution.py:31
  31.4 43.8 %collective-permute-start.8 = (bf16[512,1024]{1,0:T(8,128)(2,1)}, bf16[512,1024]{1,0:T(8,128)(2,1)S(1)}, u32[]{:S(2)}, u32[]{:S(2)}) collective-permute-start(bf16[512,1024]{1,0:T(8,128)(2,1)} %get-tuple-element.15.refs_0_), channel_id=1, source_target_pairs={{0,24},{1,25},{2,26},{3,27},{4,28},{5,29},{6,30},{7,31},{8,0},{9,1... | collective-permute-start | bytes 3145736 | tf_op jit(solution)/shard_map/ppermute | solution.py:31
  34.1 42.1 %collective-permute-start.9 = (bf16[512,1024]{1,0:T(8,128)(2,1)}, bf16[512,1024]{1,0:T(8,128)(2,1)S(1)}, u32[]{:S(2)}, u32[]{:S(2)}) collective-permute-start(bf16[512,1024]{1,0:T(8,128)(2,1)} %get-tuple-element.16.refs_1_), channel_id=1, source_target_pairs={{0,8},{1,9},{2,10},{3,11},{4,12},{5,13},{6,14},{7,15},{8,16},{9,17... | collective-permute-start | bytes 3145736 | tf_op jit(solution)/shard_map/ppermute | solution.py:31
  77.2 15.5 %collective-permute-start.12 = (bf16[512,1024]{1,0:T(8,128)(2,1)}, bf16[512,1024]{1,0:T(8,128)(2,1)}, u32[]{:S(2)}, u32[]{:S(2)}) collective-permute-start(bf16[512,1024]{1,0:T(8,128)(2,1)} %copy-done.3), channel_id=1, source_target_pairs={{0,8},{1,9},{2,10},{3,11},{4,12},{5,13},{6,14},{7,15},{8,16},{9,17... | collective-permute-start | bytes 3145736 | tf_op jit(solution)/shard_map/ppermute | solution.py:31
  78.6 14.1 %collective-permute-start.13 = (bf16[512,1024]{1,0:T(8,128)(2,1)S(1)}, bf16[512,1024]{1,0:T(8,128)(2,1)}, u32[]{:S(2)}, u32[]{:S(2)}) collective-permute-start(bf16[512,1024]{1,0:T(8,128)(2,1)S(1)} %collective-permute-done.10.refs_5_), channel_id=1, source_target_pairs={{0,24},{1,25},{2,26},{3,27},{4,28},{5,29},{6,30},{7,31},{8,0},{9,1... | collective-permute-start | bytes 3145736 | tf_op jit(solution)/shard_map/ppermute | solution.py:31
  96.5 7.3 %collective-permute-start.14 = (f32[32,512]{1,0:T(8,128)S(1)}, f32[32,512]{1,0:T(8,128)S(1)}, u32[]{:S(2)}, u32[]{:S(2)}) collective-permute-start(f32[32,512]{1,0:T(8,128)S(1)} %constant_dynamic-slice_fusion.6), channel_id=1, source_target_pairs={{0,1},{1,2},{2,3},{3,4},{4,5},{5,6},{6,7},{7,0},{8,9},{9,10},{10,1... | collective-permute-start | bytes 196616 | tf_op jit(solution)/shard_map/ppermute | solution.py:31
  98.2 7.3 %collective-permute-start.22 = (f32[32,512]{1,0:T(8,128)S(1)}, f32[32,512]{1,0:T(8,128)S(1)}, u32[]{:S(2)}, u32[]{:S(2)}) collective-permute-start(f32[32,512]{1,0:T(8,128)S(1)} %constant_dynamic-slice_fusion.3), channel_id=1, source_target_pairs={{0,1},{1,2},{2,3},{3,4},{4,5},{5,6},{6,7},{7,0},{8,9},{9,10},{10,1... | collective-permute-start | bytes 196616 | tf_op jit(solution)/shard_map/ppermute | solution.py:31
  105.4 8.2 %collective-permute-start.15 = (f32[64,512]{1,0:T(8,128)S(1)}, f32[64,512]{1,0:T(8,128)S(1)}, u32[]{:S(2)}, u32[]{:S(2)}) collective-permute-start(f32[64,512]{1,0:T(8,128)S(1)} %pad_maximum_fusion.1), channel_id=1, source_target_pairs={{0,1},{1,2},{2,3},{3,4},{4,5},{5,6},{6,7},{7,0},{8,9},{9,10},{10,1... | collective-permute-start | bytes 393224 | tf_op jit(solution)/shard_map/ppermute | solution.py:31
  105.5 5.6 %collective-permute-start.26 = (f32[32,512]{1,0:T(8,128)S(1)}, f32[32,512]{1,0:T(8,128)S(1)}, u32[]{:S(2)}, u32[]{:S(2)}) collective-permute-start(f32[32,512]{1,0:T(8,128)S(1)} %get-tuple-element.34), channel_id=1, source_target_pairs={{0,7},{1,0},{2,1},{3,2},{4,3},{5,4},{6,5},{7,6},{8,15},{9,8},{10,9... | collective-permute-start | bytes 196616 | tf_op jit(solution)/shard_map/ppermute | solution.py:31
  108.2 6.5 %collective-permute-start.23 = (f32[64,512]{1,0:T(8,128)S(1)}, f32[64,512]{1,0:T(8,128)S(1)}, u32[]{:S(2)}, u32[]{:S(2)}) collective-permute-start(f32[64,512]{1,0:T(8,128)S(1)} %pad_maximum_fusion.3), channel_id=1, source_target_pairs={{0,1},{1,2},{2,3},{3,4},{4,5},{5,6},{6,7},{7,0},{8,9},{9,10},{10,1... | collective-permute-start | bytes 393224 | tf_op jit(solution)/shard_map/ppermute | solution.py:31
  108.4 6.5 %collective-permute-start.19 = (f32[64,512]{1,0:T(8,128)S(1)}, f32[64,512]{1,0:T(8,128)S(1)}, u32[]{:S(2)}, u32[]{:S(2)}) collective-permute-start(f32[64,512]{1,0:T(8,128)S(1)} %pad_maximum_fusion.2), channel_id=1, source_target_pairs={{0,7},{1,0},{2,1},{3,2},{4,3},{5,4},{6,5},{7,6},{8,15},{9,8},{10,9... | collective-permute-start | bytes 393224 | tf_op jit(solution)/shard_map/ppermute | solution.py:31
  111.1 9.1 %collective-permute-start.27 = (f32[64,512]{1,0:T(8,128)S(1)}, f32[64,512]{1,0:T(8,128)S(1)}, u32[]{:S(2)}, u32[]{:S(2)}) collective-permute-start(f32[64,512]{1,0:T(8,128)S(1)} %pad_maximum_fusion.4), channel_id=1, source_target_pairs={{0,7},{1,0},{2,1},{3,2},{4,3},{5,4},{6,5},{7,6},{8,15},{9,8},{10,9... | collective-permute-start | bytes 393224 | tf_op jit(solution)/shard_map/ppermute | solution.py:31
  118.8 8.2 %collective-permute-start.17 = (f32[64,512]{1,0:T(8,128)S(1)}, f32[64,512]{1,0:T(8,128)S(1)}, u32[]{:S(2)}, u32[]{:S(2)}) collective-permute-start(f32[64,512]{1,0:T(8,128)S(1)} %get-tuple-element.24), channel_id=1, source_target_pairs={{0,1},{1,2},{2,3},{3,4},{4,5},{5,6},{6,7},{7,0},{8,9},{9,10},{10,1... | collective-permute-start | bytes 393224 | tf_op jit(solution)/shard_map/ppermute | solution.py:31
  121.9 5.7 %collective-permute-start.25 = (f32[64,512]{1,0:T(8,128)S(1)}, f32[64,512]{1,0:T(8,128)S(1)}, u32[]{:S(2)}, u32[]{:S(2)}) collective-permute-start(f32[64,512]{1,0:T(8,128)S(1)} %get-tuple-element.30), channel_id=1, source_target_pairs={{0,1},{1,2},{2,3},{3,4},{4,5},{5,6},{6,7},{7,0},{8,9},{9,10},{10,1... | collective-permute-start | bytes 393224 | tf_op jit(solution)/shard_map/ppermute | solution.py:31
  130.5 30.0 %all-to-all-start.1 = ((f32[256,1,128]{2,1,0:T(1,128)}), f32[256,1,128]{2,1,0:T(1,128)S(1)}, u32[]{:S(2)}, u32[]{:S(2)}) async-start(f32[256,1,128]{2,1,0:T(1,128)} %broadcast_in_dim.2), calls=%async_computation.1 | async-start | bytes 262144 | tf_op jit(solution)/shard_map/all_to_all | solution.py:200
  147.5 14.3 %collective-permute-start.30 = (f32[32,1024]{1,0:T(8,128)S(1)}, f32[32,1024]{1,0:T(8,128)S(1)}, u32[]{:S(2)}, u32[]{:S(2)}) collective-permute-start(f32[32,1024]{1,0:T(8,128)S(1)} %broadcast_select_fusion), channel_id=1, source_target_pairs={{0,32},{1,33},{2,34},{3,35},{4,36},{5,37},{6,38},{7,39},{8,40},{9,... | collective-permute-start | bytes 393224 | tf_op jit(solution)/shard_map/ppermute | solution.py:31
  (24 other events, 103.7 us)

commit v7 on v6

--- a/solution.py
+++ b/solution.py
@@ -52,9 +52,11 @@
 ANY = pl.BlockSpec(memory_space=pl.ANY)
 
 
-def mask_kernel(place_ref, lengths_ref, keys_ref, values_ref, mine_ref, theirs_ref):
-    is_keys = place_ref[0] == 0
-    limit = lengths_ref[place_ref[1]] - place_ref[2]
+def mask_kernel(lengths_ref, keys_ref, values_ref, mine_ref, theirs_ref):
+    x, c, y, z = (lax.axis_index(axis) for axis in AXES)
+    is_keys = c == 0
+    position = (((x * NC + c) * NY + y) * NZ + z) * keys_ref.shape[0]
+    limit = lengths_ref[position // CH] - position % CH
     keys, values = keys_ref[...], values_ref[...]
     rows = lax.broadcasted_iota(jnp.int32, keys.shape, 0)
     zero = jnp.zeros_like(keys)
@@ -64,31 +66,33 @@
     theirs_ref[...] = jnp.where(is_keys, values, keys)
 
 
-def mask(place, block_lengths, key_grads, value_grads):
+def mask(block_lengths, key_grads, value_grads):
     return pl.pallas_call(
         mask_kernel,
         out_shape=[jax.ShapeDtypeStruct(key_grads.shape, key_grads.dtype)] * 2,
-        in_specs=[SMEM, SMEM, VMEM, VMEM],
+        in_specs=[SMEM, VMEM, VMEM],
         out_specs=[VMEM, VMEM],
         cost_estimate=pl.CostEstimate(
             flops=key_grads.size, bytes_accessed=8 * key_grads.size, transcendentals=0
         ),
-    )(place, block_lengths, key_grads, value_grads)
+    )(block_lengths, key_grads, value_grads)
 
 
 def stack(pieces):
     tok_count, width = pieces[0].shape
-    half = len(pieces) // 2
+    half, n = len(pieces) // 2, width // 2
 
     def kernel(*refs):
-        for i, piece_ref in enumerate(refs[:-2]):
-            refs[-2 + i // half][pl.ds(i % half * tok_count, tok_count), :] = piece_ref[...]
+        for i, piece_ref in enumerate(refs[:-4]):
+            place = pl.ds(i % half * tok_count, tok_count)
+            refs[-4 + i // half][place, :] = piece_ref[:, pl.ds(0, n)]
+            refs[-2 + i // half][place, :] = piece_ref[:, pl.ds(n, n)]
 
     return pl.pallas_call(
         kernel,
-        out_shape=[jax.ShapeDtypeStruct((half * tok_count, width), pieces[0].dtype)] * 2,
+        out_shape=[jax.ShapeDtypeStruct((half * tok_count, n), pieces[0].dtype)] * 4,
         in_specs=[VMEM] * len(pieces),
-        out_specs=[VMEM] * 2,
+        out_specs=[VMEM] * 4,
         cost_estimate=pl.CostEstimate(
             flops=0, bytes_accessed=8 * half * tok_count * width, transcendentals=0
         ),
@@ -159,15 +163,14 @@
             total = product if total is None else total + product
         refs[-1][...] = total
 
-    columns = pl.BlockSpec((width, COLUMNS), lambda i: (0, i))
     return pl.pallas_call(
         kernel,
         out_shape=jax.ShapeDtypeStruct((width, n), jnp.float32),
         grid=(n // COLUMNS,),
         in_specs=[pl.BlockSpec((count, width, depth), lambda i: (first // count, 0, 0))]
         + [pl.BlockSpec((depth, COLUMNS), lambda i: (0, i))] * count
-        + ([] if start is None else [columns]),
-        out_specs=columns,
+        + ([] if start is None else [pl.BlockSpec((width, COLUMNS), lambda i: (0, i))]),
+        out_specs=pl.BlockSpec((width, COLUMNS), lambda i: (0, i)),
         compiler_params=pltpu.CompilerParams(vmem_limit_bytes=32 * 1024 * 1024),
         cost_estimate=pl.CostEstimate(
             flops=2 * width * n * depth * count,
@@ -192,7 +195,7 @@
         down = jnp.concatenate((down[:half], down[half:] + moving[1]), axis=0)
     else:
         up, down = up + moving[0], down + moving[1]
-    return z_ring(up, 1), z_ring(down, -1)
+    return lax.optimization_barrier((z_ring(up, 1), z_ring(down, -1)))
 
 
 def sum_all(squares):
@@ -205,11 +208,9 @@
     head_width = key_grads.shape[1]
     x, c, y, z = (lax.axis_index(axis) for axis in AXES)
     is_keys = c == 0
-    position = (((x * NC + c) * NY + y) * NZ + z) * tok_count
     clip_norm = math.sqrt(2.0 * model_width * head_width)
 
-    place = jnp.stack((c, lax.div(position, CH), lax.rem(position, CH))).astype(jnp.int32)
-    mine, theirs = mask(place, block_lengths, key_grads, value_grads)
+    mine, theirs = mask(block_lengths, key_grads, value_grads)
     received = swap_cores(theirs)
     mine_before, mine_after = first_ring(mine, 1), first_ring(mine, -1)
     received_before, received_after = first_ring(received, 1), first_ring(received, -1)
@@ -227,18 +228,16 @@
             index.append(jnp.where(is_keys, at2 * NX + at1, at1 * NX + at2))
     index = jnp.stack(index).astype(jnp.int32)
 
-    upper, lower = stack(pieces)
-    upper_before, upper_after = second_ring(upper, 1), second_ring(upper, -1)
-    lower_before, lower_after = second_ring(lower, 1), second_ring(lower, -1)
-    acts, upper_before, upper_after, lower_before, lower_after = lax.optimization_barrier(
-        (acts, upper_before, upper_after, lower_before, lower_after)
-    )
+    stacked = stack(pieces)
+    direct = [second_ring(part, step) for part in stacked for step in (1, -1)]
+    acts, *direct = lax.optimization_barrier((acts, *direct))
     chosen = choose(index, acts, swap_cores(acts))
-    opposite = [second_ring(upper_before, 1), second_ring(lower_after, -1)]
-    direct = [upper, lower, upper_before, lower_before, upper_after, lower_after]
-    weight = multiply(chosen, direct, 0)
-    weight = multiply(chosen, opposite, 6, weight)
-    streams = jnp.split(weight, 2, axis=1)
+    streams = []
+    for (upper, lower), sent in ((stacked[:2], direct[:4]), (stacked[2:], direct[4:])):
+        opposite = [second_ring(sent[0], 1), second_ring(sent[3], -1)]
+        near = [upper, lower, sent[0], sent[2], sent[1], sent[3]]
+        streams.append(multiply(chosen, opposite, 6, multiply(chosen, near, 0)))
+
     moving = [None] * len(streams)
     for offset in (4, 3, 2, 1):
         moving = [z_step(part, z, offset, old) for part, old in zip(streams, moving)]

time: 163 us -> 157 us (0.963)
  waiting for transfers between devices: 74 us -> 54.3 us
  starting transfers between devices: 61.4 us -> 74.3 us
  local copies, waits for them, and re-layouts: 5.38 us -> 7.15 us
    ppermute x31 -> x37, waiting for transfers between devices: 63.3 us -> 43.5 us  [send(): return lax.ppermute(value, AXES, pairs(move))]
    ppermute x31 -> x37, starting transfers between devices: 39.3 us -> 52.4 us  [send(): return lax.ppermute(value, AXES, pairs(move))]
    unnamed x30 -> x50, local copies, waits for them, and re-layouts: 4.3 us -> 6.25 us
    pallas_call x2 -> x4, Pallas kernels: 8.53 us -> 8.63 us  [multiply(): pl.pallas_call(kernel, out_shape=jax.ShapeDtypeStruct((width, n), jnp.flo...]
  transfers between devices with their start and end apart: 33 -> 39, of which waited for: 15 -> 12; matrix products, arithmetic and copies ran while one was open for 1% -> 1% of each run, Pallas kernels for 7% -> 10%
where the time goes in v7:
time: 157 us
  starting transfers between devices  74.3 us (47%)
  waiting for transfers between devices  54.3 us (35%)
  Pallas kernels  17.8 us (11%)
  local copies, waits for them, and re-layouts  7.15 us (5%)
  between operations  1.8 us (1%)
  other arithmetic  1.75 us (1%)
    ppermute x37, starting transfers between devices, send(): return lax.ppermute(value, AXES, pairs(move))  52.4 us
    ppermute x37, waiting for transfers between devices, send(): return lax.ppermute(value, AXES, pairs(move))  43.5 us
    all_to_all x1, starting transfers between devices, sum_all(): lax.all_to_all(rows, AXES, split_axis=0, concat_axis=0, tiled=True)  17.4 us
    all_to_all x1, waiting for transfers between devices, sum_all(): lax.all_to_all(rows, AXES, split_axis=0, concat_axis=0, tiled=True)  10.8 us
    pallas_call x4, Pallas kernels, multiply(): pl.pallas_call(kernel, out_shape=jax.ShapeDtypeStruct((width, n), jnp.flo...  8.63 us
    unnamed x50, local copies, waits for them, and re-layouts  6.25 us
    all_to_all x1, starting transfers between devices, body(): lax.all_to_all(across, ('y', 'x'), split_axis=0, concat_axis=0, tiled=True)  4.43 us
  transfers between devices with their start and end apart: 39, of which 12 were waited for; matrix products, arithmetic and copies ran while one was open for 1% of the time, Pallas kernels for 10%

profile of v7, /device:TPU:1, one launch (start us, length us, event | category | flops | bytes accessed | tf_op | source)
XLA Modules:
  0.0 157.0 jit_solution(10285693891110471779)
XLA Ops:
  2.5 3.2 %collective-permute-start = (bf16[128,1024]{1,0:T(8,128)(2,1)}, bf16[128,1024]{1,0:T(8,128)(2,1)S(1)}, u32[]{:S(2)}, u32[]{:S(2)}) collective-permute-start(bf16[128,1024]{1,0:T(8,128)(2,1)} %get-tuple-element.35), channel_id=1, source_target_pairs={{0,32},{1,33},{2,34},{3,35},{4,36},{5,37},{6,38},{7,39},{8,40},{9,... | collective-permute-start | bytes 786440 | tf_op jit(solution)/shard_map/ppermute | solution.py:31
  9.9 2.8 %collective-permute-done.1.refs_2_ = bf16[128,1024]{1,0:T(8,128)(2,1)S(1)} collective-permute-done((bf16[128,1024]{1,0:T(8,128)(2,1)}, bf16[128,1024]{1,0:T(8,128)(2,1)S(1)}, u32[]{:S(2)}, u32[]{:S(2)}) %collective-permute-start.1) | collective-permute-done | bytes 262176 | tf_op jit(solution)/shard_map/ppermute | solution.py:31
  12.7 2.7 %collective-permute-start.6 = (bf16[128,1024]{1,0:T(8,128)(2,1)S(1)}, bf16[128,1024]{1,0:T(8,128)(2,1)}, u32[]{:S(2)}, u32[]{:S(2)}) collective-permute-start(bf16[128,1024]{1,0:T(8,128)(2,1)S(1)} %collective-permute-done.4.refs_5_), channel_id=1, source_target_pairs={{0,192},{1,193},{2,194},{3,195},{4,196},{5,197},{6,198},{7,199},{8... | collective-permute-start | bytes 786440 | tf_op jit(solution)/shard_map/ppermute | solution.py:31
  20.9 4.4 %all-to-all-start = ((bf16[16,512,128]{2,1,0:T(8,128)(2,1)}), bf16[16,512,128]{2,1,0:T(8,128)(2,1)S(1)}, u32[]{:S(2)}, u32[]{:S(2)}) async-start(bf16[16,512,128]{2,1,0:T(8,128)(2,1)} %shard_map.59), calls=%async_computation | async-start | bytes 4194304 | tf_op jit(solution)/shard_map/all_to_all | solution.py:221
  25.3 2.9 %shard_map.61 = (bf16[512,512]{1,0:T(8,128)(2,1)}, bf16[512,512]{1,0:T(8,128)(2,1)}, bf16[512,512]{1,0:T(8,128)(2,1)}, bf16[512,512]{1,0:T(8,128)(2,1)}) custom-call(bf16[128,1024]{1,0:T(8,128)(2,1)} %get-tuple-element.34.refs_0_, bf16[128,1024]{1,0:T(8,128)(2,1)} %copy-done.19, bf16[128,1024]{1,0:T(8,128)(2,1)} %copy-done.20, bf16[128,1024]{1,0:T(8,128)(2,1)} %copy-done.23, ...), custom_call_target="tpu_custom_call" | custom-call | bytes 4194304 | tf_op jit(solution)/shard_map/pallas_call | solution.py:91
  28.2 2.6 %collective-permute-start.10 = (bf16[512,512]{1,0:T(8,128)(2,1)}, bf16[512,512]{1,0:T(8,128)(2,1)S(1)}, u32[]{:S(2)}, u32[]{:S(2)}) collective-permute-start(bf16[512,512]{1,0:T(8,128)(2,1)} %get-tuple-element.38.refs_1_), channel_id=1, source_target_pairs={{0,24},{1,25},{2,26},{3,27},{4,28},{5,29},{6,30},{7,31},{8,0},{9,1... | collective-permute-start | bytes 1572872 | tf_op jit(solution)/shard_map/ppermute | solution.py:31
  30.7 2.7 %collective-permute-start.12 = (bf16[512,512]{1,0:T(8,128)(2,1)}, bf16[512,512]{1,0:T(8,128)(2,1)S(1)}, u32[]{:S(2)}, u32[]{:S(2)}) collective-permute-start(bf16[512,512]{1,0:T(8,128)(2,1)} %get-tuple-element.39.refs_0_), channel_id=1, source_target_pairs={{0,24},{1,25},{2,26},{3,27},{4,28},{5,29},{6,30},{7,31},{8,0},{9,1... | collective-permute-start | bytes 1572872 | tf_op jit(solution)/shard_map/ppermute | solution.py:31
  33.4 2.7 %collective-permute-start.14 = (bf16[512,512]{1,0:T(8,128)(2,1)}, bf16[512,512]{1,0:T(8,128)(2,1)S(1)}, u32[]{:S(2)}, u32[]{:S(2)}) collective-permute-start(bf16[512,512]{1,0:T(8,128)(2,1)} %get-tuple-element.40.refs_1_), channel_id=1, source_target_pairs={{0,24},{1,25},{2,26},{3,27},{4,28},{5,29},{6,30},{7,31},{8,0},{9,1... | collective-permute-start | bytes 1572872 | tf_op jit(solution)/shard_map/ppermute | solution.py:31
  36.1 21.7 %collective-permute-done.10.refs_5_ = bf16[512,512]{1,0:T(8,128)(2,1)S(1)} collective-permute-done((bf16[512,512]{1,0:T(8,128)(2,1)}, bf16[512,512]{1,0:T(8,128)(2,1)S(1)}, u32[]{:S(2)}, u32[]{:S(2)}) %collective-permute-start.10) | collective-permute-done | bytes 524320 | tf_op jit(solution)/shard_map/ppermute | solution.py:31
  60.5 2.9 %collective-permute-done.12.refs_4_ = bf16[512,512]{1,0:T(8,128)(2,1)S(1)} collective-permute-done((bf16[512,512]{1,0:T(8,128)(2,1)}, bf16[512,512]{1,0:T(8,128)(2,1)S(1)}, u32[]{:S(2)}, u32[]{:S(2)}) %collective-permute-start.12) | collective-permute-done | bytes 524320 | tf_op jit(solution)/shard_map/ppermute | solution.py:31
  66.4 2.6 %collective-permute-done.14.refs_5_ = bf16[512,512]{1,0:T(8,128)(2,1)S(1)} collective-permute-done((bf16[512,512]{1,0:T(8,128)(2,1)}, bf16[512,512]{1,0:T(8,128)(2,1)S(1)}, u32[]{:S(2)}, u32[]{:S(2)}) %collective-permute-start.14) | collective-permute-done | bytes 524320 | tf_op jit(solution)/shard_map/ppermute | solution.py:31
  69.0 5.6 %collective-permute-done.8.refs_4_ = bf16[512,512]{1,0:T(8,128)(2,1)S(1)} collective-permute-done((bf16[512,512]{1,0:T(8,128)(2,1)}, bf16[512,512]{1,0:T(8,128)(2,1)S(1)}, u32[]{:S(2)}, u32[]{:S(2)}) %collective-permute-start.8) | collective-permute-done | bytes 524320 | tf_op jit(solution)/shard_map/ppermute | solution.py:31
  79.0 2.5 %collective-permute-start.27 = (bf16[512,512]{1,0:T(8,128)(2,1)}, bf16[512,512]{1,0:T(8,128)(2,1)S(1)}, u32[]{:S(2)}, u32[]{:S(2)}) collective-permute-start(bf16[512,512]{1,0:T(8,128)(2,1)} %copy-done.5), channel_id=1, source_target_pairs={{0,24},{1,25},{2,26},{3,27},{4,28},{5,29},{6,30},{7,31},{8,0},{9,1... | collective-permute-start | bytes 1572872 | tf_op jit(solution)/shard_map/ppermute | solution.py:31
  81.7 2.5 %shard_map.62.chosen_ref = bf16[8,512,512]{2,1,0:T(8,128)(2,1)S(1)} custom-call(s32[16]{0:T(128)S(1)} %stack.67.index_ref, bf16[16,512,128]{2,1,0:T(8,128)(2,1)S(1)} %all-to-all-done.acts_ref, bf16[16,512,128]{2,1,0:T(8,128)(2,1)} %collective-permute-done.15.other_ref), custom_call_target="tpu_custom_call" | custom-call | bytes 8388608 | tf_op jit(solution)/shard_map/pallas_call | solution.py:140
  90.5 4.0 %collective-permute-start.19 = (f32[32,512]{1,0:T(8,128)S(1)}, f32[32,512]{1,0:T(8,128)S(1)}, u32[]{:S(2)}, u32[]{:S(2)}) collective-permute-start(f32[32,512]{1,0:T(8,128)S(1)} %get-tuple-element.74), channel_id=1, source_target_pairs={{0,7},{1,0},{2,1},{3,2},{4,3},{5,4},{6,5},{7,6},{8,15},{9,8},{10,9... | collective-permute-start | bytes 196616 | tf_op jit(solution)/shard_map/ppermute | solution.py:31
  94.6 3.0 %shard_map.65.refs_2_ = f32[512,512]{1,0:T(8,128)S(1)} custom-call(bf16[8,512,512]{2,1,0:T(8,128)(2,1)S(1)} %shard_map.62.chosen_ref, bf16[512,512]{1,0:T(8,128)(2,1)S(1)} %copy-done.1, bf16[512,512]{1,0:T(8,128)(2,1)S(1)} %copy-done.2, bf16[512,512]{1,0:T(8,128)(2,1)} %collective-permute-done.11.refs_2_, bf16[512,512]{1,0:T(8,128)(2,1)S(1)} %copy-done.8, ...), custom_call_target="tpu_custom_call" | custom-call | flops 1610612736 | bytes 6291456 | tf_op jit(solution)/shard_map/pallas_call | solution.py:166
  98.9 2.7 %collective-permute-start.29 = (f32[32,512]{1,0:T(8,128)S(1)}, f32[32,512]{1,0:T(8,128)S(1)}, u32[]{:S(2)}, u32[]{:S(2)}) collective-permute-start(f32[32,512]{1,0:T(8,128)S(1)} %get-tuple-element.84), channel_id=1, source_target_pairs={{0,7},{1,0},{2,1},{3,2},{4,3},{5,4},{6,5},{7,6},{8,15},{9,8},{10,9... | collective-permute-start | bytes 196616 | tf_op jit(solution)/shard_map/ppermute | solution.py:31
  103.3 2.9 %collective-permute-start.31 = (f32[64,512]{1,0:T(8,128)S(1)}, f32[64,512]{1,0:T(8,128)S(1)}, u32[]{:S(2)}, u32[]{:S(2)}) collective-permute-start(f32[64,512]{1,0:T(8,128)S(1)} %pad_maximum_fusion.4), channel_id=1, source_target_pairs={{0,7},{1,0},{2,1},{3,2},{4,3},{5,4},{6,5},{7,6},{8,15},{9,8},{10,9... | collective-permute-start | bytes 393224 | tf_op jit(solution)/shard_map/ppermute | solution.py:31
  112.0 2.7 %collective-permute-start.33 = (f32[64,512]{1,0:T(8,128)S(1)}, f32[64,512]{1,0:T(8,128)S(1)}, u32[]{:S(2)}, u32[]{:S(2)}) collective-permute-start(f32[64,512]{1,0:T(8,128)S(1)} %get-tuple-element.78), channel_id=1, source_target_pairs={{0,7},{1,0},{2,1},{3,2},{4,3},{5,4},{6,5},{7,6},{8,15},{9,8},{10,9... | collective-permute-start | bytes 393224 | tf_op jit(solution)/shard_map/ppermute | solution.py:31
  114.8 2.7 %collective-permute-start.25 = (f32[64,512]{1,0:T(8,128)S(1)}, f32[64,512]{1,0:T(8,128)S(1)}, u32[]{:S(2)}, u32[]{:S(2)}) collective-permute-start(f32[64,512]{1,0:T(8,128)S(1)} %get-tuple-element.66), channel_id=1, source_target_pairs={{0,7},{1,0},{2,1},{3,2},{4,3},{5,4},{6,5},{7,6},{8,15},{9,8},{10,9... | collective-permute-start | bytes 393224 | tf_op jit(solution)/shard_map/ppermute | solution.py:31
  118.6 2.7 %collective-permute-start.35 = (f32[64,512]{1,0:T(8,128)S(1)}, f32[64,512]{1,0:T(8,128)S(1)}, u32[]{:S(2)}, u32[]{:S(2)}) collective-permute-start(f32[64,512]{1,0:T(8,128)S(1)} %get-tuple-element.76), channel_id=1, source_target_pairs={{0,7},{1,0},{2,1},{3,2},{4,3},{5,4},{6,5},{7,6},{8,15},{9,8},{10,9... | collective-permute-start | bytes 393224 | tf_op jit(solution)/shard_map/ppermute | solution.py:31
  121.2 2.3 %collective-permute-done.34 = f32[64,512]{1,0:T(8,128)S(1)} collective-permute-done((f32[64,512]{1,0:T(8,128)S(1)}, f32[64,512]{1,0:T(8,128)S(1)}, u32[]{:S(2)}, u32[]{:S(2)}) %collective-permute-start.34) | collective-permute-done | bytes 131104 | tf_op jit(solution)/shard_map/ppermute | solution.py:31
  124.6 17.4 %all-to-all-start.1 = ((f32[256,1,128]{2,1,0:T(1,128)}), f32[256,1,128]{2,1,0:T(1,128)S(1)}, u32[]{:S(2)}, u32[]{:S(2)}) async-start(f32[256,1,128]{2,1,0:T(1,128)} %broadcast_in_dim.2), calls=%async_computation.1 | async-start | bytes 262144 | tf_op jit(solution)/shard_map/all_to_all | solution.py:203
  144.3 10.8 %all-to-all-done.1 = f32[256,1,128]{2,1,0:T(1,128)S(1)} async-done(((f32[256,1,128]{2,1,0:T(1,128)}), f32[256,1,128]{2,1,0:T(1,128)S(1)}, u32[]{:S(2)}, u32[]{:S(2)}) %all-to-all-start.1) | async-done | bytes 131104 | tf_op jit(solution)/shard_map/all_to_all | solution.py:203
  (134 shorter events, 42.4 us)
Async XLA Ops:
  5.8 6.9 %collective-permute-start.1 = (bf16[128,1024]{1,0:T(8,128)(2,1)}, bf16[128,1024]{1,0:T(8,128)(2,1)S(1)}, u32[]{:S(2)}, u32[]{:S(2)}) collective-permute-start(bf16[128,1024]{1,0:T(8,128)(2,1)} %get-tuple-element.34.refs_0_), channel_id=1, source_target_pairs={{0,64},{1,65},{2,66},{3,67},{4,68},{5,69},{6,70},{7,71},{8,72},{9,... | collective-permute-start | bytes 786440 | tf_op jit(solution)/shard_map/ppermute | solution.py:31
  8.5 10.5 %collective-permute-start.3 = (bf16[128,1024]{1,0:T(8,128)(2,1)}, bf16[128,1024]{1,0:T(8,128)(2,1)S(1)}, u32[]{:S(2)}, u32[]{:S(2)}) collective-permute-start(bf16[128,1024]{1,0:T(8,128)(2,1)} %get-tuple-element.34.refs_0_), channel_id=1, source_target_pairs={{0,192},{1,193},{2,194},{3,195},{4,196},{5,197},{6,198},{7,199},{8... | collective-permute-start | bytes 786440 | tf_op jit(solution)/shard_map/ppermute | solution.py:31
  8.6 10.8 %collective-permute-start.2 = (bf16[128,1024]{1,0:T(8,128)(2,1)S(1)}, bf16[128,1024]{1,0:T(8,128)(2,1)S(1)}, u32[]{:S(2)}, u32[]{:S(2)}) collective-permute-start(bf16[128,1024]{1,0:T(8,128)(2,1)S(1)} %collective-permute-done.refs_1_), channel_id=1, source_target_pairs={{0,64},{1,65},{2,66},{3,67},{4,68},{5,69},{6,70},{7,71},{8,72},{9,... | collective-permute-start | bytes 786440 | tf_op jit(solution)/shard_map/ppermute | solution.py:31
  12.7 6.7 %collective-permute-start.5 = (bf16[128,1024]{1,0:T(8,128)(2,1)S(1)}, bf16[128,1024]{1,0:T(8,128)(2,1)S(1)}, u32[]{:S(2)}, u32[]{:S(2)}) collective-permute-start(bf16[128,1024]{1,0:T(8,128)(2,1)S(1)} %collective-permute-done.1.refs_2_), channel_id=1, source_target_pairs={{0,64},{1,65},{2,66},{3,67},{4,68},{5,69},{6,70},{7,71},{8,72},{9,... | collective-permute-start | bytes 786440 | tf_op jit(solution)/shard_map/ppermute | solution.py:31
  12.7 7.4 %collective-permute-start.6 = (bf16[128,1024]{1,0:T(8,128)(2,1)S(1)}, bf16[128,1024]{1,0:T(8,128)(2,1)}, u32[]{:S(2)}, u32[]{:S(2)}) collective-permute-start(bf16[128,1024]{1,0:T(8,128)(2,1)S(1)} %collective-permute-done.4.refs_5_), channel_id=1, source_target_pairs={{0,192},{1,193},{2,194},{3,195},{4,196},{5,197},{6,198},{7,199},{8... | collective-permute-start | bytes 786440 | tf_op jit(solution)/shard_map/ppermute | solution.py:31
  20.9 55.3 %all-to-all-start = ((bf16[16,512,128]{2,1,0:T(8,128)(2,1)}), bf16[16,512,128]{2,1,0:T(8,128)(2,1)S(1)}, u32[]{:S(2)}, u32[]{:S(2)}) async-start(bf16[16,512,128]{2,1,0:T(8,128)(2,1)} %shard_map.59), calls=%async_computation | async-start | bytes 4194304 | tf_op jit(solution)/shard_map/all_to_all | solution.py:221
  28.2 29.6 %collective-permute-start.10 = (bf16[512,512]{1,0:T(8,128)(2,1)}, bf16[512,512]{1,0:T(8,128)(2,1)S(1)}, u32[]{:S(2)}, u32[]{:S(2)}) collective-permute-start(bf16[512,512]{1,0:T(8,128)(2,1)} %get-tuple-element.38.refs_1_), channel_id=1, source_target_pairs={{0,24},{1,25},{2,26},{3,27},{4,28},{5,29},{6,30},{7,31},{8,0},{9,1... | collective-permute-start | bytes 1572872 | tf_op jit(solution)/shard_map/ppermute | solution.py:31
  30.7 28.5 %collective-permute-start.11 = (bf16[512,512]{1,0:T(8,128)(2,1)}, bf16[512,512]{1,0:T(8,128)(2,1)}, u32[]{:S(2)}, u32[]{:S(2)}) collective-permute-start(bf16[512,512]{1,0:T(8,128)(2,1)} %get-tuple-element.39.refs_0_), channel_id=1, source_target_pairs={{0,8},{1,9},{2,10},{3,11},{4,12},{5,13},{6,14},{7,15},{8,16},{9,17... | collective-permute-start | bytes 1572872 | tf_op jit(solution)/shard_map/ppermute | solution.py:31
  30.7 32.6 %collective-permute-start.12 = (bf16[512,512]{1,0:T(8,128)(2,1)}, bf16[512,512]{1,0:T(8,128)(2,1)S(1)}, u32[]{:S(2)}, u32[]{:S(2)}) collective-permute-start(bf16[512,512]{1,0:T(8,128)(2,1)} %get-tuple-element.39.refs_0_), channel_id=1, source_target_pairs={{0,24},{1,25},{2,26},{3,27},{4,28},{5,29},{6,30},{7,31},{8,0},{9,1... | collective-permute-start | bytes 1572872 | tf_op jit(solution)/shard_map/ppermute | solution.py:31
  33.4 32.1 %collective-permute-start.13 = (bf16[512,512]{1,0:T(8,128)(2,1)}, bf16[512,512]{1,0:T(8,128)(2,1)S(1)}, u32[]{:S(2)}, u32[]{:S(2)}) collective-permute-start(bf16[512,512]{1,0:T(8,128)(2,1)} %get-tuple-element.40.refs_1_), channel_id=1, source_target_pairs={{0,8},{1,9},{2,10},{3,11},{4,12},{5,13},{6,14},{7,15},{8,16},{9,17... | collective-permute-start | bytes 1572872 | tf_op jit(solution)/shard_map/ppermute | solution.py:31
  33.4 35.5 %collective-permute-start.14 = (bf16[512,512]{1,0:T(8,128)(2,1)}, bf16[512,512]{1,0:T(8,128)(2,1)S(1)}, u32[]{:S(2)}, u32[]{:S(2)}) collective-permute-start(bf16[512,512]{1,0:T(8,128)(2,1)} %get-tuple-element.40.refs_1_), channel_id=1, source_target_pairs={{0,24},{1,25},{2,26},{3,27},{4,28},{5,29},{6,30},{7,31},{8,0},{9,1... | collective-permute-start | bytes 1572872 | tf_op jit(solution)/shard_map/ppermute | solution.py:31
  57.8 11.2 %collective-permute-start.7 = (bf16[512,512]{1,0:T(8,128)(2,1)}, bf16[512,512]{1,0:T(8,128)(2,1)S(1)}, u32[]{:S(2)}, u32[]{:S(2)}) collective-permute-start(bf16[512,512]{1,0:T(8,128)(2,1)} %get-tuple-element.37.refs_0_), channel_id=1, source_target_pairs={{0,8},{1,9},{2,10},{3,11},{4,12},{5,13},{6,14},{7,15},{8,16},{9,17... | collective-permute-start | bytes 1572872 | tf_op jit(solution)/shard_map/ppermute | solution.py:31
  59.2 15.4 %collective-permute-start.8 = (bf16[512,512]{1,0:T(8,128)(2,1)}, bf16[512,512]{1,0:T(8,128)(2,1)S(1)}, u32[]{:S(2)}, u32[]{:S(2)}) collective-permute-start(bf16[512,512]{1,0:T(8,128)(2,1)} %get-tuple-element.37.refs_0_), channel_id=1, source_target_pairs={{0,24},{1,25},{2,26},{3,27},{4,28},{5,29},{6,30},{7,31},{8,0},{9,1... | collective-permute-start | bytes 1572872 | tf_op jit(solution)/shard_map/ppermute | solution.py:31
  64.1 11.2 %collective-permute-start.9 = (bf16[512,512]{1,0:T(8,128)(2,1)}, bf16[512,512]{1,0:T(8,128)(2,1)S(1)}, u32[]{:S(2)}, u32[]{:S(2)}) collective-permute-start(bf16[512,512]{1,0:T(8,128)(2,1)} %get-tuple-element.38.refs_1_), channel_id=1, source_target_pairs={{0,8},{1,9},{2,10},{3,11},{4,12},{5,13},{6,14},{7,15},{8,16},{9,17... | collective-permute-start | bytes 1572872 | tf_op jit(solution)/shard_map/ppermute | solution.py:31
  76.1 10.4 %collective-permute-start.16 = (bf16[512,512]{1,0:T(8,128)(2,1)}, bf16[512,512]{1,0:T(8,128)(2,1)}, u32[]{:S(2)}, u32[]{:S(2)}) collective-permute-start(bf16[512,512]{1,0:T(8,128)(2,1)} %copy-done.13), channel_id=1, source_target_pairs={{0,8},{1,9},{2,10},{3,11},{4,12},{5,13},{6,14},{7,15},{8,16},{9,17... | collective-permute-start | bytes 1572872 | tf_op jit(solution)/shard_map/ppermute | solution.py:31
  77.5 9.0 %collective-permute-start.17 = (bf16[512,512]{1,0:T(8,128)(2,1)}, bf16[512,512]{1,0:T(8,128)(2,1)}, u32[]{:S(2)}, u32[]{:S(2)}) collective-permute-start(bf16[512,512]{1,0:T(8,128)(2,1)} %copy-done.11), channel_id=1, source_target_pairs={{0,24},{1,25},{2,26},{3,27},{4,28},{5,29},{6,30},{7,31},{8,0},{9,1... | collective-permute-start | bytes 1572872 | tf_op jit(solution)/shard_map/ppermute | solution.py:31
  78.8 18.8 %collective-permute-start.26 = (bf16[512,512]{1,0:T(8,128)(2,1)}, bf16[512,512]{1,0:T(8,128)(2,1)S(1)}, u32[]{:S(2)}, u32[]{:S(2)}) collective-permute-start(bf16[512,512]{1,0:T(8,128)(2,1)} %collective-permute-done.11.refs_2_), channel_id=1, source_target_pairs={{0,8},{1,9},{2,10},{3,11},{4,12},{5,13},{6,14},{7,15},{8,16},{9,17... | collective-permute-start | bytes 1572872 | tf_op jit(solution)/shard_map/ppermute | solution.py:31
  79.0 18.6 %collective-permute-start.27 = (bf16[512,512]{1,0:T(8,128)(2,1)}, bf16[512,512]{1,0:T(8,128)(2,1)S(1)}, u32[]{:S(2)}, u32[]{:S(2)}) collective-permute-start(bf16[512,512]{1,0:T(8,128)(2,1)} %copy-done.5), channel_id=1, source_target_pairs={{0,24},{1,25},{2,26},{3,27},{4,28},{5,29},{6,30},{7,31},{8,0},{9,1... | collective-permute-start | bytes 1572872 | tf_op jit(solution)/shard_map/ppermute | solution.py:31
  88.8 12.8 %collective-permute-start.18 = (f32[32,512]{1,0:T(8,128)S(1)}, f32[32,512]{1,0:T(8,128)S(1)}, u32[]{:S(2)}, u32[]{:S(2)}) collective-permute-start(f32[32,512]{1,0:T(8,128)S(1)} %get-tuple-element.75), channel_id=1, source_target_pairs={{0,1},{1,2},{2,3},{3,4},{4,5},{5,6},{6,7},{7,0},{8,9},{9,10},{10,1... | collective-permute-start | bytes 196616 | tf_op jit(solution)/shard_map/ppermute | solution.py:31
  90.5 11.1 %collective-permute-start.19 = (f32[32,512]{1,0:T(8,128)S(1)}, f32[32,512]{1,0:T(8,128)S(1)}, u32[]{:S(2)}, u32[]{:S(2)}) collective-permute-start(f32[32,512]{1,0:T(8,128)S(1)} %get-tuple-element.74), channel_id=1, source_target_pairs={{0,7},{1,0},{2,1},{3,2},{4,3},{5,4},{6,5},{7,6},{8,15},{9,8},{10,9... | collective-permute-start | bytes 196616 | tf_op jit(solution)/shard_map/ppermute | solution.py:31
  107.0 7.7 %collective-permute-start.22 = (f32[64,512]{1,0:T(8,128)S(1)}, f32[64,512]{1,0:T(8,128)S(1)}, u32[]{:S(2)}, u32[]{:S(2)}) collective-permute-start(f32[64,512]{1,0:T(8,128)S(1)} %get-tuple-element.69), channel_id=1, source_target_pairs={{0,1},{1,2},{2,3},{3,4},{4,5},{5,6},{6,7},{7,0},{8,9},{9,10},{10,1... | collective-permute-start | bytes 393224 | tf_op jit(solution)/shard_map/ppermute | solution.py:31
  107.5 7.2 %collective-permute-start.23 = (f32[64,512]{1,0:T(8,128)S(1)}, f32[64,512]{1,0:T(8,128)S(1)}, u32[]{:S(2)}, u32[]{:S(2)}) collective-permute-start(f32[64,512]{1,0:T(8,128)S(1)} %get-tuple-element.68), channel_id=1, source_target_pairs={{0,7},{1,0},{2,1},{3,2},{4,3},{5,4},{6,5},{7,6},{8,15},{9,8},{10,9... | collective-permute-start | bytes 393224 | tf_op jit(solution)/shard_map/ppermute | solution.py:31
  124.6 30.5 %all-to-all-start.1 = ((f32[256,1,128]{2,1,0:T(1,128)}), f32[256,1,128]{2,1,0:T(1,128)S(1)}, u32[]{:S(2)}, u32[]{:S(2)}) async-start(f32[256,1,128]{2,1,0:T(1,128)} %broadcast_in_dim.2), calls=%async_computation.1 | async-start | bytes 262144 | tf_op jit(solution)/shard_map/all_to_all | solution.py:203
  142.0 14.3 %collective-permute-start.36 = (f32[32,1024]{1,0:T(8,128)S(1)}, f32[32,1024]{1,0:T(8,128)S(1)}, u32[]{:S(2)}, u32[]{:S(2)}) collective-permute-start(f32[32,1024]{1,0:T(8,128)S(1)} %broadcast_select_fusion), channel_id=1, source_target_pairs={{0,32},{1,33},{2,34},{3,35},{4,36},{5,37},{6,38},{7,39},{8,40},{9,... | collective-permute-start | bytes 393224 | tf_op jit(solution)/shard_map/ppermute | solution.py:31
  (40 other events, 201.7 us)

commit v8 on v7

--- a/solution.py
+++ b/solution.py
@@ -230,7 +230,9 @@
 
     stacked = stack(pieces)
     direct = [second_ring(part, step) for part in stacked for step in (1, -1)]
-    acts, *direct = lax.optimization_barrier((acts, *direct))
+    acts, *first = lax.optimization_barrier((acts, *direct[:4]))
+    acts, *second = lax.optimization_barrier((acts, *direct[4:]))
+    direct = first + second
     chosen = choose(index, acts, swap_cores(acts))
     streams = []
     for (upper, lower), sent in ((stacked[:2], direct[:4]), (stacked[2:], direct[4:])):

time: 157 us -> 157 us (level)
  starting transfers between devices: 74.3 us -> 69.1 us
  waiting for transfers between devices: 54.3 us -> 57.5 us
    ppermute x37, starting transfers between devices: 52.4 us -> 48.1 us  [send(): return lax.ppermute(value, AXES, pairs(move))]
    ppermute x37, waiting for transfers between devices: 43.5 us -> 46.7 us  [send(): return lax.ppermute(value, AXES, pairs(move))]
    unnamed x50 -> x42, local copies, waits for them, and re-layouts: 6.25 us -> 7.16 us
  transfers between devices with their start and end apart: 39 -> 39, of which waited for: 12 -> 13; matrix products, arithmetic and copies ran while one was open for 1% -> 1% of each run, Pallas kernels for 10% -> 11%
where the time goes in v8:
time: 157 us
  starting transfers between devices  69.1 us (44%)
  waiting for transfers between devices  57.5 us (37%)
  Pallas kernels  18.7 us (12%)
  local copies, waits for them, and re-layouts  8.06 us (5%)
  between operations  1.77 us (1%)
  other arithmetic  1.75 us (1%)
    ppermute x37, starting transfers between devices, send(): return lax.ppermute(value, AXES, pairs(move))  48.1 us
    ppermute x37, waiting for transfers between devices, send(): return lax.ppermute(value, AXES, pairs(move))  46.7 us
    all_to_all x1, starting transfers between devices, sum_all(): lax.all_to_all(rows, AXES, split_axis=0, concat_axis=0, tiled=True)  16.6 us
    all_to_all x1, waiting for transfers between devices, sum_all(): lax.all_to_all(rows, AXES, split_axis=0, concat_axis=0, tiled=True)  10.8 us
    pallas_call x4, Pallas kernels, multiply(): pl.pallas_call(kernel, out_shape=jax.ShapeDtypeStruct((width, n), jnp.flo...  9.51 us
    unnamed x42, local copies, waits for them, and re-layouts  7.16 us
    all_to_all x1, starting transfers between devices, body(): lax.all_to_all(across, ('y', 'x'), split_axis=0, concat_axis=0, tiled=True)  4.42 us
  transfers between devices with their start and end apart: 39, of which 13 were waited for; matrix products, arithmetic and copies ran while one was open for 1% of the time, Pallas kernels for 11%

profile of v8, /device:TPU:1, one launch (start us, length us, event | category | flops | bytes accessed | tf_op | source)
XLA Modules:
  0.0 156.8 jit_solution(4047787279137633663)
XLA Ops:
  2.5 3.2 %collective-permute-start = (bf16[128,1024]{1,0:T(8,128)(2,1)}, bf16[128,1024]{1,0:T(8,128)(2,1)S(1)}, u32[]{:S(2)}, u32[]{:S(2)}) collective-permute-start(bf16[128,1024]{1,0:T(8,128)(2,1)} %get-tuple-element.36), channel_id=1, source_target_pairs={{0,32},{1,33},{2,34},{3,35},{4,36},{5,37},{6,38},{7,39},{8,40},{9,... | collective-permute-start | bytes 786440 | tf_op jit(solution)/shard_map/ppermute | solution.py:31
  9.9 2.8 %collective-permute-done.1.refs_2_ = bf16[128,1024]{1,0:T(8,128)(2,1)S(1)} collective-permute-done((bf16[128,1024]{1,0:T(8,128)(2,1)}, bf16[128,1024]{1,0:T(8,128)(2,1)S(1)}, u32[]{:S(2)}, u32[]{:S(2)}) %collective-permute-start.1) | collective-permute-done | bytes 262176 | tf_op jit(solution)/shard_map/ppermute | solution.py:31
  12.7 2.7 %collective-permute-start.6 = (bf16[128,1024]{1,0:T(8,128)(2,1)S(1)}, bf16[128,1024]{1,0:T(8,128)(2,1)}, u32[]{:S(2)}, u32[]{:S(2)}) collective-permute-start(bf16[128,1024]{1,0:T(8,128)(2,1)S(1)} %collective-permute-done.4.refs_5_), channel_id=1, source_target_pairs={{0,192},{1,193},{2,194},{3,195},{4,196},{5,197},{6,198},{7,199},{8... | collective-permute-start | bytes 786440 | tf_op jit(solution)/shard_map/ppermute | solution.py:31
  20.9 4.4 %all-to-all-start = ((bf16[16,512,128]{2,1,0:T(8,128)(2,1)}), bf16[16,512,128]{2,1,0:T(8,128)(2,1)S(1)}, u32[]{:S(2)}, u32[]{:S(2)}) async-start(bf16[16,512,128]{2,1,0:T(8,128)(2,1)} %shard_map.59), calls=%async_computation | async-start | bytes 4194304 | tf_op jit(solution)/shard_map/all_to_all | solution.py:221
  25.3 2.9 %shard_map.61 = (bf16[512,512]{1,0:T(8,128)(2,1)}, bf16[512,512]{1,0:T(8,128)(2,1)}, bf16[512,512]{1,0:T(8,128)(2,1)}, bf16[512,512]{1,0:T(8,128)(2,1)}) custom-call(bf16[128,1024]{1,0:T(8,128)(2,1)} %get-tuple-element.35.refs_0_, bf16[128,1024]{1,0:T(8,128)(2,1)} %copy-done.15, bf16[128,1024]{1,0:T(8,128)(2,1)} %copy-done.16, bf16[128,1024]{1,0:T(8,128)(2,1)} %copy-done.19, ...), custom_call_target="tpu_custom_call" | custom-call | bytes 4194304 | tf_op jit(solution)/shard_map/pallas_call | solution.py:91
  28.2 2.6 %collective-permute-start.10 = (bf16[512,512]{1,0:T(8,128)(2,1)}, bf16[512,512]{1,0:T(8,128)(2,1)}, u32[]{:S(2)}, u32[]{:S(2)}) collective-permute-start(bf16[512,512]{1,0:T(8,128)(2,1)} %get-tuple-element.39.refs_1_), channel_id=1, source_target_pairs={{0,24},{1,25},{2,26},{3,27},{4,28},{5,29},{6,30},{7,31},{8,0},{9,1... | collective-permute-start | bytes 1572872 | tf_op jit(solution)/shard_map/ppermute | solution.py:31
  30.7 2.7 %collective-permute-start.8 = (bf16[512,512]{1,0:T(8,128)(2,1)}, bf16[512,512]{1,0:T(8,128)(2,1)S(1)}, u32[]{:S(2)}, u32[]{:S(2)}) collective-permute-start(bf16[512,512]{1,0:T(8,128)(2,1)} %get-tuple-element.38.refs_0_), channel_id=1, source_target_pairs={{0,24},{1,25},{2,26},{3,27},{4,28},{5,29},{6,30},{7,31},{8,0},{9,1... | collective-permute-start | bytes 1572872 | tf_op jit(solution)/shard_map/ppermute | solution.py:31
  33.4 24.3 %collective-permute-done.10.refs_5_ = bf16[512,512]{1,0:T(8,128)(2,1)} collective-permute-done((bf16[512,512]{1,0:T(8,128)(2,1)}, bf16[512,512]{1,0:T(8,128)(2,1)}, u32[]{:S(2)}, u32[]{:S(2)}) %collective-permute-start.10) | collective-permute-done | bytes 524320 | tf_op jit(solution)/shard_map/ppermute | solution.py:31
  60.0 3.4 %collective-permute-done.8.refs_4_ = bf16[512,512]{1,0:T(8,128)(2,1)S(1)} collective-permute-done((bf16[512,512]{1,0:T(8,128)(2,1)}, bf16[512,512]{1,0:T(8,128)(2,1)S(1)}, u32[]{:S(2)}, u32[]{:S(2)}) %collective-permute-start.8) | collective-permute-done | bytes 524320 | tf_op jit(solution)/shard_map/ppermute | solution.py:31
  65.2 3.8 %collective-permute-done.11.refs_2_ = bf16[512,512]{1,0:T(8,128)(2,1)} collective-permute-done((bf16[512,512]{1,0:T(8,128)(2,1)}, bf16[512,512]{1,0:T(8,128)(2,1)}, u32[]{:S(2)}, u32[]{:S(2)}) %collective-permute-start.11) | collective-permute-done | bytes 524320 | tf_op jit(solution)/shard_map/ppermute | solution.py:31
  69.9 4.6 %collective-permute-done.13.refs_3_ = bf16[512,512]{1,0:T(8,128)(2,1)S(1)} collective-permute-done((bf16[512,512]{1,0:T(8,128)(2,1)}, bf16[512,512]{1,0:T(8,128)(2,1)S(1)}, u32[]{:S(2)}, u32[]{:S(2)}) %collective-permute-start.13) | collective-permute-done | bytes 524320 | tf_op jit(solution)/shard_map/ppermute | solution.py:31
  78.6 2.5 %collective-permute-start.27 = (bf16[512,512]{1,0:T(8,128)(2,1)}, bf16[512,512]{1,0:T(8,128)(2,1)S(1)}, u32[]{:S(2)}, u32[]{:S(2)}) collective-permute-start(bf16[512,512]{1,0:T(8,128)(2,1)} %collective-permute-done.14.refs_5_), channel_id=1, source_target_pairs={{0,24},{1,25},{2,26},{3,27},{4,28},{5,29},{6,30},{7,31},{8,0},{9,1... | collective-permute-start | bytes 1572872 | tf_op jit(solution)/shard_map/ppermute | solution.py:31
  83.8 3.1 %shard_map.63.refs_2_ = f32[512,512]{1,0:T(8,128)S(1)} custom-call(bf16[8,512,512]{2,1,0:T(8,128)(2,1)S(1)} %shard_map.62.chosen_ref, bf16[512,512]{1,0:T(8,128)(2,1)S(1)} %copy-done.3, bf16[512,512]{1,0:T(8,128)(2,1)S(1)} %copy-done.4, bf16[512,512]{1,0:T(8,128)(2,1)S(1)} %copy-done.10, bf16[512,512]{1,0:T(8,128)(2,1)S(1)} %copy-done.14, ...), custom_call_target="tpu_custom_call" | custom-call | flops 1610612736 | bytes 6291456 | tf_op jit(solution)/shard_map/pallas_call | solution.py:166
  90.9 4.0 %collective-permute-start.19 = (f32[32,512]{1,0:T(8,128)S(1)}, f32[32,512]{1,0:T(8,128)S(1)}, u32[]{:S(2)}, u32[]{:S(2)}) collective-permute-start(f32[32,512]{1,0:T(8,128)S(1)} %get-tuple-element.76), channel_id=1, source_target_pairs={{0,7},{1,0},{2,1},{3,2},{4,3},{5,4},{6,5},{7,6},{8,15},{9,8},{10,9... | collective-permute-start | bytes 196616 | tf_op jit(solution)/shard_map/ppermute | solution.py:31
  94.9 3.1 %shard_map.65.refs_2_ = f32[512,512]{1,0:T(8,128)S(1)} custom-call(bf16[8,512,512]{2,1,0:T(8,128)(2,1)S(1)} %shard_map.62.chosen_ref, bf16[512,512]{1,0:T(8,128)(2,1)S(1)} %copy-done.1, bf16[512,512]{1,0:T(8,128)(2,1)S(1)} %copy-done.2, bf16[512,512]{1,0:T(8,128)(2,1)} %collective-permute-done.11.refs_2_, bf16[512,512]{1,0:T(8,128)(2,1)S(1)} %copy-done.8, ...), custom_call_target="tpu_custom_call" | custom-call | flops 1610612736 | bytes 6291456 | tf_op jit(solution)/shard_map/pallas_call | solution.py:166
  99.4 2.7 %collective-permute-start.29 = (f32[32,512]{1,0:T(8,128)S(1)}, f32[32,512]{1,0:T(8,128)S(1)}, u32[]{:S(2)}, u32[]{:S(2)}) collective-permute-start(f32[32,512]{1,0:T(8,128)S(1)} %get-tuple-element.86), channel_id=1, source_target_pairs={{0,7},{1,0},{2,1},{3,2},{4,3},{5,4},{6,5},{7,6},{8,15},{9,8},{10,9... | collective-permute-start | bytes 196616 | tf_op jit(solution)/shard_map/ppermute | solution.py:31
  103.8 2.9 %collective-permute-start.31 = (f32[64,512]{1,0:T(8,128)S(1)}, f32[64,512]{1,0:T(8,128)S(1)}, u32[]{:S(2)}, u32[]{:S(2)}) collective-permute-start(f32[64,512]{1,0:T(8,128)S(1)} %pad_maximum_fusion.4), channel_id=1, source_target_pairs={{0,7},{1,0},{2,1},{3,2},{4,3},{5,4},{6,5},{7,6},{8,15},{9,8},{10,9... | collective-permute-start | bytes 393224 | tf_op jit(solution)/shard_map/ppermute | solution.py:31
  107.6 2.6 %collective-permute-start.23 = (f32[64,512]{1,0:T(8,128)S(1)}, f32[64,512]{1,0:T(8,128)S(1)}, u32[]{:S(2)}, u32[]{:S(2)}) collective-permute-start(f32[64,512]{1,0:T(8,128)S(1)} %get-tuple-element.70), channel_id=1, source_target_pairs={{0,7},{1,0},{2,1},{3,2},{4,3},{5,4},{6,5},{7,6},{8,15},{9,8},{10,9... | collective-permute-start | bytes 393224 | tf_op jit(solution)/shard_map/ppermute | solution.py:31
  112.0 2.7 %collective-permute-start.33 = (f32[64,512]{1,0:T(8,128)S(1)}, f32[64,512]{1,0:T(8,128)S(1)}, u32[]{:S(2)}, u32[]{:S(2)}) collective-permute-start(f32[64,512]{1,0:T(8,128)S(1)} %get-tuple-element.80), channel_id=1, source_target_pairs={{0,7},{1,0},{2,1},{3,2},{4,3},{5,4},{6,5},{7,6},{8,15},{9,8},{10,9... | collective-permute-start | bytes 393224 | tf_op jit(solution)/shard_map/ppermute | solution.py:31
  114.8 2.7 %collective-permute-start.25 = (f32[64,512]{1,0:T(8,128)S(1)}, f32[64,512]{1,0:T(8,128)S(1)}, u32[]{:S(2)}, u32[]{:S(2)}) collective-permute-start(f32[64,512]{1,0:T(8,128)S(1)} %get-tuple-element.68), channel_id=1, source_target_pairs={{0,7},{1,0},{2,1},{3,2},{4,3},{5,4},{6,5},{7,6},{8,15},{9,8},{10,9... | collective-permute-start | bytes 393224 | tf_op jit(solution)/shard_map/ppermute | solution.py:31
  118.4 3.2 %collective-permute-start.35 = (f32[64,512]{1,0:T(8,128)S(1)}, f32[64,512]{1,0:T(8,128)S(1)}, u32[]{:S(2)}, u32[]{:S(2)}) collective-permute-start(f32[64,512]{1,0:T(8,128)S(1)} %get-tuple-element.78), channel_id=1, source_target_pairs={{0,7},{1,0},{2,1},{3,2},{4,3},{5,4},{6,5},{7,6},{8,15},{9,8},{10,9... | collective-permute-start | bytes 393224 | tf_op jit(solution)/shard_map/ppermute | solution.py:31
  121.6 2.7 %collective-permute-done.34 = f32[64,512]{1,0:T(8,128)S(1)} collective-permute-done((f32[64,512]{1,0:T(8,128)S(1)}, f32[64,512]{1,0:T(8,128)S(1)}, u32[]{:S(2)}, u32[]{:S(2)}) %collective-permute-start.34) | collective-permute-done | bytes 131104 | tf_op jit(solution)/shard_map/ppermute | solution.py:31
  125.2 16.6 %all-to-all-start.1 = ((f32[256,1,128]{2,1,0:T(1,128)}), f32[256,1,128]{2,1,0:T(1,128)S(1)}, u32[]{:S(2)}, u32[]{:S(2)}) async-start(f32[256,1,128]{2,1,0:T(1,128)} %broadcast_in_dim.2), calls=%async_computation.1 | async-start | bytes 262144 | tf_op jit(solution)/shard_map/all_to_all | solution.py:203
  144.0 10.8 %all-to-all-done.1 = f32[256,1,128]{2,1,0:T(1,128)S(1)} async-done(((f32[256,1,128]{2,1,0:T(1,128)}), f32[256,1,128]{2,1,0:T(1,128)S(1)}, u32[]{:S(2)}, u32[]{:S(2)}) %all-to-all-start.1) | async-done | bytes 131104 | tf_op jit(solution)/shard_map/all_to_all | solution.py:203
  (126 shorter events, 38.3 us)
Async XLA Ops:
  5.8 6.9 %collective-permute-start.1 = (bf16[128,1024]{1,0:T(8,128)(2,1)}, bf16[128,1024]{1,0:T(8,128)(2,1)S(1)}, u32[]{:S(2)}, u32[]{:S(2)}) collective-permute-start(bf16[128,1024]{1,0:T(8,128)(2,1)} %get-tuple-element.35.refs_0_), channel_id=1, source_target_pairs={{0,64},{1,65},{2,66},{3,67},{4,68},{5,69},{6,70},{7,71},{8,72},{9,... | collective-permute-start | bytes 786440 | tf_op jit(solution)/shard_map/ppermute | solution.py:31
  8.5 10.5 %collective-permute-start.3 = (bf16[128,1024]{1,0:T(8,128)(2,1)}, bf16[128,1024]{1,0:T(8,128)(2,1)S(1)}, u32[]{:S(2)}, u32[]{:S(2)}) collective-permute-start(bf16[128,1024]{1,0:T(8,128)(2,1)} %get-tuple-element.35.refs_0_), channel_id=1, source_target_pairs={{0,192},{1,193},{2,194},{3,195},{4,196},{5,197},{6,198},{7,199},{8... | collective-permute-start | bytes 786440 | tf_op jit(solution)/shard_map/ppermute | solution.py:31
  8.6 10.8 %collective-permute-start.2 = (bf16[128,1024]{1,0:T(8,128)(2,1)S(1)}, bf16[128,1024]{1,0:T(8,128)(2,1)S(1)}, u32[]{:S(2)}, u32[]{:S(2)}) collective-permute-start(bf16[128,1024]{1,0:T(8,128)(2,1)S(1)} %collective-permute-done.refs_1_), channel_id=1, source_target_pairs={{0,64},{1,65},{2,66},{3,67},{4,68},{5,69},{6,70},{7,71},{8,72},{9,... | collective-permute-start | bytes 786440 | tf_op jit(solution)/shard_map/ppermute | solution.py:31
  12.7 7.4 %collective-permute-start.6 = (bf16[128,1024]{1,0:T(8,128)(2,1)S(1)}, bf16[128,1024]{1,0:T(8,128)(2,1)}, u32[]{:S(2)}, u32[]{:S(2)}) collective-permute-start(bf16[128,1024]{1,0:T(8,128)(2,1)S(1)} %collective-permute-done.4.refs_5_), channel_id=1, source_target_pairs={{0,192},{1,193},{2,194},{3,195},{4,196},{5,197},{6,198},{7,199},{8... | collective-permute-start | bytes 786440 | tf_op jit(solution)/shard_map/ppermute | solution.py:31
  20.9 44.3 %all-to-all-start = ((bf16[16,512,128]{2,1,0:T(8,128)(2,1)}), bf16[16,512,128]{2,1,0:T(8,128)(2,1)S(1)}, u32[]{:S(2)}, u32[]{:S(2)}) async-start(bf16[16,512,128]{2,1,0:T(8,128)(2,1)} %shard_map.59), calls=%async_computation | async-start | bytes 4194304 | tf_op jit(solution)/shard_map/all_to_all | solution.py:221
  28.2 29.6 %collective-permute-start.10 = (bf16[512,512]{1,0:T(8,128)(2,1)}, bf16[512,512]{1,0:T(8,128)(2,1)}, u32[]{:S(2)}, u32[]{:S(2)}) collective-permute-start(bf16[512,512]{1,0:T(8,128)(2,1)} %get-tuple-element.39.refs_1_), channel_id=1, source_target_pairs={{0,24},{1,25},{2,26},{3,27},{4,28},{5,29},{6,30},{7,31},{8,0},{9,1... | collective-permute-start | bytes 1572872 | tf_op jit(solution)/shard_map/ppermute | solution.py:31
  30.7 27.0 %collective-permute-start.7 = (bf16[512,512]{1,0:T(8,128)(2,1)}, bf16[512,512]{1,0:T(8,128)(2,1)S(1)}, u32[]{:S(2)}, u32[]{:S(2)}) collective-permute-start(bf16[512,512]{1,0:T(8,128)(2,1)} %get-tuple-element.38.refs_0_), channel_id=1, source_target_pairs={{0,8},{1,9},{2,10},{3,11},{4,12},{5,13},{6,14},{7,15},{8,16},{9,17... | collective-permute-start | bytes 1572872 | tf_op jit(solution)/shard_map/ppermute | solution.py:31
  30.7 32.7 %collective-permute-start.8 = (bf16[512,512]{1,0:T(8,128)(2,1)}, bf16[512,512]{1,0:T(8,128)(2,1)S(1)}, u32[]{:S(2)}, u32[]{:S(2)}) collective-permute-start(bf16[512,512]{1,0:T(8,128)(2,1)} %get-tuple-element.38.refs_0_), channel_id=1, source_target_pairs={{0,24},{1,25},{2,26},{3,27},{4,28},{5,29},{6,30},{7,31},{8,0},{9,1... | collective-permute-start | bytes 1572872 | tf_op jit(solution)/shard_map/ppermute | solution.py:31
  33.4 30.9 %collective-permute-start.9 = (bf16[512,512]{1,0:T(8,128)(2,1)}, bf16[512,512]{1,0:T(8,128)(2,1)S(1)}, u32[]{:S(2)}, u32[]{:S(2)}) collective-permute-start(bf16[512,512]{1,0:T(8,128)(2,1)} %get-tuple-element.39.refs_1_), channel_id=1, source_target_pairs={{0,8},{1,9},{2,10},{3,11},{4,12},{5,13},{6,14},{7,15},{8,16},{9,17... | collective-permute-start | bytes 1572872 | tf_op jit(solution)/shard_map/ppermute | solution.py:31
  33.4 35.5 %collective-permute-start.11 = (bf16[512,512]{1,0:T(8,128)(2,1)}, bf16[512,512]{1,0:T(8,128)(2,1)}, u32[]{:S(2)}, u32[]{:S(2)}) collective-permute-start(bf16[512,512]{1,0:T(8,128)(2,1)} %get-tuple-element.41.refs_0_), channel_id=1, source_target_pairs={{0,8},{1,9},{2,10},{3,11},{4,12},{5,13},{6,14},{7,15},{8,16},{9,17... | collective-permute-start | bytes 1572872 | tf_op jit(solution)/shard_map/ppermute | solution.py:31
  57.7 11.3 %collective-permute-start.12 = (bf16[512,512]{1,0:T(8,128)(2,1)}, bf16[512,512]{1,0:T(8,128)(2,1)S(1)}, u32[]{:S(2)}, u32[]{:S(2)}) collective-permute-start(bf16[512,512]{1,0:T(8,128)(2,1)} %get-tuple-element.41.refs_0_), channel_id=1, source_target_pairs={{0,24},{1,25},{2,26},{3,27},{4,28},{5,29},{6,30},{7,31},{8,0},{9,1... | collective-permute-start | bytes 1572872 | tf_op jit(solution)/shard_map/ppermute | solution.py:31
  58.6 15.8 %collective-permute-start.13 = (bf16[512,512]{1,0:T(8,128)(2,1)}, bf16[512,512]{1,0:T(8,128)(2,1)S(1)}, u32[]{:S(2)}, u32[]{:S(2)}) collective-permute-start(bf16[512,512]{1,0:T(8,128)(2,1)} %get-tuple-element.42.refs_1_), channel_id=1, source_target_pairs={{0,8},{1,9},{2,10},{3,11},{4,12},{5,13},{6,14},{7,15},{8,16},{9,17... | collective-permute-start | bytes 1572872 | tf_op jit(solution)/shard_map/ppermute | solution.py:31
  64.3 11.0 %collective-permute-start.14 = (bf16[512,512]{1,0:T(8,128)(2,1)}, bf16[512,512]{1,0:T(8,128)(2,1)}, u32[]{:S(2)}, u32[]{:S(2)}) collective-permute-start(bf16[512,512]{1,0:T(8,128)(2,1)} %get-tuple-element.42.refs_1_), channel_id=1, source_target_pairs={{0,24},{1,25},{2,26},{3,27},{4,28},{5,29},{6,30},{7,31},{8,0},{9,1... | collective-permute-start | bytes 1572872 | tf_op jit(solution)/shard_map/ppermute | solution.py:31
  75.8 11.2 %collective-permute-start.16 = (bf16[512,512]{1,0:T(8,128)(2,1)}, bf16[512,512]{1,0:T(8,128)(2,1)}, u32[]{:S(2)}, u32[]{:S(2)}) collective-permute-start(bf16[512,512]{1,0:T(8,128)(2,1)} %copy-done.9), channel_id=1, source_target_pairs={{0,8},{1,9},{2,10},{3,11},{4,12},{5,13},{6,14},{7,15},{8,16},{9,17... | collective-permute-start | bytes 1572872 | tf_op jit(solution)/shard_map/ppermute | solution.py:31
  77.2 9.8 %collective-permute-start.17 = (bf16[512,512]{1,0:T(8,128)(2,1)}, bf16[512,512]{1,0:T(8,128)(2,1)}, u32[]{:S(2)}, u32[]{:S(2)}) collective-permute-start(bf16[512,512]{1,0:T(8,128)(2,1)} %collective-permute-done.10.refs_5_), channel_id=1, source_target_pairs={{0,24},{1,25},{2,26},{3,27},{4,28},{5,29},{6,30},{7,31},{8,0},{9,1... | collective-permute-start | bytes 1572872 | tf_op jit(solution)/shard_map/ppermute | solution.py:31
  78.4 19.6 %collective-permute-start.26 = (bf16[512,512]{1,0:T(8,128)(2,1)}, bf16[512,512]{1,0:T(8,128)(2,1)S(1)}, u32[]{:S(2)}, u32[]{:S(2)}) collective-permute-start(bf16[512,512]{1,0:T(8,128)(2,1)} %collective-permute-done.11.refs_2_), channel_id=1, source_target_pairs={{0,8},{1,9},{2,10},{3,11},{4,12},{5,13},{6,14},{7,15},{8,16},{9,17... | collective-permute-start | bytes 1572872 | tf_op jit(solution)/shard_map/ppermute | solution.py:31
  78.6 19.4 %collective-permute-start.27 = (bf16[512,512]{1,0:T(8,128)(2,1)}, bf16[512,512]{1,0:T(8,128)(2,1)S(1)}, u32[]{:S(2)}, u32[]{:S(2)}) collective-permute-start(bf16[512,512]{1,0:T(8,128)(2,1)} %collective-permute-done.14.refs_5_), channel_id=1, source_target_pairs={{0,24},{1,25},{2,26},{3,27},{4,28},{5,29},{6,30},{7,31},{8,0},{9,1... | collective-permute-start | bytes 1572872 | tf_op jit(solution)/shard_map/ppermute | solution.py:31
  89.2 12.8 %collective-permute-start.18 = (f32[32,512]{1,0:T(8,128)S(1)}, f32[32,512]{1,0:T(8,128)S(1)}, u32[]{:S(2)}, u32[]{:S(2)}) collective-permute-start(f32[32,512]{1,0:T(8,128)S(1)} %get-tuple-element.77), channel_id=1, source_target_pairs={{0,1},{1,2},{2,3},{3,4},{4,5},{5,6},{6,7},{7,0},{8,9},{9,10},{10,1... | collective-permute-start | bytes 196616 | tf_op jit(solution)/shard_map/ppermute | solution.py:31
  90.9 11.1 %collective-permute-start.19 = (f32[32,512]{1,0:T(8,128)S(1)}, f32[32,512]{1,0:T(8,128)S(1)}, u32[]{:S(2)}, u32[]{:S(2)}) collective-permute-start(f32[32,512]{1,0:T(8,128)S(1)} %get-tuple-element.76), channel_id=1, source_target_pairs={{0,7},{1,0},{2,1},{3,2},{4,3},{5,4},{6,5},{7,6},{8,15},{9,8},{10,9... | collective-permute-start | bytes 196616 | tf_op jit(solution)/shard_map/ppermute | solution.py:31
  107.5 7.2 %collective-permute-start.22 = (f32[64,512]{1,0:T(8,128)S(1)}, f32[64,512]{1,0:T(8,128)S(1)}, u32[]{:S(2)}, u32[]{:S(2)}) collective-permute-start(f32[64,512]{1,0:T(8,128)S(1)} %get-tuple-element.71), channel_id=1, source_target_pairs={{0,1},{1,2},{2,3},{3,4},{4,5},{5,6},{6,7},{7,0},{8,9},{9,10},{10,1... | collective-permute-start | bytes 393224 | tf_op jit(solution)/shard_map/ppermute | solution.py:31
  107.6 7.0 %collective-permute-start.23 = (f32[64,512]{1,0:T(8,128)S(1)}, f32[64,512]{1,0:T(8,128)S(1)}, u32[]{:S(2)}, u32[]{:S(2)}) collective-permute-start(f32[64,512]{1,0:T(8,128)S(1)} %get-tuple-element.70), channel_id=1, source_target_pairs={{0,7},{1,0},{2,1},{3,2},{4,3},{5,4},{6,5},{7,6},{8,15},{9,8},{10,9... | collective-permute-start | bytes 393224 | tf_op jit(solution)/shard_map/ppermute | solution.py:31
  114.7 6.9 %collective-permute-start.24 = (f32[64,512]{1,0:T(8,128)S(1)}, f32[64,512]{1,0:T(8,128)S(1)}, u32[]{:S(2)}, u32[]{:S(2)}) collective-permute-start(f32[64,512]{1,0:T(8,128)S(1)} %get-tuple-element.69), channel_id=1, source_target_pairs={{0,1},{1,2},{2,3},{3,4},{4,5},{5,6},{6,7},{7,0},{8,9},{9,10},{10,1... | collective-permute-start | bytes 393224 | tf_op jit(solution)/shard_map/ppermute | solution.py:31
  125.2 29.6 %all-to-all-start.1 = ((f32[256,1,128]{2,1,0:T(1,128)}), f32[256,1,128]{2,1,0:T(1,128)S(1)}, u32[]{:S(2)}, u32[]{:S(2)}) async-start(f32[256,1,128]{2,1,0:T(1,128)} %broadcast_in_dim.2), calls=%async_computation.1 | async-start | bytes 262144 | tf_op jit(solution)/shard_map/all_to_all | solution.py:203
  141.8 14.3 %collective-permute-start.36 = (f32[32,1024]{1,0:T(8,128)S(1)}, f32[32,1024]{1,0:T(8,128)S(1)}, u32[]{:S(2)}, u32[]{:S(2)}) collective-permute-start(f32[32,1024]{1,0:T(8,128)S(1)} %broadcast_select_fusion), channel_id=1, source_target_pairs={{0,32},{1,33},{2,34},{3,35},{4,36},{5,37},{6,38},{7,39},{8,40},{9,... | collective-permute-start | bytes 393224 | tf_op jit(solution)/shard_map/ppermute | solution.py:31
  (36 other events, 161.6 us)
